TPU v7x, 32 devices: a whole 2x2x4 slice. The times are simulated.
32 devices in a mesh: ctx: 4 (over z), tp: 4 (over x, core), dp: 2 (over y).
Axes of the slice: x: 2, y: 2, z: 4, core: 2. Of those that a mesh axis runs over, the one named last changes fastest.
Arguments:
- queries: bfloat16 [2, 768, 8192], P('dp', 'ctx', 'tp'), may hold values from -6 to 6
- keys: bfloat16 [2, 768, 8192], P('dp', 'ctx', 'tp'), may hold values from -6 to 6
- values: bfloat16 [2, 768, 8192], P('dp', 'ctx', 'tp'), may hold values from -6 to 6
- out_grad: bfloat16 [2, 768, 8192], P('dp', ('ctx', 'tp')), may hold values from -6 to 6
- filters: float32 [512, 128], P('tp'), may hold values from -0.5 to 0.5
Outputs:
- query_grad: bfloat16 [2, 768, 8192], P('dp', 'ctx', 'tp')
- key_grad: bfloat16 [2, 768, 8192], P('dp', 'ctx', 'tp')
- value_grad: bfloat16 [2, 768, 8192], P('dp', 'ctx', 'tp')
- filter_grad: float32 [512, 128], P('tp')
All inputs are finite; a program needn't handle non-finite values.
Results may differ from a plain program's by a relative error of at most 0.006.
Values may be sent and summed in bfloat16 or wider, within the bound.
No kernel may reach another device: no remote copies, remote signals or barrier semaphores. Data moves between devices by JAX's collectives and lax.ppermute only.
A program may use at most 64 MiB of HBM per device.

v0:
```python
import math

import jax
import jax.numpy as jnp
from jax import lax
from jax.sharding import PartitionSpec as P


def passed_along(value, axis, steps):
    count = lax.axis_size(axis)
    first, last = (max(0, -steps), min(count, count - steps))
    return lax.ppermute(value, axis, [(source, source + steps) for source in range(first, last)])


def toeplitz(coeffs, row_count, col_count, lag_index):
    tap_count = coeffs.shape[1]
    tap_ids = lax.broadcasted_iota(jnp.int32, (row_count, col_count, tap_count), 2)
    onehot = (lag_index[:, :, None] == tap_ids).astype(jnp.bfloat16)
    return jnp.einsum("gj,isj->gis", coeffs, onehot, preferred_element_type=jnp.float32).astype(
        jnp.bfloat16
    )


def apply_band(matrix, window):
    groups = matrix.shape[0]
    window_rows, channels = window.shape
    grouped = window.reshape(window_rows, groups, channels // groups)
    result = jnp.einsum("gis,sgc->igc", matrix, grouped, preferred_element_type=jnp.float32)
    return result.reshape(matrix.shape[1], channels)


def diagonals(scores, tap_count):
    groups, block_rows, window_rows = scores.shape
    padded = jnp.pad(scores, ((0, 0), (0, 0), (0, 1)))
    flattened = padded.reshape(groups, block_rows * (window_rows + 1))
    flattened = jnp.pad(flattened, ((0, 0), (0, block_rows)))
    skewed = flattened.reshape(groups, block_rows, window_rows + 2)
    return jnp.sum(skewed[:, :, :tap_count], axis=1)


def local(queries, keys, values, out_grad, filters):
    query_rows = queries[0]
    key_rows = keys[0]
    value_rows = values[0]
    row_count, channels = query_rows.shape
    groups, tap_count = filters.shape
    group_width = channels // groups
    block_rows = tap_count // 2
    window_rows = block_rows + tap_count - 1
    block_count = row_count // block_rows
    coeffs = filters.astype(jnp.bfloat16)
    grad_local = lax.all_to_all(out_grad[0], "tp", split_axis=1, concat_axis=0, tiled=True)
    products = (key_rows.astype(jnp.float32) * value_rows.astype(jnp.float32)).astype(jnp.bfloat16)
    earlier = passed_along(products[row_count - tap_count + 1 :], "ctx", 1)
    product_window = jnp.concatenate([earlier, products], axis=0)
    grad_mix = (grad_local.astype(jnp.float32) * query_rows.astype(jnp.float32)).astype(
        jnp.bfloat16
    )
    later = passed_along(grad_mix[: tap_count - 1], "ctx", -1)
    grad_window = jnp.concatenate([grad_mix, later], axis=0)
    row_ids = lax.broadcasted_iota(jnp.int32, (block_rows, window_rows), 0)
    col_ids = lax.broadcasted_iota(jnp.int32, (block_rows, window_rows), 1)
    causal_band = toeplitz(coeffs, block_rows, window_rows, row_ids + tap_count - 1 - col_ids)
    adjoint_band = toeplitz(coeffs, block_rows, window_rows, col_ids - row_ids)

    def one_block(position):
        begin_row = position * block_rows
        product_part = lax.dynamic_slice_in_dim(product_window, begin_row, window_rows, 0)
        grad_part = lax.dynamic_slice_in_dim(grad_window, begin_row, window_rows, 0)
        grad_own = lax.dynamic_slice_in_dim(grad_mix, begin_row, block_rows, 0)
        mixed = apply_band(causal_band, product_part)
        back = apply_band(adjoint_band, grad_part)
        scores = jnp.einsum(
            "igc,sgc->gis",
            grad_own.reshape(block_rows, groups, group_width),
            product_part.reshape(window_rows, groups, group_width),
            preferred_element_type=jnp.float32,
        )
        return (mixed, back, diagonals(scores, tap_count))

    mixed_blocks, back_blocks, lag_blocks = lax.map(
        one_block, jnp.arange(block_count, dtype=jnp.int32)
    )
    mixed = mixed_blocks.reshape(row_count, channels)
    back = back_blocks.reshape(row_count, channels)
    filter_local = jnp.flip(jnp.sum(lag_blocks, axis=0), axis=1)
    filter_total = lax.psum(filter_local, ("ctx", "dp"))
    scale = 1.0 / math.sqrt(lax.axis_size("dp") * lax.axis_size("ctx") * row_count * group_width)
    query_grad = (grad_local.astype(jnp.float32) * mixed).astype(jnp.bfloat16)
    key_grad = (back * value_rows.astype(jnp.float32)).astype(jnp.bfloat16)
    value_grad = (back * key_rows.astype(jnp.float32)).astype(jnp.bfloat16)
    return (query_grad[None], key_grad[None], value_grad[None], filter_total * scale)


def solution(mesh):
    in_specs = (
        P("dp", "ctx", "tp"),
        P("dp", "ctx", "tp"),
        P("dp", "ctx", "tp"),
        P("dp", ("ctx", "tp"), None),
        P("tp", None),
    )
    out_specs = (P("dp", "ctx", "tp"), P("dp", "ctx", "tp"), P("dp", "ctx", "tp"), P("tp", None))
    return jax.shard_map(local, mesh=mesh, in_specs=in_specs, out_specs=out_specs, check_vma=False)
```

profile of v0, /device:TPU:0, one launch (start us, length us, event | category | flops | bytes accessed | tf_op | source)
XLA Modules:
  0.0 257.4 jit_solution(2335483352765122767)
XLA Ops:
  10.7 5.7 %collective-permute-start = (bf16[127,2048]{1,0:T(8,128)(2,1)}, bf16[127,2048]{1,0:T(8,128)(2,1)}, u32[]{:S(2)}, u32[]{:S(2)}) collective-permute-start(bf16[127,2048]{1,0:T(8,128)(2,1)} %slice_bitcast_fusion), channel_id=1, source_target_pairs={{0,8},{8,16},{16,24},{1,9},{9,17},{17,25},{2,10},{10,18},{18,26},{... | collective-permute-start | bytes 1560584 | tf_op jit(solution)/shard_map/ppermute | solution.py:12
  18.3 4.2 %all-to-all-start = ((bf16[48,4,2048]{2,0,1:T(8,128)(2,1)}), bf16[48,4,2048]{2,0,1:T(8,128)(2,1)}, u32[]{:S(2)}, u32[]{:S(2)}) async-start(bf16[48,4,2048]{2,0,1:T(8,128)(2,1)} %copy.54), calls=%async_computation | async-start | bytes 1572864 | tf_op jit(solution)/shard_map/all_to_all | solution.py:52
  22.7 3.2 %convert_bitcast_fusion = bf16[128,64,191]{0,2,1:T(8,128)(2,1)S(1)} fusion(s32[64,191]{1,0:T(8,128)S(1)} %iota_subtract_fusion, f32[128,128]{1,0:T(8,128)S(1)} %copy-done.8), kind=kOutput, calls=%fused_computation.11 | convolution fusion | flops 403701760 | bytes 3243776 | tf_op jit(solution)/shard_map/gj,isj->gis/dot_general | solution.py:19
  25.9 7.6 %copy.58 = bf16[128,64,191]{2,1,0:T(8,128)(2,1)} copy(bf16[128,64,191]{0,2,1:T(8,128)(2,1)S(1)} %convert_bitcast_fusion) | data formatting | bytes 6258688 | tf_op jit(solution)/shard_map/while | solution.py:81
  38.2 3.2 %convert_bitcast_fusion.1 = bf16[128,64,191]{0,2,1:T(8,128)(2,1)S(1)} fusion(s32[64,191]{1,0:T(8,128)S(1)} %iota_subtract_fusion.1, f32[128,128]{1,0:T(8,128)S(1)} %copy-done.8), kind=kOutput, calls=%fused_computation.13 | convolution fusion | flops 403701760 | bytes 3243776 | tf_op jit(solution)/shard_map/gj,isj->gis/dot_general | solution.py:19
  41.5 7.7 %copy.56 = bf16[128,64,191]{2,1,0:T(8,128)(2,1)} copy(bf16[128,64,191]{0,2,1:T(8,128)(2,1)S(1)} %convert_bitcast_fusion.1) | data formatting | bytes 6258688 | tf_op jit(solution)/shard_map/while | solution.py:81
  49.2 2.7 %pad_maximum_fusion = bf16[319,2048]{1,0:T(8,128)(2,1)} fusion(bf16[192,2048]{1,0:T(8,128)(2,1)} %bitcast.86, bf16[127,2048]{1,0:T(8,128)(2,1)} %collective-permute-done), kind=kLoop, calls=%fused_computation.25 | loop fusion | flops 2613248 | bytes 2613248 | tf_op jit(solution)/shard_map/concatenate | solution.py:55
  53.9 124.7 %while.16 = (s32[]{:T(128)}, f32[3,64,2048]{2,1,0:T(8,128)}, f32[3,64,2048]{2,1,0:T(8,128)}, f32[3,128,128]{1,2,0:T(8,128)S(1)}, s32[3]{0:T(128)S(1)}, /*index=5...) while((s32[]{:T(128)}, f32[3,64,2048]{2,1,0:T(8,128)}, ...), condition=%wide.region_2.3_spmd, body=%wide.region_0.2_spmd.sunk | while | flops 151240704 | bytes 97046920 | solution.py:81
  57.0 3.4 %fusion.37 = f32[128,16,64]{2,1,0:T(8,128)S(1)} fusion(bf16[191,128,16]{0,2,1:T(8,128)(2,1)S(1)} %bitcast.82, bf16[128,64,191]{2,1,0:T(8,128)(2,1)} %get-tuple-element.328), kind=kOutput, calls=%fused_computation.37.clone.1 | convolution fusion | flops 50069504 | bytes 4435968 | tf_op jit(solution)/shard_map/while/body/eval_jaxpr/gis,sgc->igc/dot_general | solution.py:28
  62.6 3.4 %fusion.38 = f32[128,16,64]{2,1,0:T(8,128)S(1)} fusion(bf16[191,128,16]{0,2,1:T(8,128)(2,1)S(1)} %bitcast.80, bf16[128,64,191]{2,1,0:T(8,128)(2,1)} %get-tuple-element.326), kind=kOutput, calls=%fused_computation.36.clone.1 | convolution fusion | flops 50069504 | bytes 4435968 | tf_op jit(solution)/shard_map/while/body/eval_jaxpr/gis,sgc->igc/dot_general | solution.py:28
  67.5 4.5 %fusion.39 = f32[128,64,191]{2,1,0:T(8,128)} fusion(bf16[64,128,16]{0,2,1:T(8,128)(2,1)S(1)} %bitcast.85, bf16[191,128,16]{0,2,1:T(8,128)(2,1)S(1)} %bitcast.81), kind=kOutput, calls=%fused_computation.38.clone.1 | convolution fusion | flops 50069504 | bytes 7303168 | tf_op jit(solution)/shard_map/while/body/eval_jaxpr/igc,sgc->gis/dot_general | solution.py:73
  72.0 8.6 %copy.83 = f32[128,64,191]{0,2,1:T(8,128)} copy(f32[128,64,191]{2,1,0:T(8,128)} %fusion.39) | data formatting | bytes 12517376 | tf_op jit(solution)/shard_map/while
  80.6 3.2 %pad.12.clone.2 = f32[128,64,192]{0,2,1:T(8,128)S(1)} pad(f32[128,64,191]{0,2,1:T(8,128)} %copy.83, f32[]{:T(128)} %constant.53.clone.1..sunk), padding=0_0x0_0x0_1 | pad | bytes 12550148 | tf_op jit(solution)/shard_map/while/body/eval_jaxpr/jit(_pad)/pad | solution.py:34
  83.8 2.9 %pad.23 = f32[128,12352]{0,1:T(8,128)} pad(f32[128,12288]{0,1:T(8,128)S(1)} %bitcast.79, f32[]{:T(128)} %constant.53.clone.1..sunk), padding=0_0x0_64 | pad | bytes 12615684 | tf_op jit(solution)/shard_map/while/body/eval_jaxpr/jit(_pad)/pad | solution.py:36
  86.7 6.0 %reshape.125 = f32[128,64,193]{0,2,1:T(8,128)} reshape(f32[128,12352]{0,1:T(8,128)} %pad.23) | data formatting | bytes 12648448 | tf_op jit(solution)/shard_map/while/body/eval_jaxpr/reshape | solution.py:37
  92.7 2.6 slice_reduce_fusion.2
  98.6 3.4 %fusion.37 = f32[128,16,64]{2,1,0:T(8,128)S(1)} fusion(bf16[191,128,16]{0,2,1:T(8,128)(2,1)S(1)} %bitcast.82, bf16[128,64,191]{2,1,0:T(8,128)(2,1)} %get-tuple-element.328), kind=kOutput, calls=%fused_computation.37.clone.1 | convolution fusion | flops 50069504 | bytes 4435968 | tf_op jit(solution)/shard_map/while/body/eval_jaxpr/gis,sgc->igc/dot_general | solution.py:28
  104.1 3.4 %fusion.38 = f32[128,16,64]{2,1,0:T(8,128)S(1)} fusion(bf16[191,128,16]{0,2,1:T(8,128)(2,1)S(1)} %bitcast.80, bf16[128,64,191]{2,1,0:T(8,128)(2,1)} %get-tuple-element.326), kind=kOutput, calls=%fused_computation.36.clone.1 | convolution fusion | flops 50069504 | bytes 4435968 | tf_op jit(solution)/shard_map/while/body/eval_jaxpr/gis,sgc->igc/dot_general | solution.py:28
  109.0 4.5 %fusion.39 = f32[128,64,191]{2,1,0:T(8,128)} fusion(bf16[64,128,16]{0,2,1:T(8,128)(2,1)S(1)} %bitcast.85, bf16[191,128,16]{0,2,1:T(8,128)(2,1)S(1)} %bitcast.81), kind=kOutput, calls=%fused_computation.38.clone.1 | convolution fusion | flops 50069504 | bytes 7303168 | tf_op jit(solution)/shard_map/while/body/eval_jaxpr/igc,sgc->gis/dot_general | solution.py:73
  113.5 8.6 %copy.83 = f32[128,64,191]{0,2,1:T(8,128)} copy(f32[128,64,191]{2,1,0:T(8,128)} %fusion.39) | data formatting | bytes 12517376 | tf_op jit(solution)/shard_map/while
  122.1 3.2 %pad.12.clone.2 = f32[128,64,192]{0,2,1:T(8,128)S(1)} pad(f32[128,64,191]{0,2,1:T(8,128)} %copy.83, f32[]{:T(128)} %constant.53.clone.1..sunk), padding=0_0x0_0x0_1 | pad | bytes 12550148 | tf_op jit(solution)/shard_map/while/body/eval_jaxpr/jit(_pad)/pad | solution.py:34
  125.3 2.9 %pad.23 = f32[128,12352]{0,1:T(8,128)} pad(f32[128,12288]{0,1:T(8,128)S(1)} %bitcast.79, f32[]{:T(128)} %constant.53.clone.1..sunk), padding=0_0x0_64 | pad | bytes 12615684 | tf_op jit(solution)/shard_map/while/body/eval_jaxpr/jit(_pad)/pad | solution.py:36
  128.2 6.0 %reshape.125 = f32[128,64,193]{0,2,1:T(8,128)} reshape(f32[128,12352]{0,1:T(8,128)} %pad.23) | data formatting | bytes 12648448 | tf_op jit(solution)/shard_map/while/body/eval_jaxpr/reshape | solution.py:37
  140.1 3.4 %fusion.37 = f32[128,16,64]{2,1,0:T(8,128)S(1)} fusion(bf16[191,128,16]{0,2,1:T(8,128)(2,1)S(1)} %bitcast.82, bf16[128,64,191]{2,1,0:T(8,128)(2,1)} %get-tuple-element.328), kind=kOutput, calls=%fused_computation.37.clone.1 | convolution fusion | flops 50069504 | bytes 4435968 | tf_op jit(solution)/shard_map/while/body/eval_jaxpr/gis,sgc->igc/dot_general | solution.py:28
  145.7 3.4 %fusion.38 = f32[128,16,64]{2,1,0:T(8,128)S(1)} fusion(bf16[191,128,16]{0,2,1:T(8,128)(2,1)S(1)} %bitcast.80, bf16[128,64,191]{2,1,0:T(8,128)(2,1)} %get-tuple-element.326), kind=kOutput, calls=%fused_computation.36.clone.1 | convolution fusion | flops 50069504 | bytes 4435968 | tf_op jit(solution)/shard_map/while/body/eval_jaxpr/gis,sgc->igc/dot_general | solution.py:28
  150.6 4.5 %fusion.39 = f32[128,64,191]{2,1,0:T(8,128)} fusion(bf16[64,128,16]{0,2,1:T(8,128)(2,1)S(1)} %bitcast.85, bf16[191,128,16]{0,2,1:T(8,128)(2,1)S(1)} %bitcast.81), kind=kOutput, calls=%fused_computation.38.clone.1 | convolution fusion | flops 50069504 | bytes 7303168 | tf_op jit(solution)/shard_map/while/body/eval_jaxpr/igc,sgc->gis/dot_general | solution.py:73
  155.1 8.6 %copy.83 = f32[128,64,191]{0,2,1:T(8,128)} copy(f32[128,64,191]{2,1,0:T(8,128)} %fusion.39) | data formatting | bytes 12517376 | tf_op jit(solution)/shard_map/while
  163.7 3.2 %pad.12.clone.2 = f32[128,64,192]{0,2,1:T(8,128)S(1)} pad(f32[128,64,191]{0,2,1:T(8,128)} %copy.83, f32[]{:T(128)} %constant.53.clone.1..sunk), padding=0_0x0_0x0_1 | pad | bytes 12550148 | tf_op jit(solution)/shard_map/while/body/eval_jaxpr/jit(_pad)/pad | solution.py:34
  166.9 2.9 %pad.23 = f32[128,12352]{0,1:T(8,128)} pad(f32[128,12288]{0,1:T(8,128)S(1)} %bitcast.79, f32[]{:T(128)} %constant.53.clone.1..sunk), padding=0_0x0_64 | pad | bytes 12615684 | tf_op jit(solution)/shard_map/while/body/eval_jaxpr/jit(_pad)/pad | solution.py:36
  169.7 6.0 %reshape.125 = f32[128,64,193]{0,2,1:T(8,128)} reshape(f32[128,12352]{0,1:T(8,128)} %pad.23) | data formatting | bytes 12648448 | tf_op jit(solution)/shard_map/while/body/eval_jaxpr/reshape | solution.py:37
  179.2 4.4 %fusion.4 = (bf16[1,192,2048]{2,1,0:T(8,128)(2,1)}, bf16[1,192,2048]{2,1,0:T(8,128)(2,1)}, bf16[1,192,2048]{2,1,0:T(8,128)(2,1)}) fusion(bf16[1,192,2048]{2,1,0:T(8,128)(2,1)} %param.8, bf16[1,192,2048]{2,1,0:T(8,128)(2,1)} %param.9, bf16[48,4,2048]{2,0,1:T(8,128)(2,1)} %all-to-all-done, f32[1,192,2048]{2,1,0:T(8,128)} %bitcast.87, f32[1,192,2048]{2,1,0:T(8,128)} %bitcast.88), kind=kLoop, calls=%fused_computation.18 | loop fusion | flops 3538944 | bytes 7864320 | tf_op jit(solution)/shard_map/convert_element_type | solution.py:91
  183.6 65.4 %all-reduce.4.cloned.1.call-done = f32[128,128]{0,1:T(8,128)} async-done(((f32[128,128]{0,1:T(8,128)}), f32[128,128]{0,1:T(8,128)}) %all-reduce.4.cloned.1.call-update) | async-done | bytes 65552 | tf_op jit(solution)/shard_map/psum | solution.py:87
  (93 shorter events, 38.6 us)
Async XLA Ops:
  7.2 9.3 %copy-start.7 = (bf16[1,48,8192]{2,1,0:T(8,128)(2,1)S(1)}, bf16[1,48,8192]{2,1,0:T(8,128)(2,1)}, u32[]{:S(2)}) copy-start(bf16[1,48,8192]{2,1,0:T(8,128)(2,1)} %param.10) | copy-start | bytes 2359300
  8.9 0.9 copy-start.6
  10.7 38.5 %collective-permute-start = (bf16[127,2048]{1,0:T(8,128)(2,1)}, bf16[127,2048]{1,0:T(8,128)(2,1)}, u32[]{:S(2)}, u32[]{:S(2)}) collective-permute-start(bf16[127,2048]{1,0:T(8,128)(2,1)} %slice_bitcast_fusion), channel_id=1, source_target_pairs={{0,8},{8,16},{16,24},{1,9},{9,17},{17,25},{2,10},{10,18},{18,26},{... | collective-permute-start | bytes 1560584 | tf_op jit(solution)/shard_map/ppermute | solution.py:12
  17.0 5.6 %copy-start.8 = (f32[128,128]{1,0:T(8,128)S(1)}, f32[128,128]{1,0:T(8,128)}, u32[]{:S(2)}) copy-start(f32[128,128]{1,0:T(8,128)} %param.11) | copy-start | bytes 196612
  18.3 15.9 %all-to-all-start = ((bf16[48,4,2048]{2,0,1:T(8,128)(2,1)}), bf16[48,4,2048]{2,0,1:T(8,128)(2,1)}, u32[]{:S(2)}, u32[]{:S(2)}) async-start(bf16[48,4,2048]{2,0,1:T(8,128)(2,1)} %copy.54), calls=%async_computation | async-start | bytes 1572864 | tf_op jit(solution)/shard_map/all_to_all | solution.py:52
  22.5 226.5 %all-reduce.4.cloned.1.call-start = ((), (), s32[]{:S(2)}) async-start(), calls=%async_computation.1 | async-start | bytes 131072 | tf_op jit(solution)/shard_map/psum | solution.py:87
  35.9 1.1 copy-start.3
  37.0 15.7 %collective-permute-start.1 = (bf16[127,2048]{1,0:T(8,128)(2,1)}, bf16[127,2048]{1,0:T(8,128)(2,1)}, u32[]{:S(2)}, u32[]{:S(2)}) collective-permute-start(bf16[127,2048]{1,0:T(8,128)(2,1)} %slice.20), channel_id=1, source_target_pairs={{8,0},{16,8},{24,16},{9,1},{17,9},{25,17},{10,2},{18,10},{26,18},{... | collective-permute-start | bytes 1560584 | tf_op jit(solution)/shard_map/ppermute | solution.py:12
  49.2 3.5 %copy-start.4 = (bf16[192,2048]{1,0:T(8,128)(2,1)S(1)}, bf16[192,2048]{1,0:T(8,128)(2,1)}, u32[]{:S(2)}) copy-start(bf16[192,2048]{1,0:T(8,128)(2,1)} %copy-done.3) | copy-start | bytes 2359300
  53.9 3.1 %copy-start.1 = (bf16[319,2048]{1,0:T(8,128)(2,1)}, bf16[319,2048]{1,0:T(8,128)(2,1)S(1)}, u32[]{:S(2)}) copy-start(bf16[319,2048]{1,0:T(8,128)(2,1)S(1)} %get-tuple-element.327) | copy-start | bytes 3919876 | tf_op jit(solution)/shard_map/while
  66.3 1.2 copy-start
  92.7 2.6 %copy-start.2 = (bf16[319,2048]{1,0:T(8,128)(2,1)S(1)}, bf16[319,2048]{1,0:T(8,128)(2,1)}, u32[]{:S(2)}) copy-start(bf16[319,2048]{1,0:T(8,128)(2,1)} %copy-done.1) | copy-start | bytes 3919876 | tf_op jit(solution)/shard_map/while
  92.7 2.8 %copy-start.5 = (bf16[192,2048]{1,0:T(8,128)(2,1)S(1)}, bf16[192,2048]{1,0:T(8,128)(2,1)}, u32[]{:S(2)}) copy-start(bf16[192,2048]{1,0:T(8,128)(2,1)} %get-tuple-element.353) | copy-start | bytes 2359300 | tf_op jit(solution)/shard_map/while
  95.4 3.1 %copy-start.1 = (bf16[319,2048]{1,0:T(8,128)(2,1)}, bf16[319,2048]{1,0:T(8,128)(2,1)S(1)}, u32[]{:S(2)}) copy-start(bf16[319,2048]{1,0:T(8,128)(2,1)S(1)} %get-tuple-element.327) | copy-start | bytes 3919876 | tf_op jit(solution)/shard_map/while
  107.8 1.2 copy-start
  134.2 2.6 %copy-start.2 = (bf16[319,2048]{1,0:T(8,128)(2,1)S(1)}, bf16[319,2048]{1,0:T(8,128)(2,1)}, u32[]{:S(2)}) copy-start(bf16[319,2048]{1,0:T(8,128)(2,1)} %copy-done.1) | copy-start | bytes 3919876 | tf_op jit(solution)/shard_map/while
  134.2 2.8 %copy-start.5 = (bf16[192,2048]{1,0:T(8,128)(2,1)S(1)}, bf16[192,2048]{1,0:T(8,128)(2,1)}, u32[]{:S(2)}) copy-start(bf16[192,2048]{1,0:T(8,128)(2,1)} %get-tuple-element.353) | copy-start | bytes 2359300 | tf_op jit(solution)/shard_map/while
  137.0 3.1 %copy-start.1 = (bf16[319,2048]{1,0:T(8,128)(2,1)}, bf16[319,2048]{1,0:T(8,128)(2,1)S(1)}, u32[]{:S(2)}) copy-start(bf16[319,2048]{1,0:T(8,128)(2,1)S(1)} %get-tuple-element.327) | copy-start | bytes 3919876 | tf_op jit(solution)/shard_map/while
  149.4 1.2 copy-start
  175.7 2.6 %copy-start.2 = (bf16[319,2048]{1,0:T(8,128)(2,1)S(1)}, bf16[319,2048]{1,0:T(8,128)(2,1)}, u32[]{:S(2)}) copy-start(bf16[319,2048]{1,0:T(8,128)(2,1)} %copy-done.1) | copy-start | bytes 3919876 | tf_op jit(solution)/shard_map/while
  175.7 2.8 %copy-start.5 = (bf16[192,2048]{1,0:T(8,128)(2,1)S(1)}, bf16[192,2048]{1,0:T(8,128)(2,1)}, u32[]{:S(2)}) copy-start(bf16[192,2048]{1,0:T(8,128)(2,1)} %get-tuple-element.353) | copy-start | bytes 2359300 | tf_op jit(solution)/shard_map/while
Sparse Core Ops, SparseCore 0:
  179.3 69.6 all-reduce.3
where the time goes:
time: 259 us; the launch traced here: 257 us
  local copies, waits for them, and re-layouts  102 us (39%)
  waiting for transfers between devices  67 us (26%)
  matrix products  40.2 us (16%)
  other arithmetic  20.2 us (8%)
  between operations  14.2 us (5%)
  starting transfers between devices  11.3 us (4%)
    psum x1, waiting for transfers between devices, local(): filter_total = lax.psum(filter_local, ('ctx', 'dp'))  65.4 us
    while x27, local copies, waits for them, and re-layouts  26.7 us
    dot_general x6, matrix products, apply_band(): jnp.einsum('gis,sgc->igc', matrix, grouped, preferred_element_type=jnp.fl...  20.2 us
    reshape x3, local copies, waits for them, and re-layouts, diagonals(): skewed = flattened.reshape(groups, block_rows, window_rows + 2)  18 us
    while x2, local copies, waits for them, and re-layouts, local(): lax.map(one_block, jnp.arange(block_count, dtype=jnp.int32))  15.3 us
    dot_general x3, matrix products, one_block(): jnp.einsum('igc,sgc->gis', grad_own.reshape(block_rows, groups, group_wid...  13.6 us
    pad x3, local copies, waits for them, and re-layouts, diagonals(): padded = jnp.pad(scores, ((0, 0), (0, 0), (0, 1)))  9.58 us
    pad x3, local copies, waits for them, and re-layouts, diagonals(): flattened = jnp.pad(flattened, ((0, 0), (0, block_rows)))  8.57 us
  transfers between devices with their start and end apart: 4, of which 3 were waited for; matrix products, arithmetic and copies ran while one was open for 13% of the time, Pallas kernels for 0%

commit v1 on v0

v1 whole, which is shorter than its diff:
```python
import functools
import math

import jax
import jax.numpy as jnp
from jax import lax
from jax.experimental import pallas as pl
from jax.experimental.pallas import tpu as pltpu
from jax.sharding import PartitionSpec as P

LANES = 128
BLOCK = 32


def widen(value):
    return value.astype(jnp.float32)


def product(left, right):
    return (widen(left) * widen(right)).astype(jnp.bfloat16)


def passed_along(value, axis, steps):
    count = lax.axis_size(axis)
    first, last = (max(0, -steps), min(count, count - steps))
    return lax.ppermute(value, axis, [(source, source + steps) for source in range(first, last)])


def peer(index, step, count):
    if count & (count - 1) == 0:
        return index ^ step
    return (index + step) % count


def sender(index, step, count):
    if count & (count - 1) == 0:
        return index ^ step
    return (index - step + count) % count


def exchanged(rows, axis):
    count = lax.axis_size(axis)
    here = lax.axis_index(axis)
    height = rows.shape[0]
    width = rows.shape[1] // count
    own = lax.dynamic_slice_in_dim(rows, here * width, width, 1)
    parts = []
    for step in range(1, count):
        part = lax.dynamic_slice_in_dim(rows, peer(here, step, count) * width, width, 1)
        pairs = [(index, peer(index, step, count)) for index in range(count)]
        parts.append((sender(here, step, count), lax.ppermute(part, axis, pairs)))
    result = jnp.zeros((height * count, width), rows.dtype)
    result = lax.dynamic_update_slice_in_dim(result, own, here * height, 0)
    for source, part in parts:
        result = lax.dynamic_update_slice_in_dim(result, part, source * height, 0)
    return result


def summed(value, axis):
    count = lax.axis_size(axis)
    if count & (count - 1):
        return lax.psum(value, axis)
    if count <= 4:
        steps = range(1, count)
        parts = [
            lax.ppermute(value, axis, [(index, index ^ step) for index in range(count)])
            for step in steps
        ]
        for part in parts:
            value = value + part
        return value
    step = 1
    while step < count:
        value = value + lax.ppermute(value, axis, [(i, i ^ step) for i in range(count)])
        step *= 2
    return value


def windows(rows, blocks, height):
    return jnp.concatenate([rows[BLOCK * b : BLOCK * b + height] for b in range(blocks)], axis=1)


def bands(base, count, width):
    rows = []
    for group in range(count):
        row = jnp.broadcast_to(base[group : group + 1, :], (BLOCK, base.shape[1]))
        row = pltpu.roll(row, 0, 1, stride=1, stride_axis=0)
        rows.append(row[:, :width].astype(jnp.bfloat16))
    return jnp.concatenate(rows, axis=0)


def convolved(base, window, blocks, taps, group_width):
    count = LANES // group_width
    every = jnp.dot(
        bands(base, count, taps + BLOCK),
        windows(window, blocks, taps + BLOCK),
        preferred_element_type=jnp.float32,
    )
    lane_group = lax.broadcasted_iota(jnp.int32, (BLOCK, LANES), 1) // group_width
    outs = []
    for b in range(blocks):
        columns = slice(b * LANES, (b + 1) * LANES)
        out = every[:BLOCK, columns]
        for group in range(1, count):
            out = jnp.where(
                lane_group == group, every[group * BLOCK : (group + 1) * BLOCK, columns], out
            )
        outs.append(out)
    return jnp.concatenate(outs, axis=0)


def scores_kernel(taps, group_width, q_ref, og_ref, k_ref, v_ref, early_ref, out_ref):
    blocks = k_ref.shape[0] // BLOCK
    count = LANES // group_width
    down = lax.broadcasted_iota(jnp.int32, (BLOCK, BLOCK), 0)
    across = lax.broadcasted_iota(jnp.int32, (BLOCK, BLOCK), 1)
    reverse = (down + across == BLOCK - 1).astype(jnp.bfloat16)
    lane = lax.broadcasted_iota(jnp.int32, (BLOCK, blocks * LANES), 1)
    lane_group = (lane % LANES) // group_width
    for tile in range(k_ref.shape[1] // LANES):
        c = slice(tile * LANES, (tile + 1) * LANES)
        grad_mix = product(og_ref[:, c], q_ref[:, c])
        window = jnp.concatenate([early_ref[:, c], product(k_ref[:, c], v_ref[:, c])], axis=0)
        own = windows(grad_mix, blocks, BLOCK)
        own = jnp.dot(reverse, own, preferred_element_type=jnp.float32).astype(jnp.bfloat16)
        split = [jnp.where(lane_group == g, own, jnp.zeros_like(own)) for g in range(count)]
        scores = lax.dot_general(
            jnp.concatenate(split, axis=0),
            windows(window, blocks, taps + BLOCK),
            (((1,), (1,)), ((), ())),
            preferred_element_type=jnp.float32,
        )
        spare = jnp.zeros((scores.shape[0], 2 * taps - scores.shape[1]), jnp.float32)
        scores = jnp.concatenate([scores, spare], axis=1)
        for g in range(count):
            part = scores[g * BLOCK : (g + 1) * BLOCK]
            part = pltpu.roll(part, taps - BLOCK, 1, stride=1, stride_axis=0)[:, taps:]
            row = tile * count + g
            out_ref[row : row + 1, :] = jnp.sum(part, axis=0, keepdims=True)


def mixed_kernel(taps, group_width, k_ref, v_ref, early_ref, base_ref, og_ref, out_ref):
    blocks = k_ref.shape[0] // BLOCK
    count = LANES // group_width
    for tile in range(k_ref.shape[1] // LANES):
        c = slice(tile * LANES, (tile + 1) * LANES)
        window = jnp.concatenate([early_ref[:, c], product(k_ref[:, c], v_ref[:, c])], axis=0)
        base = base_ref[tile * count : (tile + 1) * count]
        mixed = convolved(base, window, blocks, taps, group_width)
        out_ref[:, c] = (widen(og_ref[:, c]) * mixed).astype(jnp.bfloat16)


def back_kernel(
    taps, group_width, q_ref, og_ref, late_ref, k_ref, v_ref, base_ref, kg_ref, vg_ref
):
    blocks = k_ref.shape[0] // BLOCK
    count = LANES // group_width
    for tile in range(k_ref.shape[1] // LANES):
        c = slice(tile * LANES, (tile + 1) * LANES)
        window = jnp.concatenate([product(og_ref[:, c], q_ref[:, c]), late_ref[:, c]], axis=0)
        base = base_ref[tile * count : (tile + 1) * count]
        back = convolved(base, window, blocks, taps, group_width)
        kg_ref[:, c] = (back * widen(v_ref[:, c])).astype(jnp.bfloat16)
        vg_ref[:, c] = (back * widen(k_ref[:, c])).astype(jnp.bfloat16)


def call(kernel, name, args, bases, outs, taps, group_width):
    channels = args[0].shape[1]
    wide = math.gcd(channels, 8 * LANES)
    groups = wide // group_width

    def by_column(height):
        return pl.BlockSpec((height, wide), lambda i: (0, i))

    def by_group(width):
        return pl.BlockSpec((groups, width), lambda i: (i, 0))


    return pl.pallas_call(
        functools.partial(kernel, taps, group_width),
        grid=(channels // wide,),
        in_specs=[by_group(a.shape[1]) if a.dtype == jnp.float32 else by_column(a.shape[0]) for a in args],
        out_specs=[by_group(o.shape[1]) if o.dtype == jnp.float32 else by_column(o.shape[0]) for o in outs],
        out_shape=outs,
        name=name,
        cost_estimate=pl.CostEstimate(flops=4_000_000_000, bytes_accessed=3_000_000, transcendentals=0),
        compiler_params=pltpu.CompilerParams(vmem_limit_bytes=48 * 1024 * 1024),
    )(*args)


def local(queries, keys, values, out_grad, filters):
    q, k, v = queries[0], keys[0], values[0]
    rows, channels = q.shape
    groups, taps = filters.shape
    group_width = channels // groups
    coeffs = widen(filters.astype(jnp.bfloat16))
    zeros = jnp.zeros_like(coeffs)
    causal = jnp.concatenate([zeros[:, :1], jnp.flip(coeffs, 1), zeros[:, 1:]], axis=1)
    adjoint = jnp.concatenate([coeffs, zeros], axis=1)
    grad = exchanged(out_grad[0], "tp")
    early = passed_along(product(k[rows - taps :], v[rows - taps :]), "ctx", 1)
    late = passed_along(product(grad[:taps], q[:taps]), "ctx", -1)
    wide = jax.ShapeDtypeStruct((rows, channels), jnp.bfloat16)
    small = jax.ShapeDtypeStruct((groups, taps), jnp.float32)
    (lags,) = call(scores_kernel, "lag_scores", (q, grad, k, v, early), (), [small], taps, group_width)
    lags = summed(summed(lags, "dp"), "ctx")
    (query_grad,) = call(mixed_kernel, "causal", (k, v, early, causal, grad), (), [wide], taps, group_width)
    key_grad, value_grad = call(
        back_kernel, "adjoint", (q, grad, late, k, v, adjoint), (), [wide, wide], taps, group_width
    )
    scale = 1.0 / math.sqrt(lax.axis_size("dp") * lax.axis_size("ctx") * rows * group_width)
    return (query_grad[None], key_grad[None], value_grad[None], jnp.flip(lags, 1) * scale)


def solution(mesh):
    in_specs = (
        P("dp", "ctx", "tp"),
        P("dp", "ctx", "tp"),
        P("dp", "ctx", "tp"),
        P("dp", ("ctx", "tp"), None),
        P("tp", None),
    )
    out_specs = (P("dp", "ctx", "tp"), P("dp", "ctx", "tp"), P("dp", "ctx", "tp"), P("tp", None))
    return jax.shard_map(local, mesh=mesh, in_specs=in_specs, out_specs=out_specs, check_vma=False)
```

time: 259 us -> 57.8 us (0.22)
  local copies, waits for them, and re-layouts: 102 us -> 6.25 us
  waiting for transfers between devices: 67 us -> 17.5 us
  matrix products: 40.2 us -> 0 us
  other arithmetic: 20.2 us -> 3.69 us
  between operations: 14.2 us -> 0.78 us
  Pallas kernels: 0 us -> 12.3 us
  starting transfers between devices: 11.3 us -> 16.9 us
    psum x1 -> x0, waiting for transfers between devices: 65.4 us -> none  [local(): filter_total = lax.psum(filter_local, ('ctx', 'dp'))]
    while x29 -> x0, local copies, waits for them, and re-layouts: 42 us -> none
    dot_general x11 -> x0, matrix products: 40.2 us -> none  [the longest x6 20.2 us: apply_band(): jnp.einsum('gis,sgc->igc', matrix, grouped, preferred_element_type=jnp.fl...]
    pad x6 -> x0, local copies, waits for them, and re-layouts: 18.1 us -> none  [the longest x3 9.58 us: diagonals(): padded = jnp.pad(scores, ((0, 0), (0, 0), (0, 1)))]
    reshape x3 -> x0, local copies, waits for them, and re-layouts: 18 us -> none  [diagonals(): skewed = flattened.reshape(groups, block_rows, window_rows + 2)]
    pallas_call x0 -> x3, Pallas kernels: none -> 12.3 us  [call(): pl.pallas_call(functools.partial(kernel, taps, group_width), grid=(channe...]
    ppermute x0 -> x7, starting transfers between devices: none -> 11.2 us  [the longest x4 8.07 us: summed(): lax.ppermute(value, axis, [(index, index ^ step) for index in range(count)])]
    dynamic_slice x21 -> x1, local copies, waits for them, and re-layouts: 12.8 us -> 1.98 us  [exchanged(): lax.dynamic_slice_in_dim(rows, peer(here, step, count) * width, width, 1)]
  transfers between devices with their start and end apart: 4 -> 9, of which waited for: 3 -> 5; matrix products, arithmetic and copies ran while one was open for 13% -> 14% of each run, Pallas kernels for 0% -> 7%
where the time goes in v1:
time: 57.8 us; the launch traced here: 57.5 us
  waiting for transfers between devices  17.5 us (30%)
  starting transfers between devices  16.9 us (29%)
  Pallas kernels  12.3 us (21%)
  local copies, waits for them, and re-layouts  6.25 us (11%)
  other arithmetic  3.69 us (6%)
  between operations  0.78 us (1%)
    pallas_call x3, Pallas kernels, call(): pl.pallas_call(functools.partial(kernel, taps, group_width), grid=(channe...  12.3 us
    ppermute x4, waiting for transfers between devices, summed(): lax.ppermute(value, axis, [(index, index ^ step) for index in range(count)])  10.7 us
    ppermute x4, starting transfers between devices, summed(): lax.ppermute(value, axis, [(index, index ^ step) for index in range(count)])  8.07 us
    ppermute x2, waiting for transfers between devices, passed_along(): lax.ppermute(value, axis, [(source, source + steps) for source in range(f...  6.75 us
    ppermute x2, starting transfers between devices, passed_along(): lax.ppermute(value, axis, [(source, source + steps) for source in range(f...  5.77 us
    ppermute x3, starting transfers between devices, exchanged(): parts.append((sender(here, step, count), lax.ppermute(part, axis, pairs)))  3.09 us
    convert_element_type x2, other arithmetic, product(): return (widen(left) * widen(right)).astype(jnp.bfloat16)  2.92 us
    dynamic_update_slice x3, local copies, waits for them, and re-layouts, exchanged(): result = lax.dynamic_update_slice_in_dim(result, part, source * height, 0)  2.91 us
  transfers between devices with their start and end apart: 9, of which 5 were waited for; matrix products, arithmetic and copies ran while one was open for 14% of the time, Pallas kernels for 7%

profile of v1, /device:TPU:0, one launch (start us, length us, event | category | flops | bytes accessed | tf_op | source)
XLA Modules:
  0.0 57.5 jit_solution(7169286192213512415)
XLA Ops:
  0.7 2.0 %dynamic-slice_bitcast_fusion = (bf16[48,2048]{1,0:T(8,128)(2,1)S(1)}, bf16[48,2048]{1,0:T(8,128)(2,1)}, bf16[48,2048]{1,0:T(8,128)(2,1)}) fusion(bf16[1,48,8192]{2,1,0:T(8,128)(2,1)} %param.8, s32[]{:T(128)S(6)} %select_n.30, s32[]{:T(128)S(6)} %select_n.26, s32[]{:T(128)S(6)} %select_n.28), kind=kLoop, calls=%fused_computation.5 | loop fusion | bytes 1179660 | tf_op jit(solution)/shard_map/dynamic_slice | solution.py:49
  2.6 0.5 collective-permute-start.1
  3.1 2.5 %collective-permute-start.2 = (bf16[48,2048]{1,0:T(8,128)(2,1)}, bf16[48,2048]{1,0:T(8,128)(2,1)}, u32[]{:S(2)}, u32[]{:S(2)}) collective-permute-start(bf16[48,2048]{1,0:T(8,128)(2,1)} %get-tuple-element.10), channel_id=1, source_target_pairs={{0,4},{2,6},{4,0},{6,2},{1,5},{3,7},{5,1},{7,3},{8,12},{10,14},{12... | collective-permute-start | bytes 589832 | tf_op jit(solution)/shard_map/ppermute | solution.py:51
  5.6 0.1 collective-permute-start.3
  5.7 2.0 %fusion.1 = bf16[128,2048]{1,0:T(8,128)(2,1)} fusion(bf16[1,192,2048]{2,1,0:T(8,128)(2,1)} %param.7, bf16[1,192,2048]{2,1,0:T(8,128)(2,1)S(1)} %copy-done), kind=kLoop, calls=%fused_computation.3 | loop fusion | flops 1048576 | bytes 1572864 | tf_op jit(solution)/shard_map/convert_element_type | solution.py:20
  7.7 4.5 %collective-permute-start = (bf16[128,2048]{1,0:T(8,128)(2,1)}, bf16[128,2048]{1,0:T(8,128)(2,1)}, u32[]{:S(2)}, u32[]{:S(2)}) collective-permute-start(bf16[128,2048]{1,0:T(8,128)(2,1)} %fusion.1), channel_id=1, source_target_pairs={{0,8},{8,16},{16,24},{1,9},{9,17},{17,25},{2,10},{10,18},{18,26},{... | collective-permute-start | bytes 1572872 | tf_op jit(solution)/shard_map/ppermute | solution.py:26
  12.2 0.1 rev.7
  12.3 0.1 pad.3.clone
  12.4 0.1 broadcast_in_dim.13
  12.5 0.0 copy-start.2
  12.5 1.0 %bitcast_dynamic-update-slice_fusion = bf16[192,2048]{1,0:T(8,128)(2,1)S(1)} fusion(bf16[192,2048]{1,0:T(8,128)(2,1)S(1)} %broadcast_in_dim.13, s32[]{:T(128)S(6)} %select_n.25, bf16[1,48,8192]{2,1,0:T(8,128)(2,1)} %param.8, s32[]{:T(128)S(6)} %select_n.24), kind=kLoop, calls=%fused_computation.4 | loop fusion | bytes 393224 | tf_op jit(solution)/shard_map/dynamic_update_slice | solution.py:53
  13.5 0.0 copy-start.1
  13.6 0.1 maximum_maximum_fusion.base_ref
  13.7 0.0 collective-permute-done.1
  13.7 1.0 %constant_dynamic-update-slice_fusion.1 = bf16[192,2048]{1,0:T(8,128)(2,1)S(1)} fusion(bf16[192,2048]{1,0:T(8,128)(2,1)S(1)} %bitcast_dynamic-update-slice_fusion, bf16[48,2048]{1,0:T(8,128)(2,1)} %collective-permute-done.1, s32[]{:T(128)S(6)} %select_n.27), kind=kLoop, calls=%fused_computation.13 | loop fusion | bytes 393220 | tf_op jit(solution)/shard_map/dynamic_update_slice | solution.py:55
  14.7 0.9 %constant_dynamic-update-slice_fusion = bf16[192,2048]{1,0:T(8,128)(2,1)S(1)} fusion(bf16[192,2048]{1,0:T(8,128)(2,1)S(1)} %constant_dynamic-update-slice_fusion.1, bf16[48,2048]{1,0:T(8,128)(2,1)} %collective-permute-done.2, s32[]{:T(128)S(6)} %select_n.29), kind=kLoop, calls=%fused_computation.12 | loop fusion | bytes 393220 | tf_op jit(solution)/shard_map/dynamic_update_slice | solution.py:55
  15.7 0.9 %constant_dynamic-update-slice_fusion.2.og_ref = bf16[192,2048]{1,0:T(8,128)(2,1)S(1)} fusion(bf16[192,2048]{1,0:T(8,128)(2,1)S(1)} %constant_dynamic-update-slice_fusion, bf16[48,2048]{1,0:T(8,128)(2,1)} %collective-permute-done.3, s32[]{:T(128)S(6)} %select_n.31), kind=kLoop, calls=%fused_computation.14 | loop fusion | bytes 393220 | tf_op jit(solution)/shard_map/dynamic_update_slice | solution.py:55
  16.6 6.8 %collective-permute-done.early_ref = bf16[128,2048]{1,0:T(8,128)(2,1)} collective-permute-done((bf16[128,2048]{1,0:T(8,128)(2,1)}, bf16[128,2048]{1,0:T(8,128)(2,1)}, u32[]{:S(2)}, u32[]{:S(2)}) %collective-permute-start) | collective-permute-done | bytes 524320 | tf_op jit(solution)/shard_map/ppermute | solution.py:26
  23.4 4.4 %lag_scores.1 = f32[128,128]{1,0:T(8,128)S(1)} custom-call(bf16[192,2048]{1,0:T(8,128)(2,1)S(1)} %bitcast.26, bf16[192,2048]{1,0:T(8,128)(2,1)S(1)} %constant_dynamic-update-slice_fusion.2.og_ref, bf16[192,2048]{1,0:T(8,128)(2,1)S(1)} %bitcast.20, bf16[192,2048]{1,0:T(8,128)(2,1)S(1)} %bitcast.23, bf16[128,2048]{1,0:T(8,128)(2,1)} %collective-permute-done.early_ref), custom_call_target="tpu_custom_call" | custom-call | flops 4000000000 | bytes 3000000 | tf_op jit(solution)/shard_map/lag_scores/pallas_call | solution.py:179
  27.8 1.6 %collective-permute-start.5 = (f32[128,128]{1,0:T(8,128)S(1)}, f32[128,128]{1,0:T(8,128)S(1)}, u32[]{:S(2)}, u32[]{:S(2)}) collective-permute-start(f32[128,128]{1,0:T(8,128)S(1)} %lag_scores.1), channel_id=1, source_target_pairs={{0,1},{1,0},{2,3},{3,2},{4,5},{5,4},{6,7},{7,6},{8,9},{9,8},{10,11... | collective-permute-start | bytes 196616 | tf_op jit(solution)/shard_map/ppermute | solution.py:66
  29.3 0.9 %fusion = bf16[128,2048]{1,0:T(8,128)(2,1)} fusion(bf16[192,2048]{1,0:T(8,128)(2,1)S(1)} %constant_dynamic-update-slice_fusion.2.og_ref, bf16[1,192,2048]{2,1,0:T(8,128)(2,1)S(1)} %copy-done.2), kind=kLoop, calls=%fused_computation.1 | loop fusion | flops 1048576 | bytes 1572864 | tf_op jit(solution)/shard_map/convert_element_type | solution.py:20
  30.3 1.3 %collective-permute-start.4 = (bf16[128,2048]{1,0:T(8,128)(2,1)}, bf16[128,2048]{1,0:T(8,128)(2,1)}, u32[]{:S(2)}, u32[]{:S(2)}) collective-permute-start(bf16[128,2048]{1,0:T(8,128)(2,1)} %fusion), channel_id=1, source_target_pairs={{8,0},{16,8},{24,16},{9,1},{17,9},{25,17},{10,2},{18,10},{26,18},{... | collective-permute-start | bytes 1572872 | tf_op jit(solution)/shard_map/ppermute | solution.py:26
  31.6 0.5 collective-permute-done.5
  32.1 2.7 %collective-permute-start.6 = (f32[128,128]{1,0:T(8,128)S(1)}, f32[128,128]{1,0:T(8,128)S(1)}, u32[]{:S(2)}, u32[]{:S(2)}) collective-permute-start(f32[128,128]{1,0:T(8,128)S(1)} %add.46), channel_id=1, source_target_pairs={{0,8},{8,0},{16,24},{24,16},{1,9},{9,1},{17,25},{25,17},{2,10},{10... | collective-permute-start | bytes 196616 | tf_op jit(solution)/shard_map/ppermute | solution.py:66
  34.7 3.8 %collective-permute-start.7 = (f32[128,128]{1,0:T(8,128)S(1)}, f32[128,128]{1,0:T(8,128)S(1)}, u32[]{:S(2)}, u32[]{:S(2)}) collective-permute-start(f32[128,128]{1,0:T(8,128)S(1)} %add.46), channel_id=1, source_target_pairs={{0,16},{8,24},{16,0},{24,8},{1,17},{9,25},{17,1},{25,9},{2,18},{10... | collective-permute-start | bytes 196616 | tf_op jit(solution)/shard_map/ppermute | solution.py:66
  38.6 3.9 %causal.1 = bf16[192,2048]{1,0:T(8,128)(2,1)} custom-call(bf16[192,2048]{1,0:T(8,128)(2,1)S(1)} %bitcast.21, bf16[192,2048]{1,0:T(8,128)(2,1)S(1)} %bitcast.24, bf16[128,2048]{1,0:T(8,128)(2,1)} %collective-permute-done.early_ref, f32[128,256]{1,0:T(8,128)S(1)} %maximum_maximum_fusion.base_ref, bf16[192,2048]{1,0:T(8,128)(2,1)S(1)} %constant_dynamic-update-slice_fusion.2.og_ref), custom_call_target="tpu_custom_call" | custom-call | flops 4000000000 | bytes 3000000 | tf_op jit(solution)/shard_map/causal/pallas_call | solution.py:179
  42.4 5.8 %collective-permute-done.6 = f32[128,128]{1,0:T(8,128)S(1)} collective-permute-done((f32[128,128]{1,0:T(8,128)S(1)}, f32[128,128]{1,0:T(8,128)S(1)}, u32[]{:S(2)}, u32[]{:S(2)}) %collective-permute-start.6) | collective-permute-done | bytes 65568 | tf_op jit(solution)/shard_map/ppermute | solution.py:66
  48.2 2.6 %collective-permute-done.7 = f32[128,128]{1,0:T(8,128)S(1)} collective-permute-done((f32[128,128]{1,0:T(8,128)S(1)}, f32[128,128]{1,0:T(8,128)S(1)}, u32[]{:S(2)}, u32[]{:S(2)}) %collective-permute-start.7) | collective-permute-done | bytes 65568 | tf_op jit(solution)/shard_map/ppermute | solution.py:66
  50.8 1.8 %collective-permute-done.8 = f32[128,128]{1,0:T(8,128)S(1)} collective-permute-done((f32[128,128]{1,0:T(8,128)S(1)}, f32[128,128]{1,0:T(8,128)S(1)}, u32[]{:S(2)}, u32[]{:S(2)}) %collective-permute-start.8) | collective-permute-done | bytes 65568 | tf_op jit(solution)/shard_map/ppermute | solution.py:66
  52.6 0.1 rev.8
  52.7 0.6 %broadcast_multiply_fusion = f32[128,128]{1,0:T(8,128)} fusion(f32[128,128]{1,0:T(8,128)S(1)} %rev.8), kind=kLoop, calls=%fused_computation.10 | loop fusion | flops 16384 | bytes 131072 | tf_op jit(solution)/shard_map/mul | solution.py:212
  53.4 4.1 %adjoint.1 = (bf16[192,2048]{1,0:T(8,128)(2,1)}, bf16[192,2048]{1,0:T(8,128)(2,1)}) custom-call(bf16[192,2048]{1,0:T(8,128)(2,1)S(1)} %bitcast.27, bf16[192,2048]{1,0:T(8,128)(2,1)S(1)} %constant_dynamic-update-slice_fusion.2.og_ref, bf16[128,2048]{1,0:T(8,128)(2,1)} %collective-permute-done.4.late_ref, bf16[192,2048]{1,0:T(8,128)(2,1)S(1)} %bitcast.22, ...), custom_call_target="tpu_custom_call" | custom-call | flops 4000000000 | bytes 3000000 | tf_op jit(solution)/shard_map/adjoint/pallas_call | solution.py:179
  (16 shorter events, 0.1 us)
Async XLA Ops:
  0.6 5.1 %copy-start = (bf16[1,192,2048]{2,1,0:T(8,128)(2,1)S(1)}, bf16[1,192,2048]{2,1,0:T(8,128)(2,1)}, u32[]{:S(2)}) copy-start(bf16[1,192,2048]{2,1,0:T(8,128)(2,1)} %param.6) | copy-start | bytes 2359300
  2.6 11.0 %collective-permute-start.1 = (bf16[48,2048]{1,0:T(8,128)(2,1)}, bf16[48,2048]{1,0:T(8,128)(2,1)}, u32[]{:S(2)}, u32[]{:S(2)}) collective-permute-start(bf16[48,2048]{1,0:T(8,128)(2,1)} %get-tuple-element.9), channel_id=1, source_target_pairs={{0,2},{2,0},{4,6},{6,4},{1,3},{3,1},{5,7},{7,5},{8,10},{10,8},{12,... | collective-permute-start | bytes 589832 | tf_op jit(solution)/shard_map/ppermute | solution.py:51
  3.1 11.6 %collective-permute-start.2 = (bf16[48,2048]{1,0:T(8,128)(2,1)}, bf16[48,2048]{1,0:T(8,128)(2,1)}, u32[]{:S(2)}, u32[]{:S(2)}) collective-permute-start(bf16[48,2048]{1,0:T(8,128)(2,1)} %get-tuple-element.10), channel_id=1, source_target_pairs={{0,4},{2,6},{4,0},{6,2},{1,5},{3,7},{5,1},{7,3},{8,12},{10,14},{12... | collective-permute-start | bytes 589832 | tf_op jit(solution)/shard_map/ppermute | solution.py:51
  5.6 10.1 %collective-permute-start.3 = (bf16[48,2048]{1,0:T(8,128)(2,1)S(1)}, bf16[48,2048]{1,0:T(8,128)(2,1)}, u32[]{:S(2)}, u32[]{:S(2)}) collective-permute-start(bf16[48,2048]{1,0:T(8,128)(2,1)S(1)} %get-tuple-element.8), channel_id=1, source_target_pairs={{0,6},{2,4},{4,2},{6,0},{1,7},{3,5},{5,3},{7,1},{8,14},{10,12},{12... | collective-permute-start | bytes 589832 | tf_op jit(solution)/shard_map/ppermute | solution.py:51
  5.7 6.5 %copy-start.3 = (f32[128,128]{1,0:T(8,128)S(1)}, f32[128,128]{1,0:T(8,128)}, u32[]{:S(2)}) copy-start(f32[128,128]{1,0:T(8,128)} %param.9) | copy-start | bytes 196612
  7.7 15.6 %collective-permute-start = (bf16[128,2048]{1,0:T(8,128)(2,1)}, bf16[128,2048]{1,0:T(8,128)(2,1)}, u32[]{:S(2)}, u32[]{:S(2)}) collective-permute-start(bf16[128,2048]{1,0:T(8,128)(2,1)} %fusion.1), channel_id=1, source_target_pairs={{0,8},{8,16},{16,24},{1,9},{9,17},{17,25},{2,10},{10,18},{18,26},{... | collective-permute-start | bytes 1572872 | tf_op jit(solution)/shard_map/ppermute | solution.py:26
  12.5 10.9 %copy-start.2 = (bf16[1,192,2048]{2,1,0:T(8,128)(2,1)S(1)}, bf16[1,192,2048]{2,1,0:T(8,128)(2,1)}, u32[]{:S(2)}) copy-start(bf16[1,192,2048]{2,1,0:T(8,128)(2,1)} %param.5) | copy-start | bytes 2359300
  13.5 9.8 %copy-start.1 = (bf16[1,192,2048]{2,1,0:T(8,128)(2,1)S(1)}, bf16[1,192,2048]{2,1,0:T(8,128)(2,1)}, u32[]{:S(2)}) copy-start(bf16[1,192,2048]{2,1,0:T(8,128)(2,1)} %param.7) | copy-start | bytes 2359300
  27.8 4.3 %collective-permute-start.5 = (f32[128,128]{1,0:T(8,128)S(1)}, f32[128,128]{1,0:T(8,128)S(1)}, u32[]{:S(2)}, u32[]{:S(2)}) collective-permute-start(f32[128,128]{1,0:T(8,128)S(1)} %lag_scores.1), channel_id=1, source_target_pairs={{0,1},{1,0},{2,3},{3,2},{4,5},{5,4},{6,7},{7,6},{8,9},{9,8},{10,11... | collective-permute-start | bytes 196616 | tf_op jit(solution)/shard_map/ppermute | solution.py:66
  30.3 23.1 %collective-permute-start.4 = (bf16[128,2048]{1,0:T(8,128)(2,1)}, bf16[128,2048]{1,0:T(8,128)(2,1)}, u32[]{:S(2)}, u32[]{:S(2)}) collective-permute-start(bf16[128,2048]{1,0:T(8,128)(2,1)} %fusion), channel_id=1, source_target_pairs={{8,0},{16,8},{24,16},{9,1},{17,9},{25,17},{10,2},{18,10},{26,18},{... | collective-permute-start | bytes 1572872 | tf_op jit(solution)/shard_map/ppermute | solution.py:26
  32.1 16.1 %collective-permute-start.6 = (f32[128,128]{1,0:T(8,128)S(1)}, f32[128,128]{1,0:T(8,128)S(1)}, u32[]{:S(2)}, u32[]{:S(2)}) collective-permute-start(f32[128,128]{1,0:T(8,128)S(1)} %add.46), channel_id=1, source_target_pairs={{0,8},{8,0},{16,24},{24,16},{1,9},{9,1},{17,25},{25,17},{2,10},{10... | collective-permute-start | bytes 196616 | tf_op jit(solution)/shard_map/ppermute | solution.py:66
  34.7 16.1 %collective-permute-start.7 = (f32[128,128]{1,0:T(8,128)S(1)}, f32[128,128]{1,0:T(8,128)S(1)}, u32[]{:S(2)}, u32[]{:S(2)}) collective-permute-start(f32[128,128]{1,0:T(8,128)S(1)} %add.46), channel_id=1, source_target_pairs={{0,16},{8,24},{16,0},{24,8},{1,17},{9,25},{17,1},{25,9},{2,18},{10... | collective-permute-start | bytes 196616 | tf_op jit(solution)/shard_map/ppermute | solution.py:66
  38.6 14.0 %collective-permute-start.8 = (f32[128,128]{1,0:T(8,128)S(1)}, f32[128,128]{1,0:T(8,128)S(1)}, u32[]{:S(2)}, u32[]{:S(2)}) collective-permute-start(f32[128,128]{1,0:T(8,128)S(1)} %add.46), channel_id=1, source_target_pairs={{0,24},{8,16},{16,8},{24,0},{1,25},{9,17},{17,9},{25,1},{2,26},{10... | collective-permute-start | bytes 196616 | tf_op jit(solution)/shard_map/ppermute | solution.py:66

commit v2 on v1

v2 whole, which is shorter than its diff:
```python
import functools
import math

import jax
import jax.numpy as jnp
from jax import lax
from jax.experimental import pallas as pl
from jax.experimental.pallas import tpu as pltpu
from jax.sharding import PartitionSpec as P

LANES = 128
BLOCK = 32
STEP = 4 * LANES
VMEM = pl.BlockSpec(memory_space=pltpu.VMEM)
ANYWHERE = pl.BlockSpec(memory_space=pl.ANY)
SCALAR = pl.BlockSpec(memory_space=pltpu.SMEM)


def in_hbm(value):
    return pltpu.with_memory_space_constraint(value, pltpu.HBM)


def widen(value):
    return value.astype(jnp.float32)


def product(left, right):
    return (widen(left) * widen(right)).astype(jnp.bfloat16)


def passed_along(value, axis, steps):
    count = lax.axis_size(axis)
    first, last = (max(0, -steps), min(count, count - steps))
    return lax.ppermute(value, axis, [(source, source + steps) for source in range(first, last)])


def partner(index, step, count):
    if count & (count - 1) == 0:
        return index ^ step
    return (index - step + count) % count


def target(index, step, count):
    if count & (count - 1) == 0:
        return index ^ step
    return (index + step) % count


def exchanged(parts, axis):
    count = lax.axis_size(axis)
    brought = []
    for step, part in enumerate(parts, 1):
        pairs = [(index, target(index, step, count)) for index in range(count)]
        brought.append(lax.ppermute(part, axis, pairs))
    return brought


def add_kernel(left_ref, right_ref, out_ref):
    out_ref[...] = left_ref[...] + right_ref[...]


def summed(value, axis, after=None):
    count = lax.axis_size(axis)
    if count & (count - 1):
        return lax.psum(value, axis)

    def brought(step):
        return lax.ppermute(value, axis, [(index, index ^ step) for index in range(count)])

    if count == 4:
        parts = [value] + [brought(step) for step in range(1, count)]
        if after is not None:
            parts, after = lax.optimization_barrier((parts, after))
        return (parts[0] + parts[1]) + (parts[2] + parts[3])
    step = 1
    while step < count:
        part = brought(step)
        if after is not None:
            part, after = lax.optimization_barrier((part, after))
        value = pl.pallas_call(
            add_kernel,
            in_specs=[VMEM] * 2,
            out_specs=VMEM,
            out_shape=jax.ShapeDtypeStruct(value.shape, value.dtype),
            name="add",
            compiler_params=pltpu.CompilerParams(vmem_limit_bytes=LIMIT * 1024 * 1024),
        )(value, part)
        step *= 2
    return value


def windows(rows, blocks, height):
    return jnp.concatenate([rows[BLOCK * b : BLOCK * b + height] for b in range(blocks)], axis=1)


def bands(base, count, width):
    rows = []
    for group in range(count):
        row = jnp.broadcast_to(base[group : group + 1, :], (BLOCK, base.shape[1]))
        row = pltpu.roll(row, 0, 1, stride=1, stride_axis=0)
        rows.append(row[:, :width].astype(jnp.bfloat16))
    return jnp.concatenate(rows, axis=0)


def convolved(base, window, blocks, taps, group_width):
    count = LANES // group_width
    every = jnp.dot(
        bands(base, count, taps + BLOCK),
        windows(window, blocks, taps + BLOCK),
        preferred_element_type=jnp.float32,
    )
    lane_group = lax.broadcasted_iota(jnp.int32, (BLOCK, LANES), 1) // group_width
    outs = []
    for b in range(blocks):
        columns = slice(b * LANES, (b + 1) * LANES)
        out = every[:BLOCK, columns]
        for group in range(1, count):
            out = jnp.where(
                lane_group == group, every[group * BLOCK : (group + 1) * BLOCK, columns], out
            )
        outs.append(out)
    return jnp.concatenate(outs, axis=0)


def tiles(channels, group_width):
    count = LANES // group_width
    for tile in range(channels // LANES):
        yield slice(tile * LANES, (tile + 1) * LANES), slice(tile * count, (tile + 1) * count)


def send_out(stage_ref, out_ref, sem, c):
    if c.stop % STEP == 0 or c.stop == stage_ref.shape[1]:
        begin = (c.stop - 1) // STEP * STEP
        columns = pl.ds(begin, c.stop - begin)
        copy = pltpu.make_async_copy(
            stage_ref.at[:, columns], out_ref.at[:, columns], sem.at[begin // STEP]
        )
        copy.start()
        return [copy]
    return []


def pack_kernel(count, grad_ref, k_ref, v_ref, *refs):
    parts, (tail_ref, k_stage, v_stage, stage, part_sem, tail_sem) = refs[:-6], refs[-6:]
    here = lax.axis_index("tp")
    height = k_stage.shape[0]
    width = parts[0].shape[1]
    below = pl.ds(k_ref.shape[0] - height, height)
    tails = [
        pltpu.make_async_copy(ref.at[below], into, tail_sem.at[n])
        for n, (ref, into) in enumerate([(k_ref, k_stage), (v_ref, v_stage)])
    ]
    cuts = []
    for n, part in enumerate(parts):
        place = target(here, n + 1, count) * width
        columns = pl.ds(pl.multiple_of(place, width), width)
        cuts.append(pltpu.make_async_copy(grad_ref.at[:, columns], part, part_sem.at[n]))
    for copy in tails + cuts:
        copy.start()
    for copy in tails:
        copy.wait()
    stage[...] = product(k_stage[...], v_stage[...])
    out = pltpu.make_async_copy(stage, tail_ref, tail_sem.at[0])
    out.start()
    for copy in [out] + cuts:
        copy.wait()


def gather_kernel(count, grad_ref, q_ref, *refs):
    parts, refs = refs[: count - 1], refs[count - 1 :]
    og_refs, (head_ref, q_stage, own_sem, q_sem) = refs[:HALVES], refs[HALVES:]
    height, width = parts[0].shape
    piece = width // HALVES
    here = lax.axis_index("tp")

    def rows_of(step):
        return pl.ds(pl.multiple_of(partner(here, step, count) * height, height), height)

    copies = [pltpu.make_async_copy(q_ref.at[pl.ds(0, q_stage.shape[0])], q_stage, q_sem)]
    for half, og_ref in enumerate(og_refs):
        columns = pl.ds(pl.multiple_of(here * width + half * piece, piece), piece)
        own = pltpu.make_async_copy(
            grad_ref.at[:, columns], og_ref.at[rows_of(0)], own_sem.at[half]
        )
        copies.append(own)
    for copy in copies:
        copy.start()
    for half, og_ref in enumerate(og_refs):
        for step, part in enumerate(parts, 1):
            og_ref[rows_of(step), :] = part[:, half * piece : (half + 1) * piece]
    for copy in copies:
        copy.wait()
    for half, og_ref in enumerate(og_refs):
        c = slice(half * piece, (half + 1) * piece)
        head_ref[:, c] = product(og_ref[: q_stage.shape[0], :], q_stage[:, c])


def columns_of(refs, c):
    width = refs[0].shape[1]
    half = c.start // width
    return refs[half][:, c.start - half * width : c.stop - half * width]


def scores_kernel(taps, group_width, q_ref, *refs):
    og_refs, (k_ref, v_ref, early_ref, out_ref) = refs[:HALVES], refs[HALVES:]
    blocks = k_ref.shape[0] // BLOCK
    count = LANES // group_width
    upward = 7 - lax.broadcasted_iota(jnp.int32, (8, LANES), 0)
    lane = lax.broadcasted_iota(jnp.int32, (BLOCK, blocks * LANES), 1)
    lane_group = (lane % LANES) // group_width
    for c, rows in tiles(k_ref.shape[1], group_width):
        grad_mix = widen(columns_of(og_refs, c)) * widen(q_ref[:, c])
        turned = []
        for b in range(blocks):
            for end in range((b + 1) * BLOCK, b * BLOCK, -8):
                eight = grad_mix[end - 8 : end]
                turned.append(jnp.take_along_axis(eight, upward, axis=0, mode="promise_in_bounds"))
        own = windows(jnp.concatenate(turned, axis=0).astype(jnp.bfloat16), blocks, BLOCK)
        window = jnp.concatenate([early_ref[:, c], product(k_ref[:, c], v_ref[:, c])], axis=0)
        split = [jnp.where(lane_group == g, own, jnp.zeros_like(own)) for g in range(count)]
        scores = lax.dot_general(
            jnp.concatenate(split, axis=0),
            windows(window, blocks, taps + BLOCK),
            (((1,), (1,)), ((), ())),
            preferred_element_type=jnp.float32,
        )
        spare = jnp.zeros((scores.shape[0], 2 * taps - scores.shape[1]), jnp.float32)
        scores = jnp.concatenate([scores, spare], axis=1)
        sums = []
        for g in range(count):
            part = scores[g * BLOCK : (g + 1) * BLOCK]
            part = pltpu.roll(part, taps - BLOCK, 1, stride=1, stride_axis=0)[:, taps:]
            sums.append(jnp.sum(part, axis=0, keepdims=True))
        out_ref[rows, :] = jnp.concatenate(sums, axis=0)


def mixed_kernel(taps, group_width, k_ref, v_ref, early_ref, filter_ref, *refs):
    og_refs, (out_ref, stage_ref, sem) = refs[:HALVES], refs[HALVES:]
    blocks = k_ref.shape[0] // BLOCK
    tap = lax.broadcasted_iota(jnp.int32, (taps, 2 * taps), 0)
    place = lax.broadcasted_iota(jnp.int32, (taps, 2 * taps), 1)
    turn = (tap + place == taps).astype(jnp.bfloat16)
    base = jnp.dot(filter_ref[...].astype(jnp.bfloat16), turn, preferred_element_type=jnp.float32)
    copies = []
    for c, rows in tiles(k_ref.shape[1], group_width):
        window = jnp.concatenate([early_ref[:, c], product(k_ref[:, c], v_ref[:, c])], axis=0)
        mixed = convolved(base[rows], window, blocks, taps, group_width)
        stage_ref[:, c] = (widen(columns_of(og_refs, c)) * mixed).astype(jnp.bfloat16)
        copies += send_out(stage_ref, out_ref, sem, c)
    for copy in copies:
        copy.wait()


def back_kernel(taps, group_width, q_ref, k_ref, v_ref, filter_ref, *refs):
    og_refs, refs = refs[:HALVES], refs[HALVES:]
    late_ref, kg_ref, vg_ref, k_stage, v_stage, k_sem, v_sem = refs
    blocks = k_ref.shape[0] // BLOCK
    coeffs = widen(filter_ref[...].astype(jnp.bfloat16))
    base = jnp.concatenate([coeffs, jnp.zeros_like(coeffs)], axis=1)
    copies = []
    for c, rows in tiles(k_ref.shape[1], group_width):
        grad_mix = product(columns_of(og_refs, c), q_ref[:, c])
        window = jnp.concatenate([grad_mix, late_ref[:, c]], axis=0)
        back = convolved(base[rows], window, blocks, taps, group_width)
        k_stage[:, c] = (back * widen(v_ref[:, c])).astype(jnp.bfloat16)
        v_stage[:, c] = (back * widen(k_ref[:, c])).astype(jnp.bfloat16)
        copies += send_out(k_stage, kg_ref, k_sem, c) + send_out(v_stage, vg_ref, v_sem, c)
    for copy in copies:
        copy.wait()


def call(kernel, name, args, outs, staged, cost):
    steps = -(-outs[0].shape[-1] // STEP)
    stages = [pltpu.VMEM(o.shape, o.dtype) for o in outs] + [pltpu.SemaphoreType.DMA((steps,)) for _ in outs]
    return pl.pallas_call(
        kernel,
        in_specs=[SCALAR if a.dtype == jnp.int32 else VMEM for a in args],
        out_specs=[ANYWHERE if staged else VMEM for _ in outs],
        out_shape=outs,
        scratch_shapes=stages if staged else [],
        name=name,
        cost_estimate=pl.CostEstimate(flops=cost, bytes_accessed=1000, transcendentals=0),
        compiler_params=pltpu.CompilerParams(vmem_limit_bytes=LIMIT * 1024 * 1024),
    )(*args)


def local(queries, keys, values, out_grad, filters):
    q, k, v = queries[0], keys[0], values[0]
    rows, channels = q.shape
    groups, taps = filters.shape
    group_width = channels // groups
    wide = jax.ShapeDtypeStruct((rows, channels), jnp.bfloat16)
    edge = jax.ShapeDtypeStruct((taps, channels), jnp.bfloat16)
    small = jax.ShapeDtypeStruct((groups, taps), jnp.float32)
    half = jax.ShapeDtypeStruct((rows, channels // HALVES), jnp.bfloat16)
    count = lax.axis_size("tp")
    height = rows // count
    piece = jax.ShapeDtypeStruct((height, channels), jnp.bfloat16)
    *parts, tail = pl.pallas_call(
        functools.partial(pack_kernel, count),
        in_specs=[ANYWHERE] * 3,
        out_specs=[ANYWHERE] * count,
        out_shape=[piece] * (count - 1) + [edge],
        scratch_shapes=[pltpu.VMEM(edge.shape, edge.dtype)] * 3
        + [pltpu.SemaphoreType.DMA((count - 1,)), pltpu.SemaphoreType.DMA((2,))],
        name="pack",
        compiler_params=pltpu.CompilerParams(vmem_limit_bytes=LIMIT * 1024 * 1024),
    )(*[in_hbm(a) for a in (out_grad[0], k, v)])
    early = passed_along(tail, "ctx", 1)
    parts = exchanged(parts, "tp")
    if height % 16 == 0:
        *grads, head = pl.pallas_call(
            functools.partial(gather_kernel, count),
            in_specs=[ANYWHERE] * 2 + [VMEM] * (count - 1),
            out_specs=[VMEM] * (HALVES + 1),
            out_shape=[half] * HALVES + [edge],
            scratch_shapes=[pltpu.VMEM(edge.shape, edge.dtype)]
            + [pltpu.SemaphoreType.DMA((HALVES,)), pltpu.SemaphoreType.DMA],
            name="gather",
            compiler_params=pltpu.CompilerParams(vmem_limit_bytes=LIMIT * 1024 * 1024),
        )(in_hbm(out_grad[0]), q, *parts)
    else:
        here = lax.axis_index("tp")
        own = lax.dynamic_slice_in_dim(out_grad[0], here * channels, channels, 1)
        grad = jnp.zeros(wide.shape, wide.dtype)
        for step, part in enumerate([own] + parts):
            place = partner(here, step, count)
            grad = lax.dynamic_update_slice_in_dim(grad, part, place * height, 0)
        head = product(grad[:taps], q[:taps])
        grads = jnp.split(grad, HALVES, axis=1)
    late = passed_along(head, "ctx", -1)
    work = functools.partial
    (lags,) = call(
        work(scores_kernel, taps, group_width), "lag_scores", (q, *grads, k, v, early), [small], False, COST
    )
    (query_grad,) = call(
        work(mixed_kernel, taps, group_width), "causal", (k, v, early, filters, *grads), [wide], True, COST
    )
    lags = summed(lags, "dp", query_grad)
    key_grad, value_grad = call(
        work(back_kernel, taps, group_width), "adjoint", (q, k, v, filters, *grads, late), [wide, wide], True, COST
    )
    lags = summed(lags, "ctx", key_grad)
    scale = 1.0 / math.sqrt(lax.axis_size("dp") * lax.axis_size("ctx") * rows * group_width)
    return (query_grad[None], key_grad[None], value_grad[None], jnp.flip(lags, 1) * scale)


COST = 100_000_000
HALVES = 1
LIMIT = 8


def solution(mesh):
    in_specs = (
        P("dp", "ctx", "tp"),
        P("dp", "ctx", "tp"),
        P("dp", "ctx", "tp"),
        P("dp", ("ctx", "tp"), None),
        P("tp", None),
    )
    out_specs = (P("dp", "ctx", "tp"), P("dp", "ctx", "tp"), P("dp", "ctx", "tp"), P("tp", None))
    return jax.shard_map(local, mesh=mesh, in_specs=in_specs, out_specs=out_specs, check_vma=False)
```

time: 57.8 us -> 39.8 us (0.69)
  local copies, waits for them, and re-layouts: 6.25 us -> 0.09 us
  waiting for transfers between devices: 17.5 us -> 12.9 us
  other arithmetic: 3.69 us -> 0.66 us
  Pallas kernels: 12.3 us -> 10.3 us
  starting transfers between devices: 16.9 us -> 15 us
    dynamic_update_slice x4 -> x0, local copies, waits for them, and re-layouts: 3.93 us -> none  [the longest x3 2.91 us: exchanged(): result = lax.dynamic_update_slice_in_dim(result, part, source * height, 0)]
    ppermute x2, waiting for transfers between devices: 6.75 us -> 3.48 us  [passed_along(): lax.ppermute(value, axis, [(source, source + steps) for source in range(f...]
    convert_element_type x3 -> x0, other arithmetic: 2.92 us -> none  [the longest x2 2.92 us: product(): return (widen(left) * widen(right)).astype(jnp.bfloat16)]
    pallas_call x3 -> x6, Pallas kernels: 12.3 us -> 10.3 us  [the longest x3 7.62 us: call(): pl.pallas_call(kernel, in_specs=[SCALAR if a.dtype == jnp.int32 else VMEM...]
    dynamic_slice x1 -> x0, local copies, waits for them, and re-layouts: 1.98 us -> none  [exchanged(): lax.dynamic_slice_in_dim(rows, peer(here, step, count) * width, width, 1)]
    ppermute x7, waiting for transfers between devices: 10.7 us -> 9.39 us  [the longest x3 5.62 us: exchanged(): brought.append(lax.ppermute(part, axis, pairs))]
    ppermute x7, starting transfers between devices: 11.2 us -> 9.93 us  [the longest x4 6.78 us: brought(): lax.ppermute(value, axis, [(index, index ^ step) for index in range(count)])]
    ppermute x2, starting transfers between devices: 5.77 us -> 5.03 us  [passed_along(): lax.ppermute(value, axis, [(source, source + steps) for source in range(f...]
  transfers between devices with their start and end apart: 9 -> 9, of which waited for: 5 -> 5; matrix products, arithmetic and copies ran while one was open for 14% -> 0% of each run, Pallas kernels for 7% -> 22%
where the time goes in v2:
time: 39.8 us; the launch traced here: 39.6 us
  starting transfers between devices  15 us (38%)
  waiting for transfers between devices  12.9 us (32%)
  Pallas kernels  10.3 us (26%)
  between operations  0.73 us (2%)
  other arithmetic  0.66 us (2%)
    pallas_call x3, Pallas kernels, call(): pl.pallas_call(kernel, in_specs=[SCALAR if a.dtype == jnp.int32 else VMEM...  7.62 us
    ppermute x4, starting transfers between devices, brought(): lax.ppermute(value, axis, [(index, index ^ step) for index in range(count)])  6.78 us
    ppermute x3, waiting for transfers between devices, exchanged(): brought.append(lax.ppermute(part, axis, pairs))  5.62 us
    ppermute x2, starting transfers between devices, passed_along(): lax.ppermute(value, axis, [(source, source + steps) for source in range(f...  5.03 us
    ppermute x4, waiting for transfers between devices, brought(): lax.ppermute(value, axis, [(index, index ^ step) for index in range(count)])  3.76 us
    ppermute x2, waiting for transfers between devices, passed_along(): lax.ppermute(value, axis, [(source, source + steps) for source in range(f...  3.48 us
    ppermute x3, starting transfers between devices, exchanged(): brought.append(lax.ppermute(part, axis, pairs))  3.15 us
    pallas_call x1, Pallas kernels, local(): pl.pallas_call(functools.partial(pack_kernel, count), in_specs=[ANYWHERE]...  1.48 us
  transfers between devices with their start and end apart: 9, of which 5 were waited for; matrix products, arithmetic and copies ran while one was open for 0% of the time, Pallas kernels for 22%

profile of v2, /device:TPU:0, one launch (start us, length us, event | category | flops | bytes accessed | tf_op | source)
XLA Modules:
  0.0 39.6 jit_solution(10854610344723821722)
XLA Ops:
  0.6 0.0 copy-start.2
  0.6 1.5 %pack.1 = (bf16[48,2048]{1,0:T(8,128)(2,1)S(1)}, bf16[48,2048]{1,0:T(8,128)(2,1)S(1)}, bf16[48,2048]{1,0:T(8,128)(2,1)S(1)}, bf16[128,2048]{1,0:T(8,128)(2,1)S(1)}) custom-call(bf16[48,8192]{1,0:T(8,128)(2,1)} %bitcast.18, bf16[192,2048]{1,0:T(8,128)(2,1)} %bitcast.7, bf16[192,2048]{1,0:T(8,128)(2,1)} %bitcast.11), custom_call_target="tpu_custom_call" | custom-call | tf_op jit(solution)/shard_map/pack/pallas_call | solution.py:299
  2.1 0.5 %collective-permute-start.1 = (bf16[48,2048]{1,0:T(8,128)(2,1)S(1)}, bf16[48,2048]{1,0:T(8,128)(2,1)S(1)}, u32[]{:S(2)}, u32[]{:S(2)}) collective-permute-start(bf16[48,2048]{1,0:T(8,128)(2,1)S(1)} %get-tuple-element.18), channel_id=1, source_target_pairs={{0,2},{2,0},{4,6},{6,4},{1,3},{3,1},{5,7},{7,5},{8,10},{10,8},{12,... | collective-permute-start | bytes 589832 | tf_op jit(solution)/shard_map/ppermute | solution.py:54
  2.6 2.6 %collective-permute-start.2 = (bf16[48,2048]{1,0:T(8,128)(2,1)S(1)}, bf16[48,2048]{1,0:T(8,128)(2,1)S(1)}, u32[]{:S(2)}, u32[]{:S(2)}) collective-permute-start(bf16[48,2048]{1,0:T(8,128)(2,1)S(1)} %get-tuple-element.19), channel_id=1, source_target_pairs={{0,4},{2,6},{4,0},{6,2},{1,5},{3,7},{5,1},{7,3},{8,12},{10,14},{12... | collective-permute-start | bytes 589832 | tf_op jit(solution)/shard_map/ppermute | solution.py:54
  5.2 0.1 collective-permute-start.3
  5.3 3.7 %collective-permute-start = (bf16[128,2048]{1,0:T(8,128)(2,1)S(1)}, bf16[128,2048]{1,0:T(8,128)(2,1)S(1)}, u32[]{:S(2)}, u32[]{:S(2)}) collective-permute-start(bf16[128,2048]{1,0:T(8,128)(2,1)S(1)} %get-tuple-element.17), channel_id=1, source_target_pairs={{0,8},{8,16},{16,24},{1,9},{9,17},{17,25},{2,10},{10,18},{18,26},{... | collective-permute-start | bytes 1572872 | tf_op jit(solution)/shard_map/ppermute | solution.py:34
  9.0 0.0 collective-permute-done.1.refs_0_
  9.0 1.9 %collective-permute-done.2.refs_1_ = bf16[48,2048]{1,0:T(8,128)(2,1)S(1)} collective-permute-done((bf16[48,2048]{1,0:T(8,128)(2,1)S(1)}, bf16[48,2048]{1,0:T(8,128)(2,1)S(1)}, u32[]{:S(2)}, u32[]{:S(2)}) %collective-permute-start.2) | collective-permute-done | bytes 196640 | tf_op jit(solution)/shard_map/ppermute | solution.py:54
  11.0 3.7 %collective-permute-done.3.refs_2_ = bf16[48,2048]{1,0:T(8,128)(2,1)S(1)} collective-permute-done((bf16[48,2048]{1,0:T(8,128)(2,1)S(1)}, bf16[48,2048]{1,0:T(8,128)(2,1)S(1)}, u32[]{:S(2)}, u32[]{:S(2)}) %collective-permute-start.3) | collective-permute-done | bytes 196640 | tf_op jit(solution)/shard_map/ppermute | solution.py:54
  14.7 0.0 copy-done.2
  14.7 0.0 copy-start
  14.7 0.0 copy-start.1
  14.7 1.2 %gather.1 = (bf16[192,2048]{1,0:T(8,128)(2,1)S(1)}, bf16[128,2048]{1,0:T(8,128)(2,1)S(1)}) custom-call(bf16[48,8192]{1,0:T(8,128)(2,1)} %bitcast.19, bf16[192,2048]{1,0:T(8,128)(2,1)S(1)} %bitcast.15, bf16[48,2048]{1,0:T(8,128)(2,1)S(1)} %collective-permute-done.1.refs_0_, bf16[48,2048]{1,0:T(8,128)(2,1)S(1)} %collective-permute-done.2.refs_1_, ...), custom_call_target="tpu_custom_call" | custom-call | tf_op jit(solution)/shard_map/gather/pallas_call | solution.py:312
  15.9 1.3 %collective-permute-start.4 = (bf16[128,2048]{1,0:T(8,128)(2,1)S(1)}, bf16[128,2048]{1,0:T(8,128)(2,1)S(1)}, u32[]{:S(2)}, u32[]{:S(2)}) collective-permute-start(bf16[128,2048]{1,0:T(8,128)(2,1)S(1)} %get-tuple-element.22), channel_id=1, source_target_pairs={{8,0},{16,8},{24,16},{9,1},{17,9},{25,17},{10,2},{18,10},{26,18},{... | collective-permute-start | bytes 1572872 | tf_op jit(solution)/shard_map/ppermute | solution.py:34
  17.2 3.5 %collective-permute-done.early_ref.refs_3_ = bf16[128,2048]{1,0:T(8,128)(2,1)S(1)} collective-permute-done((bf16[128,2048]{1,0:T(8,128)(2,1)S(1)}, bf16[128,2048]{1,0:T(8,128)(2,1)S(1)}, u32[]{:S(2)}, u32[]{:S(2)}) %collective-permute-start) | collective-permute-done | bytes 524320 | tf_op jit(solution)/shard_map/ppermute | solution.py:34
  20.7 0.0 copy-done
  20.7 0.0 copy-done.1
  20.7 2.0 %lag_scores.1.left_ref = f32[128,128]{1,0:T(8,128)S(1)} custom-call(bf16[192,2048]{1,0:T(8,128)(2,1)S(1)} %bitcast.16, bf16[192,2048]{1,0:T(8,128)(2,1)S(1)} %get-tuple-element.21.refs_0_, bf16[192,2048]{1,0:T(8,128)(2,1)S(1)} %bitcast.8, bf16[192,2048]{1,0:T(8,128)(2,1)S(1)} %bitcast.12, bf16[128,2048]{1,0:T(8,128)(2,1)S(1)} %collective-permute-done.early_ref.refs_3_), custom_call_target="tpu_custom_call" | custom-call | flops 100000000 | bytes 1000 | tf_op jit(solution)/shard_map/lag_scores/pallas_call | solution.py:275
  22.6 1.6 %collective-permute-start.5 = (f32[128,128]{1,0:T(8,128)S(1)}, f32[128,128]{1,0:T(8,128)S(1)}, u32[]{:S(2)}, u32[]{:S(2)}) collective-permute-start(f32[128,128]{1,0:T(8,128)S(1)} %lag_scores.1.left_ref), channel_id=1, source_target_pairs={{0,1},{1,0},{2,3},{3,2},{4,5},{5,4},{6,7},{7,6},{8,9},{9,8},{10,11... | collective-permute-start | bytes 196616 | tf_op jit(solution)/shard_map/ppermute | solution.py:68
  24.2 0.0 copy-done.3
  24.2 2.8 %causal.1 = bf16[192,2048]{1,0:T(8,128)(2,1)} custom-call(bf16[192,2048]{1,0:T(8,128)(2,1)S(1)} %bitcast.9, bf16[192,2048]{1,0:T(8,128)(2,1)S(1)} %bitcast.13, bf16[128,2048]{1,0:T(8,128)(2,1)S(1)} %collective-permute-done.early_ref.refs_3_, f32[128,128]{1,0:T(8,128)S(1)} %copy-done.3, bf16[192,2048]{1,0:T(8,128)(2,1)S(1)} %get-tuple-element.21.refs_0_), custom_call_target="tpu_custom_call" | custom-call | flops 100000000 | bytes 1000 | tf_op jit(solution)/shard_map/causal/pallas_call | solution.py:275
  27.0 0.0 collective-permute-done.5.right_ref
  27.1 4.6 %collective-permute-start.8 = (f32[128,128]{1,0:T(8,128)S(1)}, f32[128,128]{1,0:T(8,128)S(1)}, u32[]{:S(2)}, u32[]{:S(2)}) collective-permute-start(f32[128,128]{1,0:T(8,128)S(1)} %add.16), channel_id=1, source_target_pairs={{0,24},{8,16},{16,8},{24,0},{1,25},{9,17},{17,9},{25,1},{2,26},{10... | collective-permute-start | bytes 196616 | tf_op jit(solution)/shard_map/ppermute | solution.py:68
  31.6 0.0 collective-permute-start.7
  31.6 0.6 %collective-permute-start.6 = (f32[128,128]{1,0:T(8,128)S(1)}, f32[128,128]{1,0:T(8,128)S(1)}, u32[]{:S(2)}, u32[]{:S(2)}) collective-permute-start(f32[128,128]{1,0:T(8,128)S(1)} %add.16), channel_id=1, source_target_pairs={{0,8},{8,0},{16,24},{24,16},{1,9},{9,1},{17,25},{25,17},{2,10},{10... | collective-permute-start | bytes 196616 | tf_op jit(solution)/shard_map/ppermute | solution.py:68
  32.3 0.0 collective-permute-done.4.refs_1_
  32.3 2.8 %adjoint.1 = (bf16[192,2048]{1,0:T(8,128)(2,1)}, bf16[192,2048]{1,0:T(8,128)(2,1)}) custom-call(bf16[192,2048]{1,0:T(8,128)(2,1)S(1)} %bitcast.17, bf16[192,2048]{1,0:T(8,128)(2,1)S(1)} %bitcast.10, bf16[192,2048]{1,0:T(8,128)(2,1)S(1)} %bitcast.14, f32[128,128]{1,0:T(8,128)S(1)} %copy-done.3, bf16[192,2048]{1,0:T(8,128)(2,1)S(1)} %get-tuple-element.21.refs_0_, ...), custom_call_target="tpu_custom_call" | custom-call | flops 100000000 | bytes 1000 | tf_op jit(solution)/shard_map/adjoint/pallas_call | solution.py:275
  35.1 1.0 %collective-permute-done.8 = f32[128,128]{1,0:T(8,128)S(1)} collective-permute-done((f32[128,128]{1,0:T(8,128)S(1)}, f32[128,128]{1,0:T(8,128)S(1)}, u32[]{:S(2)}, u32[]{:S(2)}) %collective-permute-start.8) | collective-permute-done | bytes 65568 | tf_op jit(solution)/shard_map/ppermute | solution.py:68
  36.1 2.8 %collective-permute-done.7 = f32[128,128]{1,0:T(8,128)S(1)} collective-permute-done((f32[128,128]{1,0:T(8,128)S(1)}, f32[128,128]{1,0:T(8,128)S(1)}, u32[]{:S(2)}, u32[]{:S(2)}) %collective-permute-start.7) | collective-permute-done | bytes 65568 | tf_op jit(solution)/shard_map/ppermute | solution.py:68
  38.9 0.0 collective-permute-done.6
  38.9 0.1 rev.4
  39.0 0.6 %broadcast_multiply_fusion = f32[128,128]{1,0:T(8,128)} fusion(f32[128,128]{1,0:T(8,128)S(1)} %rev.4), kind=kLoop, calls=%fused_computation.1 | loop fusion | flops 16384 | bytes 131072 | tf_op jit(solution)/shard_map/mul | solution.py:345
  (3 shorter events, 0.0 us)
Async XLA Ops:
  0.6 14.0 %copy-start.2 = (bf16[1,192,2048]{2,1,0:T(8,128)(2,1)S(1)}, bf16[1,192,2048]{2,1,0:T(8,128)(2,1)}, u32[]{:S(2)}) copy-start(bf16[1,192,2048]{2,1,0:T(8,128)(2,1)} %param.5) | copy-start | bytes 2359300
  2.1 6.9 %collective-permute-start.1 = (bf16[48,2048]{1,0:T(8,128)(2,1)S(1)}, bf16[48,2048]{1,0:T(8,128)(2,1)S(1)}, u32[]{:S(2)}, u32[]{:S(2)}) collective-permute-start(bf16[48,2048]{1,0:T(8,128)(2,1)S(1)} %get-tuple-element.18), channel_id=1, source_target_pairs={{0,2},{2,0},{4,6},{6,4},{1,3},{3,1},{5,7},{7,5},{8,10},{10,8},{12,... | collective-permute-start | bytes 589832 | tf_op jit(solution)/shard_map/ppermute | solution.py:54
  2.6 8.3 %collective-permute-start.2 = (bf16[48,2048]{1,0:T(8,128)(2,1)S(1)}, bf16[48,2048]{1,0:T(8,128)(2,1)S(1)}, u32[]{:S(2)}, u32[]{:S(2)}) collective-permute-start(bf16[48,2048]{1,0:T(8,128)(2,1)S(1)} %get-tuple-element.19), channel_id=1, source_target_pairs={{0,4},{2,6},{4,0},{6,2},{1,5},{3,7},{5,1},{7,3},{8,12},{10,14},{12... | collective-permute-start | bytes 589832 | tf_op jit(solution)/shard_map/ppermute | solution.py:54
  5.2 9.4 %collective-permute-start.3 = (bf16[48,2048]{1,0:T(8,128)(2,1)S(1)}, bf16[48,2048]{1,0:T(8,128)(2,1)S(1)}, u32[]{:S(2)}, u32[]{:S(2)}) collective-permute-start(bf16[48,2048]{1,0:T(8,128)(2,1)S(1)} %get-tuple-element.20), channel_id=1, source_target_pairs={{0,6},{2,4},{4,2},{6,0},{1,7},{3,5},{5,3},{7,1},{8,14},{10,12},{12... | collective-permute-start | bytes 589832 | tf_op jit(solution)/shard_map/ppermute | solution.py:54
  5.3 15.4 %collective-permute-start = (bf16[128,2048]{1,0:T(8,128)(2,1)S(1)}, bf16[128,2048]{1,0:T(8,128)(2,1)S(1)}, u32[]{:S(2)}, u32[]{:S(2)}) collective-permute-start(bf16[128,2048]{1,0:T(8,128)(2,1)S(1)} %get-tuple-element.17), channel_id=1, source_target_pairs={{0,8},{8,16},{16,24},{1,9},{9,17},{17,25},{2,10},{10,18},{18,26},{... | collective-permute-start | bytes 1572872 | tf_op jit(solution)/shard_map/ppermute | solution.py:34
  14.7 6.0 %copy-start = (bf16[1,192,2048]{2,1,0:T(8,128)(2,1)S(1)}, bf16[1,192,2048]{2,1,0:T(8,128)(2,1)}, u32[]{:S(2)}) copy-start(bf16[1,192,2048]{2,1,0:T(8,128)(2,1)} %param.6) | copy-start | bytes 2359300
  14.7 6.0 %copy-start.1 = (bf16[1,192,2048]{2,1,0:T(8,128)(2,1)S(1)}, bf16[1,192,2048]{2,1,0:T(8,128)(2,1)}, u32[]{:S(2)}) copy-start(bf16[1,192,2048]{2,1,0:T(8,128)(2,1)} %param.7) | copy-start | bytes 2359300
  15.9 16.4 %collective-permute-start.4 = (bf16[128,2048]{1,0:T(8,128)(2,1)S(1)}, bf16[128,2048]{1,0:T(8,128)(2,1)S(1)}, u32[]{:S(2)}, u32[]{:S(2)}) collective-permute-start(bf16[128,2048]{1,0:T(8,128)(2,1)S(1)} %get-tuple-element.22), channel_id=1, source_target_pairs={{8,0},{16,8},{24,16},{9,1},{17,9},{25,17},{10,2},{18,10},{26,18},{... | collective-permute-start | bytes 1572872 | tf_op jit(solution)/shard_map/ppermute | solution.py:34
  20.7 3.5 %copy-start.3 = (f32[128,128]{1,0:T(8,128)S(1)}, f32[128,128]{1,0:T(8,128)}, u32[]{:S(2)}) copy-start(f32[128,128]{1,0:T(8,128)} %filter_ref.3) | copy-start | bytes 196612
  22.6 4.4 %collective-permute-start.5 = (f32[128,128]{1,0:T(8,128)S(1)}, f32[128,128]{1,0:T(8,128)S(1)}, u32[]{:S(2)}, u32[]{:S(2)}) collective-permute-start(f32[128,128]{1,0:T(8,128)S(1)} %lag_scores.1.left_ref), channel_id=1, source_target_pairs={{0,1},{1,0},{2,3},{3,2},{4,5},{5,4},{6,7},{7,6},{8,9},{9,8},{10,11... | collective-permute-start | bytes 196616 | tf_op jit(solution)/shard_map/ppermute | solution.py:68
  27.1 9.0 %collective-permute-start.8 = (f32[128,128]{1,0:T(8,128)S(1)}, f32[128,128]{1,0:T(8,128)S(1)}, u32[]{:S(2)}, u32[]{:S(2)}) collective-permute-start(f32[128,128]{1,0:T(8,128)S(1)} %add.16), channel_id=1, source_target_pairs={{0,24},{8,16},{16,8},{24,0},{1,25},{9,17},{17,9},{25,1},{2,26},{10... | collective-permute-start | bytes 196616 | tf_op jit(solution)/shard_map/ppermute | solution.py:68
  31.6 7.3 %collective-permute-start.7 = (f32[128,128]{1,0:T(8,128)S(1)}, f32[128,128]{1,0:T(8,128)S(1)}, u32[]{:S(2)}, u32[]{:S(2)}) collective-permute-start(f32[128,128]{1,0:T(8,128)S(1)} %add.16), channel_id=1, source_target_pairs={{0,16},{8,24},{16,0},{24,8},{1,17},{9,25},{17,1},{25,9},{2,18},{10... | collective-permute-start | bytes 196616 | tf_op jit(solution)/shard_map/ppermute | solution.py:68
  31.6 7.3 %collective-permute-start.6 = (f32[128,128]{1,0:T(8,128)S(1)}, f32[128,128]{1,0:T(8,128)S(1)}, u32[]{:S(2)}, u32[]{:S(2)}) collective-permute-start(f32[128,128]{1,0:T(8,128)S(1)} %add.16), channel_id=1, source_target_pairs={{0,8},{8,0},{16,24},{24,16},{1,9},{9,1},{17,25},{25,17},{2,10},{10... | collective-permute-start | bytes 196616 | tf_op jit(solution)/shard_map/ppermute | solution.py:68

commit v3 on v2

--- a/solution.py
+++ b/solution.py
@@ -55,38 +55,29 @@
     return brought
 
 
-def add_kernel(left_ref, right_ref, out_ref):
-    out_ref[...] = left_ref[...] + right_ref[...]
-
-
-def summed(value, axis, after=None):
-    count = lax.axis_size(axis)
-    if count & (count - 1):
-        return lax.psum(value, axis)
-
-    def brought(step):
-        return lax.ppermute(value, axis, [(index, index ^ step) for index in range(count)])
-
-    if count == 4:
-        parts = [value] + [brought(step) for step in range(1, count)]
-        if after is not None:
-            parts, after = lax.optimization_barrier((parts, after))
-        return (parts[0] + parts[1]) + (parts[2] + parts[3])
-    step = 1
-    while step < count:
-        part = brought(step)
-        if after is not None:
-            part, after = lax.optimization_barrier((part, after))
-        value = pl.pallas_call(
-            add_kernel,
-            in_specs=[VMEM] * 2,
-            out_specs=VMEM,
-            out_shape=jax.ShapeDtypeStruct(value.shape, value.dtype),
-            name="add",
-            compiler_params=pltpu.CompilerParams(vmem_limit_bytes=LIMIT * 1024 * 1024),
-        )(value, part)
-        step *= 2
-    return value
+def add_kernel(*refs):
+    *parts, out_ref = refs
+    total = [widen(part[...]) for part in parts]
+    while len(total) > 1:
+        total = [sum(total[n : n + 2][1:], total[n]) for n in range(0, len(total), 2)]
+    out_ref[...] = total[0].astype(out_ref.dtype)
+
+
+def added(parts, dtype):
+    return pl.pallas_call(
+        add_kernel,
+        in_specs=[VMEM] * len(parts),
+        out_specs=VMEM,
+        out_shape=jax.ShapeDtypeStruct(parts[0].shape, dtype),
+        name="add",
+        compiler_params=pltpu.CompilerParams(vmem_limit_bytes=LIMIT * 1024 * 1024),
+    )(*parts)
+
+
+def brought(value, step):
+    axes = ("ctx", "dp")
+    count = lax.axis_size("ctx") * lax.axis_size("dp")
+    return lax.ppermute(value, axes, [(index, index ^ step) for index in range(count)])
 
 
 def windows(rows, blocks, height):
@@ -141,7 +132,7 @@
 
 
 def pack_kernel(count, grad_ref, k_ref, v_ref, *refs):
-    parts, (tail_ref, k_stage, v_stage, stage, part_sem, tail_sem) = refs[:-6], refs[-6:]
+    parts, (tail_ref, k_stage, v_stage, part_sem, tail_sem) = refs[:count], refs[count:]
     here = lax.axis_index("tp")
     height = k_stage.shape[0]
     width = parts[0].shape[1]
@@ -152,47 +143,30 @@
     ]
     cuts = []
     for n, part in enumerate(parts):
-        place = target(here, n + 1, count) * width
+        place = target(here, n, count) * width
         columns = pl.ds(pl.multiple_of(place, width), width)
         cuts.append(pltpu.make_async_copy(grad_ref.at[:, columns], part, part_sem.at[n]))
     for copy in tails + cuts:
         copy.start()
     for copy in tails:
         copy.wait()
-    stage[...] = product(k_stage[...], v_stage[...])
-    out = pltpu.make_async_copy(stage, tail_ref, tail_sem.at[0])
-    out.start()
-    for copy in [out] + cuts:
+    tail_ref[...] = product(k_stage[...], v_stage[...])
+    for copy in cuts:
         copy.wait()
 
 
-def gather_kernel(count, grad_ref, q_ref, *refs):
-    parts, refs = refs[: count - 1], refs[count - 1 :]
-    og_refs, (head_ref, q_stage, own_sem, q_sem) = refs[:HALVES], refs[HALVES:]
+def gather_kernel(count, q_ref, *refs):
+    parts, og_refs, head_ref = refs[:count], refs[count:-1], refs[-1]
     height, width = parts[0].shape
     piece = width // HALVES
     here = lax.axis_index("tp")
-
-    def rows_of(step):
-        return pl.ds(pl.multiple_of(partner(here, step, count) * height, height), height)
-
-    copies = [pltpu.make_async_copy(q_ref.at[pl.ds(0, q_stage.shape[0])], q_stage, q_sem)]
-    for half, og_ref in enumerate(og_refs):
-        columns = pl.ds(pl.multiple_of(here * width + half * piece, piece), piece)
-        own = pltpu.make_async_copy(
-            grad_ref.at[:, columns], og_ref.at[rows_of(0)], own_sem.at[half]
-        )
-        copies.append(own)
-    for copy in copies:
-        copy.start()
-    for half, og_ref in enumerate(og_refs):
-        for step, part in enumerate(parts, 1):
-            og_ref[rows_of(step), :] = part[:, half * piece : (half + 1) * piece]
-    for copy in copies:
-        copy.wait()
+    head = head_ref.shape[0]
     for half, og_ref in enumerate(og_refs):
         c = slice(half * piece, (half + 1) * piece)
-        head_ref[:, c] = product(og_ref[: q_stage.shape[0], :], q_stage[:, c])
+        for step, part in enumerate(parts):
+            place = partner(here, step, count)
+            og_ref[pl.ds(pl.multiple_of(place * height, height), height), :] = part[:, c]
+        head_ref[:, c] = product(og_ref[:head, :], q_ref[:head, c])
 
 
 def columns_of(refs, c):
@@ -201,22 +175,25 @@
     return refs[half][:, c.start - half * width : c.stop - half * width]
 
 
-def scores_kernel(taps, group_width, q_ref, *refs):
-    og_refs, (k_ref, v_ref, early_ref, out_ref) = refs[:HALVES], refs[HALVES:]
-    blocks = k_ref.shape[0] // BLOCK
+def scores_kernel(taps, group_width, inner, q_ref, *refs):
+    og_refs, (k_ref, v_ref, *more_refs, out_ref) = refs[:HALVES], refs[HALVES:]
+    first, last = (taps, k_ref.shape[0]) if inner else (0, taps)
+    blocks = (last - first) // BLOCK
     count = LANES // group_width
     upward = 7 - lax.broadcasted_iota(jnp.int32, (8, LANES), 0)
     lane = lax.broadcasted_iota(jnp.int32, (BLOCK, blocks * LANES), 1)
     lane_group = (lane % LANES) // group_width
     for c, rows in tiles(k_ref.shape[1], group_width):
-        grad_mix = widen(columns_of(og_refs, c)) * widen(q_ref[:, c])
+        grad_mix = widen(columns_of(og_refs, c)[first:last]) * widen(q_ref[first:last, c])
         turned = []
         for b in range(blocks):
             for end in range((b + 1) * BLOCK, b * BLOCK, -8):
                 eight = grad_mix[end - 8 : end]
                 turned.append(jnp.take_along_axis(eight, upward, axis=0, mode="promise_in_bounds"))
         own = windows(jnp.concatenate(turned, axis=0).astype(jnp.bfloat16), blocks, BLOCK)
-        window = jnp.concatenate([early_ref[:, c], product(k_ref[:, c], v_ref[:, c])], axis=0)
+        window = product(k_ref[:last, c], v_ref[:last, c])
+        if not inner:
+            window = jnp.concatenate([more_refs[0][:, c], window], axis=0)
         split = [jnp.where(lane_group == g, own, jnp.zeros_like(own)) for g in range(count)]
         scores = lax.dot_general(
             jnp.concatenate(split, axis=0),
@@ -228,24 +205,41 @@
         scores = jnp.concatenate([scores, spare], axis=1)
         sums = []
         for g in range(count):
-            part = scores[g * BLOCK : (g + 1) * BLOCK]
-            part = pltpu.roll(part, taps - BLOCK, 1, stride=1, stride_axis=0)[:, taps:]
-            sums.append(jnp.sum(part, axis=0, keepdims=True))
-        out_ref[rows, :] = jnp.concatenate(sums, axis=0)
-
-
-def mixed_kernel(taps, group_width, k_ref, v_ref, early_ref, filter_ref, *refs):
-    og_refs, (out_ref, stage_ref, sem) = refs[:HALVES], refs[HALVES:]
-    blocks = k_ref.shape[0] // BLOCK
+            lags = scores[g * BLOCK : (g + 1) * BLOCK]
+            lags = pltpu.roll(lags, taps - BLOCK, 1, stride=1, stride_axis=0)[:, taps:]
+            sums.append(jnp.sum(lags, axis=0, keepdims=True))
+        sums = jnp.concatenate(sums, axis=0)
+        out_ref[rows, :] = sums if inner else (sums + more_refs[1][rows, :]).astype(out_ref.dtype)
+
+
+def turned_base(filter_ref):
+    taps = filter_ref.shape[1]
     tap = lax.broadcasted_iota(jnp.int32, (taps, 2 * taps), 0)
     place = lax.broadcasted_iota(jnp.int32, (taps, 2 * taps), 1)
     turn = (tap + place == taps).astype(jnp.bfloat16)
-    base = jnp.dot(filter_ref[...].astype(jnp.bfloat16), turn, preferred_element_type=jnp.float32)
+    return jnp.dot(filter_ref[...].astype(jnp.bfloat16), turn, preferred_element_type=jnp.float32)
+
+
+def inner_mixed_kernel(taps, group_width, k_ref, v_ref, filter_ref, out_ref):
+    blocks = (k_ref.shape[0] - taps) // BLOCK
+    base = turned_base(filter_ref)
+    for c, rows in tiles(k_ref.shape[1], group_width):
+        window = product(k_ref[:, c], v_ref[:, c])
+        out_ref[:, c] = convolved(base[rows], window, blocks, taps, group_width)
+
+
+def mixed_kernel(taps, group_width, k_ref, v_ref, early_ref, filter_ref, inner_ref, *refs):
+    og_refs, (out_ref, stage_ref, sem) = refs[:HALVES], refs[HALVES:]
+    blocks = taps // BLOCK
+    base = turned_base(filter_ref)
     copies = []
     for c, rows in tiles(k_ref.shape[1], group_width):
-        window = jnp.concatenate([early_ref[:, c], product(k_ref[:, c], v_ref[:, c])], axis=0)
+        window = product(k_ref[:taps, c], v_ref[:taps, c])
+        window = jnp.concatenate([early_ref[:, c], window], axis=0)
         mixed = convolved(base[rows], window, blocks, taps, group_width)
-        stage_ref[:, c] = (widen(columns_of(og_refs, c)) * mixed).astype(jnp.bfloat16)
+        og = columns_of(og_refs, c)
+        stage_ref[:taps, c] = (widen(og[:taps]) * mixed).astype(jnp.bfloat16)
+        stage_ref[taps:, c] = (widen(og[taps:]) * inner_ref[:, c]).astype(jnp.bfloat16)
         copies += send_out(stage_ref, out_ref, sem, c)
     for copy in copies:
         copy.wait()
@@ -292,6 +286,7 @@
     wide = jax.ShapeDtypeStruct((rows, channels), jnp.bfloat16)
     edge = jax.ShapeDtypeStruct((taps, channels), jnp.bfloat16)
     small = jax.ShapeDtypeStruct((groups, taps), jnp.float32)
+    thin = jax.ShapeDtypeStruct((groups, taps), TRAVEL)
     half = jax.ShapeDtypeStruct((rows, channels // HALVES), jnp.bfloat16)
     count = lax.axis_size("tp")
     height = rows // count
@@ -299,31 +294,28 @@
     *parts, tail = pl.pallas_call(
         functools.partial(pack_kernel, count),
         in_specs=[ANYWHERE] * 3,
-        out_specs=[ANYWHERE] * count,
-        out_shape=[piece] * (count - 1) + [edge],
-        scratch_shapes=[pltpu.VMEM(edge.shape, edge.dtype)] * 3
-        + [pltpu.SemaphoreType.DMA((count - 1,)), pltpu.SemaphoreType.DMA((2,))],
+        out_specs=[ANYWHERE] * count + [VMEM],
+        out_shape=[piece] * count + [edge],
+        scratch_shapes=[pltpu.VMEM(edge.shape, edge.dtype)] * 2
+        + [pltpu.SemaphoreType.DMA((count,)), pltpu.SemaphoreType.DMA((2,))],
         name="pack",
         compiler_params=pltpu.CompilerParams(vmem_limit_bytes=LIMIT * 1024 * 1024),
     )(*[in_hbm(a) for a in (out_grad[0], k, v)])
     early = passed_along(tail, "ctx", 1)
-    parts = exchanged(parts, "tp")
+    inner_rows = jax.ShapeDtypeStruct((rows - taps, channels), jnp.float32)
+    (inner,) = call(
+        functools.partial(inner_mixed_kernel, taps, group_width), "inner_causal", (k, v, filters), [inner_rows], False, COST
+    )
+    parts = parts[:1] + exchanged(parts[1:], "tp")
+    parts, inner = lax.optimization_barrier((parts, inner))
     if height % 16 == 0:
-        *grads, head = pl.pallas_call(
-            functools.partial(gather_kernel, count),
-            in_specs=[ANYWHERE] * 2 + [VMEM] * (count - 1),
-            out_specs=[VMEM] * (HALVES + 1),
-            out_shape=[half] * HALVES + [edge],
-            scratch_shapes=[pltpu.VMEM(edge.shape, edge.dtype)]
-            + [pltpu.SemaphoreType.DMA((HALVES,)), pltpu.SemaphoreType.DMA],
-            name="gather",
-            compiler_params=pltpu.CompilerParams(vmem_limit_bytes=LIMIT * 1024 * 1024),
-        )(in_hbm(out_grad[0]), q, *parts)
+        *grads, head = call(
+            functools.partial(gather_kernel, count), "gather", (q, *parts), [half] * HALVES + [edge], False, 1000
+        )
     else:
         here = lax.axis_index("tp")
-        own = lax.dynamic_slice_in_dim(out_grad[0], here * channels, channels, 1)
         grad = jnp.zeros(wide.shape, wide.dtype)
-        for step, part in enumerate([own] + parts):
+        for step, part in enumerate(parts):
             place = partner(here, step, count)
             grad = lax.dynamic_update_slice_in_dim(grad, part, place * height, 0)
         head = product(grad[:taps], q[:taps])
@@ -331,22 +323,33 @@
     late = passed_along(head, "ctx", -1)
     work = functools.partial
     (lags,) = call(
-        work(scores_kernel, taps, group_width), "lag_scores", (q, *grads, k, v, early), [small], False, COST
+        work(scores_kernel, taps, group_width, True), "inner_scores", (q, *grads, k, v), [small], False, COST
+    )
+    (lags,) = call(
+        work(scores_kernel, taps, group_width, False), "edge_scores", (q, *grads, k, v, early, lags), [thin], False, COST
     )
     (query_grad,) = call(
-        work(mixed_kernel, taps, group_width), "causal", (k, v, early, filters, *grads), [wide], True, COST
-    )
-    lags = summed(lags, "dp", query_grad)
+        work(mixed_kernel, taps, group_width), "causal", (k, v, early, filters, inner, *grads), [wide], True, COST
+    )
+    lags = [lags] + [brought(lags, step) for step in FIRST]
+    lags, query_grad = lax.optimization_barrier((lags, query_grad))
+    lags = added(lags, TRAVEL)
     key_grad, value_grad = call(
         work(back_kernel, taps, group_width), "adjoint", (q, k, v, filters, *grads, late), [wide, wide], True, COST
     )
-    lags = summed(lags, "ctx", key_grad)
+    lags = [lags] + [brought(lags, step) for step in SECOND]
+    lags, key_grad = lax.optimization_barrier((lags, key_grad))
+    lags = [widen(part) for part in lags]
+    lags = (lags[0] + lags[1]) + (lags[2] + lags[3])
     scale = 1.0 / math.sqrt(lax.axis_size("dp") * lax.axis_size("ctx") * rows * group_width)
     return (query_grad[None], key_grad[None], value_grad[None], jnp.flip(lags, 1) * scale)
 
 
 COST = 100_000_000
 HALVES = 1
+TRAVEL = jnp.bfloat16
+FIRST = (1,)
+SECOND = (2, 4, 6)
 LIMIT = 8
 
 

time: 39.8 us -> 36.7 us (0.922)
  waiting for transfers between devices: 12.9 us -> 8.92 us
  Pallas kernels: 10.3 us -> 11 us
    ppermute x4, waiting for transfers between devices: 3.76 us -> 1.41 us  [brought(): lax.ppermute(value, axes, [(index, index ^ step) for index in range(count)])]
    pallas_call x3 -> x6, Pallas kernels: 7.62 us -> 9.35 us  [call(): pl.pallas_call(kernel, in_specs=[SCALAR if a.dtype == jnp.int32 else VMEM...]
    ppermute x3, waiting for transfers between devices: 5.62 us -> 4.38 us  [exchanged(): brought.append(lax.ppermute(part, axis, pairs))]
    pallas_call x2 -> x1, Pallas kernels: 1.22 us -> 0.01 us  [added(): pl.pallas_call(add_kernel, in_specs=[VMEM] * len(parts), out_specs=VMEM,...]
  transfers between devices with their start and end apart: 9 -> 9, of which waited for: 5 -> 6; matrix products, arithmetic and copies ran while one was open for 0% -> 0% of each run, Pallas kernels for 22% -> 26%
where the time goes in v3:
time: 36.7 us; the launch traced here: 36.5 us
  starting transfers between devices  15.1 us (41%)
  Pallas kernels  11 us (30%)
  waiting for transfers between devices  8.92 us (24%)
  between operations  0.76 us (2%)
  other arithmetic  0.67 us (2%)
    pallas_call x6, Pallas kernels, call(): pl.pallas_call(kernel, in_specs=[SCALAR if a.dtype == jnp.int32 else VMEM...  9.35 us
    ppermute x4, starting transfers between devices, brought(): lax.ppermute(value, axes, [(index, index ^ step) for index in range(count)])  6.8 us
    ppermute x2, starting transfers between devices, passed_along(): lax.ppermute(value, axis, [(source, source + steps) for source in range(f...  5.16 us
    ppermute x3, waiting for transfers between devices, exchanged(): brought.append(lax.ppermute(part, axis, pairs))  4.38 us
    ppermute x3, starting transfers between devices, exchanged(): brought.append(lax.ppermute(part, axis, pairs))  3.15 us
    ppermute x2, waiting for transfers between devices, passed_along(): lax.ppermute(value, axis, [(source, source + steps) for source in range(f...  3.14 us
    pallas_call x1, Pallas kernels, local(): pl.pallas_call(functools.partial(pack_kernel, count), in_specs=[ANYWHERE]...  1.59 us
    ppermute x4, waiting for transfers between devices, brought(): lax.ppermute(value, axes, [(index, index ^ step) for index in range(count)])  1.41 us
  transfers between devices with their start and end apart: 9, of which 6 were waited for; matrix products, arithmetic and copies ran while one was open for 0% of the time, Pallas kernels for 26%

profile of v3, /device:TPU:0, one launch (start us, length us, event | category | flops | bytes accessed | tf_op | source)
XLA Modules:
  0.0 36.5 jit_solution(16970514744127502387)
XLA Ops:
  0.6 0.0 copy-start
  0.6 0.0 copy-start.1
  0.7 0.0 copy-start.3
  0.7 1.6 %pack.1 = (bf16[48,2048]{1,0:T(8,128)(2,1)S(1)}, bf16[48,2048]{1,0:T(8,128)(2,1)S(1)}, bf16[48,2048]{1,0:T(8,128)(2,1)S(1)}, bf16[48,2048]{1,0:T(8,128)(2,1)S(1)}, bf16[128,2048]{1,0:T(8,128)(2,1)S(1)}) custom-call(bf16[48,8192]{1,0:T(8,128)(2,1)} %bitcast.24, bf16[192,2048]{1,0:T(8,128)(2,1)} %bitcast.7, bf16[192,2048]{1,0:T(8,128)(2,1)} %bitcast.13), custom_call_target="tpu_custom_call" | custom-call | tf_op jit(solution)/shard_map/pack/pallas_call | solution.py:294
  2.3 0.5 %collective-permute-start = (bf16[48,2048]{1,0:T(8,128)(2,1)S(1)}, bf16[48,2048]{1,0:T(8,128)(2,1)S(1)}, u32[]{:S(2)}, u32[]{:S(2)}) collective-permute-start(bf16[48,2048]{1,0:T(8,128)(2,1)S(1)} %get-tuple-element.27), channel_id=1, source_target_pairs={{0,2},{2,0},{4,6},{6,4},{1,3},{3,1},{5,7},{7,5},{8,10},{10,8},{12,... | collective-permute-start | bytes 589832 | tf_op jit(solution)/shard_map/ppermute | solution.py:54
  2.8 2.6 %collective-permute-start.1 = (bf16[48,2048]{1,0:T(8,128)(2,1)S(1)}, bf16[48,2048]{1,0:T(8,128)(2,1)S(1)}, u32[]{:S(2)}, u32[]{:S(2)}) collective-permute-start(bf16[48,2048]{1,0:T(8,128)(2,1)S(1)} %get-tuple-element.28), channel_id=1, source_target_pairs={{0,4},{2,6},{4,0},{6,2},{1,5},{3,7},{5,1},{7,3},{8,12},{10,14},{12... | collective-permute-start | bytes 589832 | tf_op jit(solution)/shard_map/ppermute | solution.py:54
  5.3 0.1 collective-permute-start.2
  5.4 3.9 %collective-permute-start.3 = (bf16[128,2048]{1,0:T(8,128)(2,1)S(1)}, bf16[128,2048]{1,0:T(8,128)(2,1)S(1)}, u32[]{:S(2)}, u32[]{:S(2)}) collective-permute-start(bf16[128,2048]{1,0:T(8,128)(2,1)S(1)} %get-tuple-element.35), channel_id=1, source_target_pairs={{0,8},{8,16},{16,24},{1,9},{9,17},{17,25},{2,10},{10,18},{18,26},{... | collective-permute-start | bytes 1572872 | tf_op jit(solution)/shard_map/ppermute | solution.py:34
  9.3 0.0 copy-done
  9.3 0.0 copy-done.1
  9.3 1.1 %inner_causal.1.inner_ref = f32[64,2048]{1,0:T(8,128)S(1)} custom-call(bf16[192,2048]{1,0:T(8,128)(2,1)S(1)} %bitcast.8, bf16[192,2048]{1,0:T(8,128)(2,1)S(1)} %bitcast.14, f32[128,128]{1,0:T(8,128)S(1)} %copy-done.3), custom_call_target="tpu_custom_call" | custom-call | flops 100000000 | bytes 1000 | tf_op jit(solution)/shard_map/inner_causal/pallas_call | solution.py:269
  10.4 0.0 collective-permute-done.refs_1_
  10.4 0.7 %collective-permute-done.1.refs_2_ = bf16[48,2048]{1,0:T(8,128)(2,1)S(1)} collective-permute-done((bf16[48,2048]{1,0:T(8,128)(2,1)S(1)}, bf16[48,2048]{1,0:T(8,128)(2,1)S(1)}, u32[]{:S(2)}, u32[]{:S(2)}) %collective-permute-start.1) | collective-permute-done | bytes 196640 | tf_op jit(solution)/shard_map/ppermute | solution.py:54
  11.1 3.7 %collective-permute-done.2.refs_3_ = bf16[48,2048]{1,0:T(8,128)(2,1)S(1)} collective-permute-done((bf16[48,2048]{1,0:T(8,128)(2,1)S(1)}, bf16[48,2048]{1,0:T(8,128)(2,1)S(1)}, u32[]{:S(2)}, u32[]{:S(2)}) %collective-permute-start.2) | collective-permute-done | bytes 196640 | tf_op jit(solution)/shard_map/ppermute | solution.py:54
  14.8 0.3 gather.1
  15.1 1.3 %collective-permute-start.8 = (bf16[128,2048]{1,0:T(8,128)(2,1)S(1)}, bf16[128,2048]{1,0:T(8,128)(2,1)S(1)}, u32[]{:S(2)}, u32[]{:S(2)}) collective-permute-start(bf16[128,2048]{1,0:T(8,128)(2,1)S(1)} %get-tuple-element.40), channel_id=1, source_target_pairs={{8,0},{16,8},{24,16},{9,1},{17,9},{25,17},{10,2},{18,10},{26,18},{... | collective-permute-start | bytes 1572872 | tf_op jit(solution)/shard_map/ppermute | solution.py:34
  16.4 1.4 %inner_scores.1.refs_4_ = f32[128,128]{1,0:T(8,128)S(1)} custom-call(bf16[192,2048]{1,0:T(8,128)(2,1)S(1)} %bitcast.20, bf16[192,2048]{1,0:T(8,128)(2,1)S(1)} %get-tuple-element.34.refs_0_, bf16[192,2048]{1,0:T(8,128)(2,1)S(1)} %bitcast.9, bf16[192,2048]{1,0:T(8,128)(2,1)S(1)} %bitcast.15), custom_call_target="tpu_custom_call" | custom-call | flops 100000000 | bytes 1000 | tf_op jit(solution)/shard_map/inner_scores/pallas_call | solution.py:269
  17.8 3.1 %collective-permute-done.3.refs_3_.early_ref = bf16[128,2048]{1,0:T(8,128)(2,1)S(1)} collective-permute-done((bf16[128,2048]{1,0:T(8,128)(2,1)S(1)}, bf16[128,2048]{1,0:T(8,128)(2,1)S(1)}, u32[]{:S(2)}, u32[]{:S(2)}) %collective-permute-start.3) | collective-permute-done | bytes 524320 | tf_op jit(solution)/shard_map/ppermute | solution.py:34
  20.9 1.4 %edge_scores.1.refs_0_ = bf16[128,128]{1,0:T(8,128)(2,1)S(1)} custom-call(bf16[192,2048]{1,0:T(8,128)(2,1)S(1)} %bitcast.21, bf16[192,2048]{1,0:T(8,128)(2,1)S(1)} %get-tuple-element.34.refs_0_, bf16[192,2048]{1,0:T(8,128)(2,1)S(1)} %bitcast.10, bf16[192,2048]{1,0:T(8,128)(2,1)S(1)} %bitcast.16, ...), custom_call_target="tpu_custom_call" | custom-call | flops 100000000 | bytes 1000 | tf_op jit(solution)/shard_map/edge_scores/pallas_call | solution.py:269
  22.4 1.6 %collective-permute-start.4 = (bf16[128,128]{1,0:T(8,128)(2,1)S(1)}, bf16[128,128]{1,0:T(8,128)(2,1)S(1)}, u32[]{:S(2)}, u32[]{:S(2)}) collective-permute-start(bf16[128,128]{1,0:T(8,128)(2,1)S(1)} %edge_scores.1.refs_0_), channel_id=1, source_target_pairs={{0,1},{1,0},{8,9},{9,8},{16,17},{17,16},{24,25},{25,24},{2,3},{3,2... | collective-permute-start | bytes 98312 | tf_op jit(solution)/shard_map/ppermute | solution.py:80
  24.0 2.3 %causal.1 = bf16[192,2048]{1,0:T(8,128)(2,1)} custom-call(bf16[192,2048]{1,0:T(8,128)(2,1)S(1)} %bitcast.11, bf16[192,2048]{1,0:T(8,128)(2,1)S(1)} %bitcast.17, bf16[128,2048]{1,0:T(8,128)(2,1)S(1)} %collective-permute-done.3.refs_3_.early_ref, f32[128,128]{1,0:T(8,128)S(1)} %copy-done.3, f32[64,2048]{1,0:T(8,128)S(1)} %inner_causal.1.inner_ref, ...), custom_call_target="tpu_custom_call" | custom-call | flops 100000000 | bytes 1000 | tf_op jit(solution)/shard_map/causal/pallas_call | solution.py:269
  26.3 0.1 collective-permute-done.4.refs_1_
  26.4 4.6 %collective-permute-start.7 = (bf16[128,128]{1,0:T(8,128)(2,1)S(1)}, bf16[128,128]{1,0:T(8,128)(2,1)S(1)}, u32[]{:S(2)}, u32[]{:S(2)}) collective-permute-start(bf16[128,128]{1,0:T(8,128)(2,1)S(1)} %add.16), channel_id=1, source_target_pairs={{0,24},{1,25},{8,16},{9,17},{16,8},{17,9},{24,0},{25,1},{2,26},{3,... | collective-permute-start | bytes 98312 | tf_op jit(solution)/shard_map/ppermute | solution.py:80
  30.9 0.0 collective-permute-start.6
  30.9 0.6 %collective-permute-start.5 = (bf16[128,128]{1,0:T(8,128)(2,1)S(1)}, bf16[128,128]{1,0:T(8,128)(2,1)S(1)}, u32[]{:S(2)}, u32[]{:S(2)}) collective-permute-start(bf16[128,128]{1,0:T(8,128)(2,1)S(1)} %add.16), channel_id=1, source_target_pairs={{0,8},{1,9},{8,0},{9,1},{16,24},{17,25},{24,16},{25,17},{2,10},{3,... | collective-permute-start | bytes 98312 | tf_op jit(solution)/shard_map/ppermute | solution.py:80
  31.6 0.0 collective-permute-done.8.refs_1_
  31.6 2.8 %adjoint.1 = (bf16[192,2048]{1,0:T(8,128)(2,1)}, bf16[192,2048]{1,0:T(8,128)(2,1)}) custom-call(bf16[192,2048]{1,0:T(8,128)(2,1)S(1)} %bitcast.22, bf16[192,2048]{1,0:T(8,128)(2,1)S(1)} %bitcast.12, bf16[192,2048]{1,0:T(8,128)(2,1)S(1)} %bitcast.18, f32[128,128]{1,0:T(8,128)S(1)} %copy-done.3, bf16[192,2048]{1,0:T(8,128)(2,1)S(1)} %get-tuple-element.34.refs_0_, ...), custom_call_target="tpu_custom_call" | custom-call | flops 100000000 | bytes 1000 | tf_op jit(solution)/shard_map/adjoint/pallas_call | solution.py:269
  34.4 0.2 collective-permute-done.7
  34.6 1.1 %collective-permute-done.6 = bf16[128,128]{1,0:T(8,128)(2,1)S(1)} collective-permute-done((bf16[128,128]{1,0:T(8,128)(2,1)S(1)}, bf16[128,128]{1,0:T(8,128)(2,1)S(1)}, u32[]{:S(2)}, u32[]{:S(2)}) %collective-permute-start.6) | collective-permute-done | bytes 32800 | tf_op jit(solution)/shard_map/ppermute | solution.py:80
  35.7 0.0 collective-permute-done.5
  35.8 0.1 rev.4
  35.9 0.6 %broadcast_multiply_fusion = f32[128,128]{1,0:T(8,128)} fusion(f32[128,128]{1,0:T(8,128)S(1)} %rev.4), kind=kLoop, calls=%fused_computation.1 | loop fusion | flops 16384 | bytes 131072 | tf_op jit(solution)/shard_map/mul | solution.py:345
  (5 shorter events, 0.0 us)
Async XLA Ops:
  0.6 8.7 %copy-start = (bf16[1,192,2048]{2,1,0:T(8,128)(2,1)S(1)}, bf16[1,192,2048]{2,1,0:T(8,128)(2,1)}, u32[]{:S(2)}) copy-start(bf16[1,192,2048]{2,1,0:T(8,128)(2,1)} %param.6) | copy-start | bytes 2359300
  0.6 8.7 %copy-start.1 = (bf16[1,192,2048]{2,1,0:T(8,128)(2,1)S(1)}, bf16[1,192,2048]{2,1,0:T(8,128)(2,1)}, u32[]{:S(2)}) copy-start(bf16[1,192,2048]{2,1,0:T(8,128)(2,1)} %param.7) | copy-start | bytes 2359300
  0.7 8.7 %copy-start.3 = (f32[128,128]{1,0:T(8,128)S(1)}, f32[128,128]{1,0:T(8,128)}, u32[]{:S(2)}) copy-start(f32[128,128]{1,0:T(8,128)} %filter_ref.5) | copy-start | bytes 196612
  2.3 8.1 %collective-permute-start = (bf16[48,2048]{1,0:T(8,128)(2,1)S(1)}, bf16[48,2048]{1,0:T(8,128)(2,1)S(1)}, u32[]{:S(2)}, u32[]{:S(2)}) collective-permute-start(bf16[48,2048]{1,0:T(8,128)(2,1)S(1)} %get-tuple-element.27), channel_id=1, source_target_pairs={{0,2},{2,0},{4,6},{6,4},{1,3},{3,1},{5,7},{7,5},{8,10},{10,8},{12,... | collective-permute-start | bytes 589832 | tf_op jit(solution)/shard_map/ppermute | solution.py:54
  2.8 8.3 %collective-permute-start.1 = (bf16[48,2048]{1,0:T(8,128)(2,1)S(1)}, bf16[48,2048]{1,0:T(8,128)(2,1)S(1)}, u32[]{:S(2)}, u32[]{:S(2)}) collective-permute-start(bf16[48,2048]{1,0:T(8,128)(2,1)S(1)} %get-tuple-element.28), channel_id=1, source_target_pairs={{0,4},{2,6},{4,0},{6,2},{1,5},{3,7},{5,1},{7,3},{8,12},{10,14},{12... | collective-permute-start | bytes 589832 | tf_op jit(solution)/shard_map/ppermute | solution.py:54
  5.3 9.4 %collective-permute-start.2 = (bf16[48,2048]{1,0:T(8,128)(2,1)S(1)}, bf16[48,2048]{1,0:T(8,128)(2,1)S(1)}, u32[]{:S(2)}, u32[]{:S(2)}) collective-permute-start(bf16[48,2048]{1,0:T(8,128)(2,1)S(1)} %get-tuple-element.29), channel_id=1, source_target_pairs={{0,6},{2,4},{4,2},{6,0},{1,7},{3,5},{5,3},{7,1},{8,14},{10,12},{12... | collective-permute-start | bytes 589832 | tf_op jit(solution)/shard_map/ppermute | solution.py:54
  5.4 9.4 %copy-start.2 = (bf16[1,192,2048]{2,1,0:T(8,128)(2,1)S(1)}, bf16[1,192,2048]{2,1,0:T(8,128)(2,1)}, u32[]{:S(2)}) copy-start(bf16[1,192,2048]{2,1,0:T(8,128)(2,1)} %param.5) | copy-start | bytes 2359300
  5.4 15.5 %collective-permute-start.3 = (bf16[128,2048]{1,0:T(8,128)(2,1)S(1)}, bf16[128,2048]{1,0:T(8,128)(2,1)S(1)}, u32[]{:S(2)}, u32[]{:S(2)}) collective-permute-start(bf16[128,2048]{1,0:T(8,128)(2,1)S(1)} %get-tuple-element.35), channel_id=1, source_target_pairs={{0,8},{8,16},{16,24},{1,9},{9,17},{17,25},{2,10},{10,18},{18,26},{... | collective-permute-start | bytes 1572872 | tf_op jit(solution)/shard_map/ppermute | solution.py:34
  15.1 16.5 %collective-permute-start.8 = (bf16[128,2048]{1,0:T(8,128)(2,1)S(1)}, bf16[128,2048]{1,0:T(8,128)(2,1)S(1)}, u32[]{:S(2)}, u32[]{:S(2)}) collective-permute-start(bf16[128,2048]{1,0:T(8,128)(2,1)S(1)} %get-tuple-element.40), channel_id=1, source_target_pairs={{8,0},{16,8},{24,16},{9,1},{17,9},{25,17},{10,2},{18,10},{26,18},{... | collective-permute-start | bytes 1572872 | tf_op jit(solution)/shard_map/ppermute | solution.py:34
  22.4 4.0 %collective-permute-start.4 = (bf16[128,128]{1,0:T(8,128)(2,1)S(1)}, bf16[128,128]{1,0:T(8,128)(2,1)S(1)}, u32[]{:S(2)}, u32[]{:S(2)}) collective-permute-start(bf16[128,128]{1,0:T(8,128)(2,1)S(1)} %edge_scores.1.refs_0_), channel_id=1, source_target_pairs={{0,1},{1,0},{8,9},{9,8},{16,17},{17,16},{24,25},{25,24},{2,3},{3,2... | collective-permute-start | bytes 98312 | tf_op jit(solution)/shard_map/ppermute | solution.py:80
  26.4 8.3 %collective-permute-start.7 = (bf16[128,128]{1,0:T(8,128)(2,1)S(1)}, bf16[128,128]{1,0:T(8,128)(2,1)S(1)}, u32[]{:S(2)}, u32[]{:S(2)}) collective-permute-start(bf16[128,128]{1,0:T(8,128)(2,1)S(1)} %add.16), channel_id=1, source_target_pairs={{0,24},{1,25},{8,16},{9,17},{16,8},{17,9},{24,0},{25,1},{2,26},{3,... | collective-permute-start | bytes 98312 | tf_op jit(solution)/shard_map/ppermute | solution.py:80
  30.9 4.8 %collective-permute-start.6 = (bf16[128,128]{1,0:T(8,128)(2,1)S(1)}, bf16[128,128]{1,0:T(8,128)(2,1)S(1)}, u32[]{:S(2)}, u32[]{:S(2)}) collective-permute-start(bf16[128,128]{1,0:T(8,128)(2,1)S(1)} %add.16), channel_id=1, source_target_pairs={{0,16},{1,17},{8,24},{9,25},{16,0},{17,1},{24,8},{25,9},{2,18},{3,... | collective-permute-start | bytes 98312 | tf_op jit(solution)/shard_map/ppermute | solution.py:80
  30.9 4.8 %collective-permute-start.5 = (bf16[128,128]{1,0:T(8,128)(2,1)S(1)}, bf16[128,128]{1,0:T(8,128)(2,1)S(1)}, u32[]{:S(2)}, u32[]{:S(2)}) collective-permute-start(bf16[128,128]{1,0:T(8,128)(2,1)S(1)} %add.16), channel_id=1, source_target_pairs={{0,8},{1,9},{8,0},{9,1},{16,24},{17,25},{24,16},{25,17},{2,10},{3,... | collective-permute-start | bytes 98312 | tf_op jit(solution)/shard_map/ppermute | solution.py:80

commit v4 on v3

--- a/solution.py
+++ b/solution.py
@@ -34,6 +34,11 @@
     return lax.ppermute(value, axis, [(source, source + steps) for source in range(first, last)])
 
 
+def passed_round(value, axis, steps):
+    count = lax.axis_size(axis)
+    return lax.ppermute(value, axis, [(index, (index + steps) % count) for index in range(count)])
+
+
 def partner(index, step, count):
     if count & (count - 1) == 0:
         return index ^ step
@@ -46,13 +51,10 @@
     return (index + step) % count
 
 
-def exchanged(parts, axis):
+def exchanged(part, axis, step):
     count = lax.axis_size(axis)
-    brought = []
-    for step, part in enumerate(parts, 1):
-        pairs = [(index, target(index, step, count)) for index in range(count)]
-        brought.append(lax.ppermute(part, axis, pairs))
-    return brought
+    pairs = [(index, target(index, step, count)) for index in range(count)]
+    return lax.ppermute(part, axis, pairs)
 
 
 def add_kernel(*refs):
@@ -131,8 +133,8 @@
     return []
 
 
-def pack_kernel(count, grad_ref, k_ref, v_ref, *refs):
-    parts, (tail_ref, k_stage, v_stage, part_sem, tail_sem) = refs[:count], refs[count:]
+def pack_kernel(count, last, grad_ref, k_ref, v_ref, *refs):
+    parts, (tail_ref, k_stage, v_stage, part_sem, tail_sem) = refs[:-5], refs[-5:]
     here = lax.axis_index("tp")
     height = k_stage.shape[0]
     width = parts[0].shape[1]
@@ -143,30 +145,41 @@
     ]
     cuts = []
     for n, part in enumerate(parts):
-        place = target(here, n, count) * width
-        columns = pl.ds(pl.multiple_of(place, width), width)
+        half, step = (0, n) if n < NEAR else divmod(n - NEAR, count - NEAR)
+        step += 0 if n < NEAR else NEAR
+        columns = part.shape[1]
+        place = pl.multiple_of(target(here, step, count) * width + half * columns, columns)
+        columns = pl.ds(place, columns)
         cuts.append(pltpu.make_async_copy(grad_ref.at[:, columns], part, part_sem.at[n]))
     for copy in tails + cuts:
         copy.start()
     for copy in tails:
         copy.wait()
-    tail_ref[...] = product(k_stage[...], v_stage[...])
+    place = lax.axis_index("ctx")
+
+    @pl.when(place == last)
+    def _():
+        tail_ref[...] = jnp.zeros(tail_ref.shape, tail_ref.dtype)
+
+    @pl.when(place != last)
+    def _():
+        tail_ref[...] = product(k_stage[...], v_stage[...])
+
     for copy in cuts:
         copy.wait()
 
 
-def gather_kernel(count, q_ref, *refs):
-    parts, og_refs, head_ref = refs[:count], refs[count:-1], refs[-1]
-    height, width = parts[0].shape
-    piece = width // HALVES
+def gather_kernel(count, half, q_ref, *refs):
+    parts, (og_ref, head_ref) = refs[:-2], refs[-2:]
+    height, width = parts[-1].shape
     here = lax.axis_index("tp")
     head = head_ref.shape[0]
-    for half, og_ref in enumerate(og_refs):
-        c = slice(half * piece, (half + 1) * piece)
-        for step, part in enumerate(parts):
-            place = partner(here, step, count)
-            og_ref[pl.ds(pl.multiple_of(place * height, height), height), :] = part[:, c]
-        head_ref[:, c] = product(og_ref[:head, :], q_ref[:head, c])
+    c = slice(half * width, (half + 1) * width)
+    for step, part in enumerate(parts):
+        place = partner(here, step, count)
+        rows = pl.ds(pl.multiple_of(place * height, height), height)
+        og_ref[rows, :] = part[:, c] if step < NEAR else part[...]
+    head_ref[...] = product(og_ref[:head, :], q_ref[:head, c])
 
 
 def columns_of(refs, c):
@@ -175,41 +188,54 @@
     return refs[half][:, c.start - half * width : c.stop - half * width]
 
 
-def scores_kernel(taps, group_width, inner, q_ref, *refs):
-    og_refs, (k_ref, v_ref, *more_refs, out_ref) = refs[:HALVES], refs[HALVES:]
-    first, last = (taps, k_ref.shape[0]) if inner else (0, taps)
-    blocks = (last - first) // BLOCK
+def lag_sums(taps, group_width, grad_mix, window):
+    blocks = grad_mix.shape[0] // BLOCK
     count = LANES // group_width
     upward = 7 - lax.broadcasted_iota(jnp.int32, (8, LANES), 0)
     lane = lax.broadcasted_iota(jnp.int32, (BLOCK, blocks * LANES), 1)
     lane_group = (lane % LANES) // group_width
+    turned = []
+    for b in range(blocks):
+        for end in range((b + 1) * BLOCK, b * BLOCK, -8):
+            eight = grad_mix[end - 8 : end]
+            turned.append(jnp.take_along_axis(eight, upward, axis=0, mode="promise_in_bounds"))
+    own = windows(jnp.concatenate(turned, axis=0).astype(jnp.bfloat16), blocks, BLOCK)
+    split = [jnp.where(lane_group == g, own, jnp.zeros_like(own)) for g in range(count)]
+    scores = lax.dot_general(
+        jnp.concatenate(split, axis=0),
+        windows(window, blocks, taps + BLOCK),
+        (((1,), (1,)), ((), ())),
+        preferred_element_type=jnp.float32,
+    )
+    spare = jnp.zeros((scores.shape[0], 2 * taps - scores.shape[1]), jnp.float32)
+    scores = jnp.concatenate([scores, spare], axis=1)
+    sums = []
+    for g in range(count):
+        lags = scores[g * BLOCK : (g + 1) * BLOCK]
+        lags = pltpu.roll(lags, taps - BLOCK, 1, stride=1, stride_axis=0)[:, taps:]
+        sums.append(jnp.sum(lags, axis=0, keepdims=True))
+    return jnp.concatenate(sums, axis=0)
+
+
+def inner_scores_kernel(taps, group_width, half, q_ref, og_ref, k_ref, v_ref, out_ref):
+    begin = half * og_ref.shape[1]
+    for own, rows in tiles(og_ref.shape[1], group_width):
+        c = slice(begin + own.start, begin + own.stop)
+        grad_mix = widen(og_ref[taps:, own]) * widen(q_ref[taps:, c])
+        out_ref[rows, :] = lag_sums(taps, group_width, grad_mix, product(k_ref[:, c], v_ref[:, c]))
+
+
+def scores_kernel(taps, group_width, q_ref, *refs):
+    og_refs, (k_ref, v_ref, early_ref) = refs[:HALVES], refs[HALVES : HALVES + 3]
+    inner_refs, out_ref = refs[HALVES + 3 : -1], refs[-1]
+    height = inner_refs[0].shape[0]
     for c, rows in tiles(k_ref.shape[1], group_width):
-        grad_mix = widen(columns_of(og_refs, c)[first:last]) * widen(q_ref[first:last, c])
-        turned = []
-        for b in range(blocks):
-            for end in range((b + 1) * BLOCK, b * BLOCK, -8):
-                eight = grad_mix[end - 8 : end]
-                turned.append(jnp.take_along_axis(eight, upward, axis=0, mode="promise_in_bounds"))
-        own = windows(jnp.concatenate(turned, axis=0).astype(jnp.bfloat16), blocks, BLOCK)
-        window = product(k_ref[:last, c], v_ref[:last, c])
-        if not inner:
-            window = jnp.concatenate([more_refs[0][:, c], window], axis=0)
-        split = [jnp.where(lane_group == g, own, jnp.zeros_like(own)) for g in range(count)]
-        scores = lax.dot_general(
-            jnp.concatenate(split, axis=0),
-            windows(window, blocks, taps + BLOCK),
-            (((1,), (1,)), ((), ())),
-            preferred_element_type=jnp.float32,
-        )
-        spare = jnp.zeros((scores.shape[0], 2 * taps - scores.shape[1]), jnp.float32)
-        scores = jnp.concatenate([scores, spare], axis=1)
-        sums = []
-        for g in range(count):
-            lags = scores[g * BLOCK : (g + 1) * BLOCK]
-            lags = pltpu.roll(lags, taps - BLOCK, 1, stride=1, stride_axis=0)[:, taps:]
-            sums.append(jnp.sum(lags, axis=0, keepdims=True))
-        sums = jnp.concatenate(sums, axis=0)
-        out_ref[rows, :] = sums if inner else (sums + more_refs[1][rows, :]).astype(out_ref.dtype)
+        grad_mix = widen(columns_of(og_refs, c)[:taps]) * widen(q_ref[:taps, c])
+        window = product(k_ref[:taps, c], v_ref[:taps, c])
+        window = jnp.concatenate([early_ref[:, c], window], axis=0)
+        half, first = divmod(rows.start, height)
+        inner = inner_refs[half][first : first + rows.stop - rows.start, :]
+        out_ref[rows, :] = lag_sums(taps, group_width, grad_mix, window) + inner
 
 
 def turned_base(filter_ref):
@@ -246,15 +272,15 @@
 
 
 def back_kernel(taps, group_width, q_ref, k_ref, v_ref, filter_ref, *refs):
-    og_refs, refs = refs[:HALVES], refs[HALVES:]
-    late_ref, kg_ref, vg_ref, k_stage, v_stage, k_sem, v_sem = refs
+    og_refs, late_refs, refs = refs[:HALVES], refs[HALVES : 2 * HALVES], refs[2 * HALVES :]
+    kg_ref, vg_ref, k_stage, v_stage, k_sem, v_sem = refs
     blocks = k_ref.shape[0] // BLOCK
     coeffs = widen(filter_ref[...].astype(jnp.bfloat16))
     base = jnp.concatenate([coeffs, jnp.zeros_like(coeffs)], axis=1)
     copies = []
     for c, rows in tiles(k_ref.shape[1], group_width):
         grad_mix = product(columns_of(og_refs, c), q_ref[:, c])
-        window = jnp.concatenate([grad_mix, late_ref[:, c]], axis=0)
+        window = jnp.concatenate([grad_mix, columns_of(late_refs, c)], axis=0)
         back = convolved(base[rows], window, blocks, taps, group_width)
         k_stage[:, c] = (back * widen(v_ref[:, c])).astype(jnp.bfloat16)
         v_stage[:, c] = (back * widen(k_ref[:, c])).astype(jnp.bfloat16)
@@ -286,48 +312,66 @@
     wide = jax.ShapeDtypeStruct((rows, channels), jnp.bfloat16)
     edge = jax.ShapeDtypeStruct((taps, channels), jnp.bfloat16)
     small = jax.ShapeDtypeStruct((groups, taps), jnp.float32)
+    half_small = jax.ShapeDtypeStruct((groups // HALVES, taps), jnp.float32)
     thin = jax.ShapeDtypeStruct((groups, taps), TRAVEL)
-    half = jax.ShapeDtypeStruct((rows, channels // HALVES), jnp.bfloat16)
+    width = channels // HALVES
     count = lax.axis_size("tp")
     height = rows // count
-    piece = jax.ShapeDtypeStruct((height, channels), jnp.bfloat16)
+    far = count - NEAR
+    pieces = [jax.ShapeDtypeStruct((height, channels), jnp.bfloat16)] * NEAR
+    pieces += [jax.ShapeDtypeStruct((height, width), jnp.bfloat16)] * (HALVES * far)
+    half_wide = jax.ShapeDtypeStruct((rows, width), jnp.bfloat16)
+    half_edge = jax.ShapeDtypeStruct((taps, width), jnp.bfloat16)
     *parts, tail = pl.pallas_call(
-        functools.partial(pack_kernel, count),
+        functools.partial(pack_kernel, count, lax.axis_size("ctx") - 1),
         in_specs=[ANYWHERE] * 3,
-        out_specs=[ANYWHERE] * count + [VMEM],
-        out_shape=[piece] * count + [edge],
+        out_specs=[ANYWHERE] * len(pieces) + [VMEM],
+        out_shape=pieces + [edge],
         scratch_shapes=[pltpu.VMEM(edge.shape, edge.dtype)] * 2
-        + [pltpu.SemaphoreType.DMA((count,)), pltpu.SemaphoreType.DMA((2,))],
+        + [pltpu.SemaphoreType.DMA((len(pieces),)), pltpu.SemaphoreType.DMA((2,))],
         name="pack",
         compiler_params=pltpu.CompilerParams(vmem_limit_bytes=LIMIT * 1024 * 1024),
     )(*[in_hbm(a) for a in (out_grad[0], k, v)])
-    early = passed_along(tail, "ctx", 1)
+    early = passed_round(tail, "ctx", 1)
+    near = parts[:1] + [exchanged(part, "tp", step) for step, part in enumerate(parts[1:NEAR], 1)]
     inner_rows = jax.ShapeDtypeStruct((rows - taps, channels), jnp.float32)
     (inner,) = call(
         functools.partial(inner_mixed_kernel, taps, group_width), "inner_causal", (k, v, filters), [inner_rows], False, COST
     )
-    parts = parts[:1] + exchanged(parts[1:], "tp")
-    parts, inner = lax.optimization_barrier((parts, inner))
-    if height % 16 == 0:
-        *grads, head = call(
-            functools.partial(gather_kernel, count), "gather", (q, *parts), [half] * HALVES + [edge], False, 1000
+    grads, heads, inners = [], [], []
+    for half in range(HALVES):
+        mine = parts[NEAR + half * far : NEAR + (half + 1) * far]
+        if half:
+            mine, near[-1] = lax.optimization_barrier((mine, near[-1]))
+        brought_in = [exchanged(part, "tp", step) for step, part in enumerate(mine, NEAR)]
+        if half:
+            brought_in, inners[0] = lax.optimization_barrier((brought_in, inners[0]))
+        else:
+            brought_in, inner = lax.optimization_barrier((brought_in, inner))
+        if height % 16 == 0:
+            grad, head = call(
+                functools.partial(gather_kernel, count, half), "gather", (q, *near, *brought_in),
+                [half_wide, half_edge], False, 1000,
+            )
+        else:
+            here = lax.axis_index("tp")
+            c = slice(half * width, (half + 1) * width)
+            grad = jnp.zeros(half_wide.shape, half_wide.dtype)
+            for step, part in enumerate([part[:, c] for part in near] + brought_in):
+                place = partner(here, step, count)
+                grad = lax.dynamic_update_slice_in_dim(grad, part, place * height, 0)
+            head = product(grad[:taps], q[:taps, c])
+        grads.append(grad)
+        heads.append(head)
+        (lags,) = call(
+            functools.partial(inner_scores_kernel, taps, group_width, half), "inner_scores", (q, grad, k, v), [half_small], False, COST
         )
-    else:
-        here = lax.axis_index("tp")
-        grad = jnp.zeros(wide.shape, wide.dtype)
-        for step, part in enumerate(parts):
-            place = partner(here, step, count)
-            grad = lax.dynamic_update_slice_in_dim(grad, part, place * height, 0)
-        head = product(grad[:taps], q[:taps])
-        grads = jnp.split(grad, HALVES, axis=1)
-    late = passed_along(head, "ctx", -1)
+        inners.append(lags)
     work = functools.partial
     (lags,) = call(
-        work(scores_kernel, taps, group_width, True), "inner_scores", (q, *grads, k, v), [small], False, COST
-    )
-    (lags,) = call(
-        work(scores_kernel, taps, group_width, False), "edge_scores", (q, *grads, k, v, early, lags), [thin], False, COST
-    )
+        work(scores_kernel, taps, group_width), "edge_scores", (q, *grads, k, v, early, *inners), [small], False, COST
+    )
+    lates = [passed_along(head, "ctx", -1) for head in heads]
     (query_grad,) = call(
         work(mixed_kernel, taps, group_width), "causal", (k, v, early, filters, inner, *grads), [wide], True, COST
     )
@@ -335,7 +379,7 @@
     lags, query_grad = lax.optimization_barrier((lags, query_grad))
     lags = added(lags, TRAVEL)
     key_grad, value_grad = call(
-        work(back_kernel, taps, group_width), "adjoint", (q, k, v, filters, *grads, late), [wide, wide], True, COST
+        work(back_kernel, taps, group_width), "adjoint", (q, k, v, filters, *grads, *lates), [wide, wide], True, COST
     )
     lags = [lags] + [brought(lags, step) for step in SECOND]
     lags, key_grad = lax.optimization_barrier((lags, key_grad))
@@ -346,7 +390,8 @@
 
 
 COST = 100_000_000
-HALVES = 1
+HALVES = 2
+NEAR = 2
 TRAVEL = jnp.bfloat16
 FIRST = (1,)
 SECOND = (2, 4, 6)

time: 36.7 us -> 35.1 us (0.956)
  waiting for transfers between devices: 8.92 us -> 6.54 us
  starting transfers between devices: 15.1 us -> 15.5 us
    ppermute x3 -> x6, starting transfers between devices: 3.15 us -> 6.57 us  [the longest x5 3.49 us: exchanged(): return lax.ppermute(part, axis, pairs)]
    ppermute x2, starting transfers between devices: 5.16 us -> 2.58 us  [passed_along(): lax.ppermute(value, axis, [(source, source + steps) for source in range(f...]
    ppermute x2, waiting for transfers between devices: 3.14 us -> 0.59 us  [passed_along(): lax.ppermute(value, axis, [(source, source + steps) for source in range(f...]
    ppermute x4, starting transfers between devices: 6.8 us -> 6.37 us  [brought(): lax.ppermute(value, axes, [(index, index ^ step) for index in range(count)])]
    ppermute x3 -> x6, waiting for transfers between devices: 4.38 us -> 4.8 us  [the longest x5 4.25 us: exchanged(): return lax.ppermute(part, axis, pairs)]
    pallas_call x6 -> x8, Pallas kernels: 9.35 us -> 9.6 us  [call(): pl.pallas_call(kernel, in_specs=[SCALAR if a.dtype == jnp.int32 else VMEM...]
  transfers between devices with their start and end apart: 9 -> 12, of which waited for: 6 -> 8; matrix products, arithmetic and copies ran while one was open for 0% -> 0% of each run, Pallas kernels for 26% -> 28%
where the time goes in v4:
time: 35.1 us; the launch traced here: 34.9 us
  starting transfers between devices  15.5 us (44%)
  Pallas kernels  11.3 us (32%)
  waiting for transfers between devices  6.54 us (19%)
  between operations  0.75 us (2%)
  other arithmetic  0.67 us (2%)
    pallas_call x8, Pallas kernels, call(): pl.pallas_call(kernel, in_specs=[SCALAR if a.dtype == jnp.int32 else VMEM...  9.6 us
    ppermute x4, starting transfers between devices, brought(): lax.ppermute(value, axes, [(index, index ^ step) for index in range(count)])  6.37 us
    ppermute x5, waiting for transfers between devices, exchanged(): return lax.ppermute(part, axis, pairs)  4.25 us
    ppermute x5, starting transfers between devices, exchanged(): return lax.ppermute(part, axis, pairs)  3.49 us
    ppermute x1, starting transfers between devices, passed_round(): lax.ppermute(value, axis, [(index, (index + steps) % count) for index in...  3.08 us
    ppermute x2, starting transfers between devices, passed_along(): lax.ppermute(value, axis, [(source, source + steps) for source in range(f...  2.58 us
    pallas_call x1, Pallas kernels, local(): pl.pallas_call(functools.partial(pack_kernel, count, lax.axis_size('ctx')...  1.74 us
    ppermute x4, waiting for transfers between devices, brought(): lax.ppermute(value, axes, [(index, index ^ step) for index in range(count)])  1.15 us
  transfers between devices with their start and end apart: 12, of which 8 were waited for; matrix products, arithmetic and copies ran while one was open for 0% of the time, Pallas kernels for 28%

profile of v4, /device:TPU:0, one launch (start us, length us, event | category | flops | bytes accessed | tf_op | source)
XLA Modules:
  0.0 34.9 jit_solution(3934834885753580373)
XLA Ops:
  0.7 1.7 %pack.1 = (bf16[48,2048]{1,0:T(8,128)(2,1)S(1)}, bf16[48,2048]{1,0:T(8,128)(2,1)S(1)}, bf16[48,1024]{1,0:T(8,128)(2,1)S(1)}, bf16[48,1024]{1,0:T(8,128)(2,1)S(1)...) custom-call(bf16[48,8192]{1,0:T(8,128)(2,1)} %bitcast.28, ...), custom_call_target="tpu_custom_call" | custom-call | tf_op jit(solution)/shard_map/pack/pallas_call | solution.py:325
  2.4 3.1 %collective-permute-start.5 = (bf16[128,2048]{1,0:T(8,128)(2,1)S(1)}, bf16[128,2048]{1,0:T(8,128)(2,1)S(1)}, u32[]{:S(2)}, u32[]{:S(2)}) collective-permute-start(bf16[128,2048]{1,0:T(8,128)(2,1)S(1)} %get-tuple-element.49), channel_id=1, source_target_pairs={{0,8},{8,16},{16,24},{24,0},{1,9},{9,17},{17,25},{25,1},{2,10},{10... | collective-permute-start | bytes 1572872 | tf_op jit(solution)/shard_map/ppermute | solution.py:39
  5.5 1.5 %collective-permute-start.1 = (bf16[48,1024]{1,0:T(8,128)(2,1)S(1)}, bf16[48,1024]{1,0:T(8,128)(2,1)S(1)}, u32[]{:S(2)}, u32[]{:S(2)}) collective-permute-start(bf16[48,1024]{1,0:T(8,128)(2,1)S(1)} %get-tuple-element.36), channel_id=1, source_target_pairs={{0,4},{2,6},{4,0},{6,2},{1,5},{3,7},{5,1},{7,3},{8,12},{10,14},{12... | collective-permute-start | bytes 294920 | tf_op jit(solution)/shard_map/ppermute | solution.py:57
  7.0 0.4 %collective-permute-start.2 = (bf16[48,1024]{1,0:T(8,128)(2,1)S(1)}, bf16[48,1024]{1,0:T(8,128)(2,1)S(1)}, u32[]{:S(2)}, u32[]{:S(2)}) collective-permute-start(bf16[48,1024]{1,0:T(8,128)(2,1)S(1)} %get-tuple-element.37), channel_id=1, source_target_pairs={{0,6},{2,4},{4,2},{6,0},{1,7},{3,5},{5,3},{7,1},{8,14},{10,12},{12... | collective-permute-start | bytes 294920 | tf_op jit(solution)/shard_map/ppermute | solution.py:57
  7.3 0.0 collective-permute-done.refs_1_
  7.3 1.5 %collective-permute-start.3 = (bf16[48,1024]{1,0:T(8,128)(2,1)S(1)}, bf16[48,1024]{1,0:T(8,128)(2,1)S(1)}, u32[]{:S(2)}, u32[]{:S(2)}) collective-permute-start(bf16[48,1024]{1,0:T(8,128)(2,1)S(1)} %get-tuple-element.44), channel_id=1, source_target_pairs={{0,4},{2,6},{4,0},{6,2},{1,5},{3,7},{5,1},{7,3},{8,12},{10,14},{12... | collective-permute-start | bytes 294920 | tf_op jit(solution)/shard_map/ppermute | solution.py:57
  8.8 0.1 collective-permute-start.4
  9.0 1.1 %inner_causal.1.inner_ref = f32[64,2048]{1,0:T(8,128)S(1)} custom-call(bf16[192,2048]{1,0:T(8,128)(2,1)S(1)} %bitcast.8, bf16[192,2048]{1,0:T(8,128)(2,1)S(1)} %bitcast.15, f32[128,128]{1,0:T(8,128)S(1)} %copy-done.3), custom_call_target="tpu_custom_call" | custom-call | flops 100000000 | bytes 1000 | tf_op jit(solution)/shard_map/inner_causal/pallas_call | solution.py:295
  10.1 1.0 %collective-permute-done.1.refs_2_ = bf16[48,1024]{1,0:T(8,128)(2,1)S(1)} collective-permute-done((bf16[48,1024]{1,0:T(8,128)(2,1)S(1)}, bf16[48,1024]{1,0:T(8,128)(2,1)S(1)}, u32[]{:S(2)}, u32[]{:S(2)}) %collective-permute-start.1) | collective-permute-done | bytes 98336 | tf_op jit(solution)/shard_map/ppermute | solution.py:57
  11.1 1.3 %collective-permute-done.2.refs_3_ = bf16[48,1024]{1,0:T(8,128)(2,1)S(1)} collective-permute-done((bf16[48,1024]{1,0:T(8,128)(2,1)S(1)}, bf16[48,1024]{1,0:T(8,128)(2,1)S(1)}, u32[]{:S(2)}, u32[]{:S(2)}) %collective-permute-start.2) | collective-permute-done | bytes 98336 | tf_op jit(solution)/shard_map/ppermute | solution.py:57
  12.4 0.1 gather.2
  12.6 1.3 %collective-permute-start.10 = (bf16[128,1024]{1,0:T(8,128)(2,1)S(1)}, bf16[128,1024]{1,0:T(8,128)(2,1)S(1)}, u32[]{:S(2)}, u32[]{:S(2)}) collective-permute-start(bf16[128,1024]{1,0:T(8,128)(2,1)S(1)} %get-tuple-element.55), channel_id=1, source_target_pairs={{8,0},{16,8},{24,16},{9,1},{17,9},{25,17},{10,2},{18,10},{26,18},{... | collective-permute-start | bytes 786440 | tf_op jit(solution)/shard_map/ppermute | solution.py:34
  13.9 0.8 %inner_scores.2.refs_5_ = f32[64,128]{1,0:T(8,128)S(1)} custom-call(bf16[192,2048]{1,0:T(8,128)(2,1)S(1)} %bitcast.22, bf16[192,1024]{1,0:T(8,128)(2,1)S(1)} %get-tuple-element.40.og_ref.refs_0_, bf16[192,2048]{1,0:T(8,128)(2,1)S(1)} %bitcast.9, bf16[192,2048]{1,0:T(8,128)(2,1)S(1)} %bitcast.16), custom_call_target="tpu_custom_call" | custom-call | flops 100000000 | bytes 1000 | tf_op jit(solution)/shard_map/inner_scores/pallas_call | solution.py:295
  14.7 0.6 %collective-permute-done.3.refs_2_ = bf16[48,1024]{1,0:T(8,128)(2,1)S(1)} collective-permute-done((bf16[48,1024]{1,0:T(8,128)(2,1)S(1)}, bf16[48,1024]{1,0:T(8,128)(2,1)S(1)}, u32[]{:S(2)}, u32[]{:S(2)}) %collective-permute-start.3) | collective-permute-done | bytes 98336 | tf_op jit(solution)/shard_map/ppermute | solution.py:57
  15.3 1.3 %collective-permute-done.4.refs_3_ = bf16[48,1024]{1,0:T(8,128)(2,1)S(1)} collective-permute-done((bf16[48,1024]{1,0:T(8,128)(2,1)S(1)}, bf16[48,1024]{1,0:T(8,128)(2,1)S(1)}, u32[]{:S(2)}, u32[]{:S(2)}) %collective-permute-start.4) | collective-permute-done | bytes 98336 | tf_op jit(solution)/shard_map/ppermute | solution.py:57
  16.6 0.1 gather.3
  16.8 1.3 %collective-permute-start.11 = (bf16[128,1024]{1,0:T(8,128)(2,1)S(1)}, bf16[128,1024]{1,0:T(8,128)(2,1)S(1)}, u32[]{:S(2)}, u32[]{:S(2)}) collective-permute-start(bf16[128,1024]{1,0:T(8,128)(2,1)S(1)} %get-tuple-element.56), channel_id=1, source_target_pairs={{8,0},{16,8},{24,16},{9,1},{17,9},{25,17},{10,2},{18,10},{26,18},{... | collective-permute-start | bytes 786440 | tf_op jit(solution)/shard_map/ppermute | solution.py:34
  18.1 0.8 %inner_scores.3.refs_6_ = f32[64,128]{1,0:T(8,128)S(1)} custom-call(bf16[192,2048]{1,0:T(8,128)(2,1)S(1)} %bitcast.24, bf16[192,1024]{1,0:T(8,128)(2,1)S(1)} %get-tuple-element.48.og_ref.refs_1_, bf16[192,2048]{1,0:T(8,128)(2,1)S(1)} %bitcast.10, bf16[192,2048]{1,0:T(8,128)(2,1)S(1)} %bitcast.17), custom_call_target="tpu_custom_call" | custom-call | flops 100000000 | bytes 1000 | tf_op jit(solution)/shard_map/inner_scores/pallas_call | solution.py:295
  18.9 0.5 %collective-permute-done.5.refs_4_.early_ref = bf16[128,2048]{1,0:T(8,128)(2,1)S(1)} collective-permute-done((bf16[128,2048]{1,0:T(8,128)(2,1)S(1)}, bf16[128,2048]{1,0:T(8,128)(2,1)S(1)}, u32[]{:S(2)}, u32[]{:S(2)}) %collective-permute-start.5) | collective-permute-done | bytes 524320 | tf_op jit(solution)/shard_map/ppermute | solution.py:39
  19.4 1.4 %edge_scores.1.refs_0_ = f32[128,128]{1,0:T(8,128)S(1)} custom-call(bf16[192,2048]{1,0:T(8,128)(2,1)S(1)} %bitcast.25, bf16[192,1024]{1,0:T(8,128)(2,1)S(1)} %get-tuple-element.40.og_ref.refs_0_, bf16[192,1024]{1,0:T(8,128)(2,1)S(1)} %get-tuple-element.48.og_ref.refs_1_, bf16[192,2048]{1,0:T(8,128)(2,1)S(1)} %bitcast.11, bf16[192,2048]{1,0:T(8,128)(2,1)S(1)} %bitcast.18, ...), custom_call_target="tpu_custom_call" | custom-call | flops 100000000 | bytes 1000 | tf_op jit(solution)/shard_map/edge_scores/pallas_call | solution.py:295
  20.9 1.6 %collective-permute-start.6 = (f32[128,128]{1,0:T(8,128)S(1)}, f32[128,128]{1,0:T(8,128)S(1)}, u32[]{:S(2)}, u32[]{:S(2)}) collective-permute-start(f32[128,128]{1,0:T(8,128)S(1)} %edge_scores.1.refs_0_), channel_id=1, source_target_pairs={{0,1},{1,0},{8,9},{9,8},{16,17},{17,16},{24,25},{25,24},{2,3},{3,2... | collective-permute-start | bytes 196616 | tf_op jit(solution)/shard_map/ppermute | solution.py:82
  22.5 2.3 %causal.1 = bf16[192,2048]{1,0:T(8,128)(2,1)} custom-call(bf16[192,2048]{1,0:T(8,128)(2,1)S(1)} %bitcast.12, bf16[192,2048]{1,0:T(8,128)(2,1)S(1)} %bitcast.19, bf16[128,2048]{1,0:T(8,128)(2,1)S(1)} %collective-permute-done.5.refs_4_.early_ref, f32[128,128]{1,0:T(8,128)S(1)} %copy-done.3, f32[64,2048]{1,0:T(8,128)S(1)} %inner_causal.1.inner_ref, ...), custom_call_target="tpu_custom_call" | custom-call | flops 100000000 | bytes 1000 | tf_op jit(solution)/shard_map/causal/pallas_call | solution.py:295
  24.8 0.4 %collective-permute-done.6.refs_1_ = f32[128,128]{1,0:T(8,128)S(1)} collective-permute-done((f32[128,128]{1,0:T(8,128)S(1)}, f32[128,128]{1,0:T(8,128)S(1)}, u32[]{:S(2)}, u32[]{:S(2)}) %collective-permute-start.6) | collective-permute-done | bytes 65568 | tf_op jit(solution)/shard_map/ppermute | solution.py:82
  25.2 4.1 %collective-permute-start.9 = (bf16[128,128]{1,0:T(8,128)(2,1)S(1)}, bf16[128,128]{1,0:T(8,128)(2,1)S(1)}, u32[]{:S(2)}, u32[]{:S(2)}) collective-permute-start(bf16[128,128]{1,0:T(8,128)(2,1)S(1)} %add.16), channel_id=1, source_target_pairs={{0,24},{1,25},{8,16},{9,17},{16,8},{17,9},{24,0},{25,1},{2,26},{3,... | collective-permute-start | bytes 98312 | tf_op jit(solution)/shard_map/ppermute | solution.py:82
  29.4 0.6 %collective-permute-start.7 = (bf16[128,128]{1,0:T(8,128)(2,1)S(1)}, bf16[128,128]{1,0:T(8,128)(2,1)S(1)}, u32[]{:S(2)}, u32[]{:S(2)}) collective-permute-start(bf16[128,128]{1,0:T(8,128)(2,1)S(1)} %add.16), channel_id=1, source_target_pairs={{0,8},{1,9},{8,0},{9,1},{16,24},{17,25},{24,16},{25,17},{2,10},{3,... | collective-permute-start | bytes 98312 | tf_op jit(solution)/shard_map/ppermute | solution.py:82
  30.0 0.6 %collective-permute-done.11.refs_3_ = bf16[128,1024]{1,0:T(8,128)(2,1)S(1)} collective-permute-done((bf16[128,1024]{1,0:T(8,128)(2,1)S(1)}, bf16[128,1024]{1,0:T(8,128)(2,1)S(1)}, u32[]{:S(2)}, u32[]{:S(2)}) %collective-permute-start.11) | collective-permute-done | bytes 262176 | tf_op jit(solution)/shard_map/ppermute | solution.py:34
  30.6 2.8 %adjoint.1 = (bf16[192,2048]{1,0:T(8,128)(2,1)}, bf16[192,2048]{1,0:T(8,128)(2,1)}) custom-call(bf16[192,2048]{1,0:T(8,128)(2,1)S(1)} %bitcast.26, bf16[192,2048]{1,0:T(8,128)(2,1)S(1)} %bitcast.13, bf16[192,2048]{1,0:T(8,128)(2,1)S(1)} %bitcast.20, f32[128,128]{1,0:T(8,128)S(1)} %copy-done.3, bf16[192,1024]{1,0:T(8,128)(2,1)S(1)} %get-tuple-element.40.og_ref.refs_0_, ...), custom_call_target="tpu_custom_call" | custom-call | flops 100000000 | bytes 1000 | tf_op jit(solution)/shard_map/adjoint/pallas_call | solution.py:295
  33.4 0.0 collective-permute-done.9
  33.4 0.7 %collective-permute-done.8 = bf16[128,128]{1,0:T(8,128)(2,1)S(1)} collective-permute-done((bf16[128,128]{1,0:T(8,128)(2,1)S(1)}, bf16[128,128]{1,0:T(8,128)(2,1)S(1)}, u32[]{:S(2)}, u32[]{:S(2)}) %collective-permute-start.8) | collective-permute-done | bytes 32800 | tf_op jit(solution)/shard_map/ppermute | solution.py:82
  34.2 0.0 collective-permute-done.7
  34.2 0.1 rev.4
  34.3 0.6 %broadcast_multiply_fusion = f32[128,128]{1,0:T(8,128)} fusion(f32[128,128]{1,0:T(8,128)S(1)} %rev.4), kind=kLoop, calls=%fused_computation.1 | loop fusion | flops 16384 | bytes 131072 | tf_op jit(solution)/shard_map/mul | solution.py:389
  (13 shorter events, 0.1 us)
Async XLA Ops:
  0.6 8.4 %copy-start = (bf16[1,192,2048]{2,1,0:T(8,128)(2,1)S(1)}, bf16[1,192,2048]{2,1,0:T(8,128)(2,1)}, u32[]{:S(2)}) copy-start(bf16[1,192,2048]{2,1,0:T(8,128)(2,1)} %param.6) | copy-start | bytes 2359300
  0.6 8.3 %copy-start.1 = (bf16[1,192,2048]{2,1,0:T(8,128)(2,1)S(1)}, bf16[1,192,2048]{2,1,0:T(8,128)(2,1)}, u32[]{:S(2)}) copy-start(bf16[1,192,2048]{2,1,0:T(8,128)(2,1)} %param.7) | copy-start | bytes 2359300
  0.7 8.3 %copy-start.3 = (f32[128,128]{1,0:T(8,128)S(1)}, f32[128,128]{1,0:T(8,128)}, u32[]{:S(2)}) copy-start(f32[128,128]{1,0:T(8,128)} %filter_ref.5) | copy-start | bytes 196612
  2.4 17.0 %collective-permute-start.5 = (bf16[128,2048]{1,0:T(8,128)(2,1)S(1)}, bf16[128,2048]{1,0:T(8,128)(2,1)S(1)}, u32[]{:S(2)}, u32[]{:S(2)}) collective-permute-start(bf16[128,2048]{1,0:T(8,128)(2,1)S(1)} %get-tuple-element.49), channel_id=1, source_target_pairs={{0,8},{8,16},{16,24},{24,0},{1,9},{9,17},{17,25},{25,1},{2,10},{10... | collective-permute-start | bytes 1572872 | tf_op jit(solution)/shard_map/ppermute | solution.py:39
  5.5 1.9 %collective-permute-start = (bf16[48,2048]{1,0:T(8,128)(2,1)S(1)}, bf16[48,2048]{1,0:T(8,128)(2,1)S(1)}, u32[]{:S(2)}, u32[]{:S(2)}) collective-permute-start(bf16[48,2048]{1,0:T(8,128)(2,1)S(1)} %get-tuple-element.35), channel_id=1, source_target_pairs={{0,2},{2,0},{4,6},{6,4},{1,3},{3,1},{5,7},{7,5},{8,10},{10,8},{12,... | collective-permute-start | bytes 589832 | tf_op jit(solution)/shard_map/ppermute | solution.py:57
  5.5 5.6 %collective-permute-start.1 = (bf16[48,1024]{1,0:T(8,128)(2,1)S(1)}, bf16[48,1024]{1,0:T(8,128)(2,1)S(1)}, u32[]{:S(2)}, u32[]{:S(2)}) collective-permute-start(bf16[48,1024]{1,0:T(8,128)(2,1)S(1)} %get-tuple-element.36), channel_id=1, source_target_pairs={{0,4},{2,6},{4,0},{6,2},{1,5},{3,7},{5,1},{7,3},{8,12},{10,14},{12... | collective-permute-start | bytes 294920 | tf_op jit(solution)/shard_map/ppermute | solution.py:57
  7.0 5.4 %collective-permute-start.2 = (bf16[48,1024]{1,0:T(8,128)(2,1)S(1)}, bf16[48,1024]{1,0:T(8,128)(2,1)S(1)}, u32[]{:S(2)}, u32[]{:S(2)}) collective-permute-start(bf16[48,1024]{1,0:T(8,128)(2,1)S(1)} %get-tuple-element.37), channel_id=1, source_target_pairs={{0,6},{2,4},{4,2},{6,0},{1,7},{3,5},{5,3},{7,1},{8,14},{10,12},{12... | collective-permute-start | bytes 294920 | tf_op jit(solution)/shard_map/ppermute | solution.py:57
  7.3 5.1 %copy-start.2 = (bf16[1,192,2048]{2,1,0:T(8,128)(2,1)S(1)}, bf16[1,192,2048]{2,1,0:T(8,128)(2,1)}, u32[]{:S(2)}) copy-start(bf16[1,192,2048]{2,1,0:T(8,128)(2,1)} %param.5) | copy-start | bytes 2359300
  7.3 7.9 %collective-permute-start.3 = (bf16[48,1024]{1,0:T(8,128)(2,1)S(1)}, bf16[48,1024]{1,0:T(8,128)(2,1)S(1)}, u32[]{:S(2)}, u32[]{:S(2)}) collective-permute-start(bf16[48,1024]{1,0:T(8,128)(2,1)S(1)} %get-tuple-element.44), channel_id=1, source_target_pairs={{0,4},{2,6},{4,0},{6,2},{1,5},{3,7},{5,1},{7,3},{8,12},{10,14},{12... | collective-permute-start | bytes 294920 | tf_op jit(solution)/shard_map/ppermute | solution.py:57
  8.8 7.8 %collective-permute-start.4 = (bf16[48,1024]{1,0:T(8,128)(2,1)S(1)}, bf16[48,1024]{1,0:T(8,128)(2,1)S(1)}, u32[]{:S(2)}, u32[]{:S(2)}) collective-permute-start(bf16[48,1024]{1,0:T(8,128)(2,1)S(1)} %get-tuple-element.45), channel_id=1, source_target_pairs={{0,6},{2,4},{4,2},{6,0},{1,7},{3,5},{5,3},{7,1},{8,14},{10,12},{12... | collective-permute-start | bytes 294920 | tf_op jit(solution)/shard_map/ppermute | solution.py:57
  12.6 17.4 %collective-permute-start.10 = (bf16[128,1024]{1,0:T(8,128)(2,1)S(1)}, bf16[128,1024]{1,0:T(8,128)(2,1)S(1)}, u32[]{:S(2)}, u32[]{:S(2)}) collective-permute-start(bf16[128,1024]{1,0:T(8,128)(2,1)S(1)} %get-tuple-element.55), channel_id=1, source_target_pairs={{8,0},{16,8},{24,16},{9,1},{17,9},{25,17},{10,2},{18,10},{26,18},{... | collective-permute-start | bytes 786440 | tf_op jit(solution)/shard_map/ppermute | solution.py:34
  16.8 13.8 %collective-permute-start.11 = (bf16[128,1024]{1,0:T(8,128)(2,1)S(1)}, bf16[128,1024]{1,0:T(8,128)(2,1)S(1)}, u32[]{:S(2)}, u32[]{:S(2)}) collective-permute-start(bf16[128,1024]{1,0:T(8,128)(2,1)S(1)} %get-tuple-element.56), channel_id=1, source_target_pairs={{8,0},{16,8},{24,16},{9,1},{17,9},{25,17},{10,2},{18,10},{26,18},{... | collective-permute-start | bytes 786440 | tf_op jit(solution)/shard_map/ppermute | solution.py:34
  20.9 4.3 %collective-permute-start.6 = (f32[128,128]{1,0:T(8,128)S(1)}, f32[128,128]{1,0:T(8,128)S(1)}, u32[]{:S(2)}, u32[]{:S(2)}) collective-permute-start(f32[128,128]{1,0:T(8,128)S(1)} %edge_scores.1.refs_0_), channel_id=1, source_target_pairs={{0,1},{1,0},{8,9},{9,8},{16,17},{17,16},{24,25},{25,24},{2,3},{3,2... | collective-permute-start | bytes 196616 | tf_op jit(solution)/shard_map/ppermute | solution.py:82
  25.2 8.2 %collective-permute-start.9 = (bf16[128,128]{1,0:T(8,128)(2,1)S(1)}, bf16[128,128]{1,0:T(8,128)(2,1)S(1)}, u32[]{:S(2)}, u32[]{:S(2)}) collective-permute-start(bf16[128,128]{1,0:T(8,128)(2,1)S(1)} %add.16), channel_id=1, source_target_pairs={{0,24},{1,25},{8,16},{9,17},{16,8},{17,9},{24,0},{25,1},{2,26},{3,... | collective-permute-start | bytes 98312 | tf_op jit(solution)/shard_map/ppermute | solution.py:82
  29.4 4.8 %collective-permute-start.8 = (bf16[128,128]{1,0:T(8,128)(2,1)S(1)}, bf16[128,128]{1,0:T(8,128)(2,1)S(1)}, u32[]{:S(2)}, u32[]{:S(2)}) collective-permute-start(bf16[128,128]{1,0:T(8,128)(2,1)S(1)} %add.16), channel_id=1, source_target_pairs={{0,16},{1,17},{8,24},{9,25},{16,0},{17,1},{24,8},{25,9},{2,18},{3,... | collective-permute-start | bytes 98312 | tf_op jit(solution)/shard_map/ppermute | solution.py:82
  29.4 4.8 %collective-permute-start.7 = (bf16[128,128]{1,0:T(8,128)(2,1)S(1)}, bf16[128,128]{1,0:T(8,128)(2,1)S(1)}, u32[]{:S(2)}, u32[]{:S(2)}) collective-permute-start(bf16[128,128]{1,0:T(8,128)(2,1)S(1)} %add.16), channel_id=1, source_target_pairs={{0,8},{1,9},{8,0},{9,1},{16,24},{17,25},{24,16},{25,17},{2,10},{3,... | collective-permute-start | bytes 98312 | tf_op jit(solution)/shard_map/ppermute | solution.py:82

commit v5 on v4

--- a/solution.py
+++ b/solution.py
@@ -10,7 +10,7 @@
 
 LANES = 128
 BLOCK = 32
-STEP = 4 * LANES
+STEP = 1 * LANES
 VMEM = pl.BlockSpec(memory_space=pltpu.VMEM)
 ANYWHERE = pl.BlockSpec(memory_space=pl.ANY)
 SCALAR = pl.BlockSpec(memory_space=pltpu.SMEM)
@@ -133,24 +133,34 @@
     return []
 
 
-def pack_kernel(count, last, grad_ref, k_ref, v_ref, *refs):
+def cut_out(cuts_of, count, grad_ref, parts, sem):
+    here = lax.axis_index("tp")
+    width = grad_ref.shape[1] // count
+    cuts = []
+    for n, ((step, half), part) in enumerate(zip(cuts_of, parts)):
+        columns = part.shape[1]
+        place = pl.multiple_of(target(here, step, count) * width + max(half, 0) * columns, columns)
+        cuts.append(pltpu.make_async_copy(grad_ref.at[:, pl.ds(place, columns)], part, sem.at[n]))
+    return cuts
+
+
+def second_pack_kernel(cuts_of, count, grad_ref, *refs):
+    cuts = cut_out(cuts_of, count, grad_ref, refs[:-1], refs[-1])
+    for copy in cuts:
+        copy.start()
+    for copy in cuts:
+        copy.wait()
+
+
+def pack_kernel(cuts_of, count, last, grad_ref, k_ref, v_ref, *refs):
     parts, (tail_ref, k_stage, v_stage, part_sem, tail_sem) = refs[:-5], refs[-5:]
-    here = lax.axis_index("tp")
     height = k_stage.shape[0]
-    width = parts[0].shape[1]
     below = pl.ds(k_ref.shape[0] - height, height)
     tails = [
         pltpu.make_async_copy(ref.at[below], into, tail_sem.at[n])
         for n, (ref, into) in enumerate([(k_ref, k_stage), (v_ref, v_stage)])
     ]
-    cuts = []
-    for n, part in enumerate(parts):
-        half, step = (0, n) if n < NEAR else divmod(n - NEAR, count - NEAR)
-        step += 0 if n < NEAR else NEAR
-        columns = part.shape[1]
-        place = pl.multiple_of(target(here, step, count) * width + half * columns, columns)
-        columns = pl.ds(place, columns)
-        cuts.append(pltpu.make_async_copy(grad_ref.at[:, columns], part, part_sem.at[n]))
+    cuts = cut_out(cuts_of, count, grad_ref, parts, part_sem)
     for copy in tails + cuts:
         copy.start()
     for copy in tails:
@@ -226,16 +236,15 @@
 
 
 def scores_kernel(taps, group_width, q_ref, *refs):
-    og_refs, (k_ref, v_ref, early_ref) = refs[:HALVES], refs[HALVES : HALVES + 3]
-    inner_refs, out_ref = refs[HALVES + 3 : -1], refs[-1]
-    height = inner_refs[0].shape[0]
+    og_refs, (k_ref, v_ref, early_ref, inner_ref, out_ref) = refs[:HALVES], refs[HALVES:]
     for c, rows in tiles(k_ref.shape[1], group_width):
-        grad_mix = widen(columns_of(og_refs, c)[:taps]) * widen(q_ref[:taps, c])
-        window = product(k_ref[:taps, c], v_ref[:taps, c])
+        there = c.stop <= og_refs[0].shape[1]
+        last = taps if there else k_ref.shape[0]
+        grad_mix = widen(columns_of(og_refs, c)[:last]) * widen(q_ref[:last, c])
+        window = product(k_ref[:last, c], v_ref[:last, c])
         window = jnp.concatenate([early_ref[:, c], window], axis=0)
-        half, first = divmod(rows.start, height)
-        inner = inner_refs[half][first : first + rows.stop - rows.start, :]
-        out_ref[rows, :] = lag_sums(taps, group_width, grad_mix, window) + inner
+        sums = lag_sums(taps, group_width, grad_mix, window)
+        out_ref[rows, :] = sums + inner_ref[rows, :] if there else sums
 
 
 def turned_base(filter_ref):
@@ -318,12 +327,16 @@
     count = lax.axis_size("tp")
     height = rows // count
     far = count - NEAR
-    pieces = [jax.ShapeDtypeStruct((height, channels), jnp.bfloat16)] * NEAR
-    pieces += [jax.ShapeDtypeStruct((height, width), jnp.bfloat16)] * (HALVES * far)
+    piece = jax.ShapeDtypeStruct((height, channels), jnp.bfloat16)
+    half_piece = jax.ShapeDtypeStruct((height, width), jnp.bfloat16)
+    first_cuts = [(step, -1) for step in range(1, NEAR)] + [(step, 0) for step in range(NEAR, count)]
+    second_cuts = [(0, -1)] + [(step, 1) for step in range(NEAR, count)]
+    pieces = [half_piece if half >= 0 else piece for _, half in first_cuts]
+    second_pieces = [half_piece if half >= 0 else piece for _, half in second_cuts]
     half_wide = jax.ShapeDtypeStruct((rows, width), jnp.bfloat16)
     half_edge = jax.ShapeDtypeStruct((taps, width), jnp.bfloat16)
     *parts, tail = pl.pallas_call(
-        functools.partial(pack_kernel, count, lax.axis_size("ctx") - 1),
+        functools.partial(pack_kernel, first_cuts, count, lax.axis_size("ctx") - 1),
         in_specs=[ANYWHERE] * 3,
         out_specs=[ANYWHERE] * len(pieces) + [VMEM],
         out_shape=pieces + [edge],
@@ -333,16 +346,25 @@
         compiler_params=pltpu.CompilerParams(vmem_limit_bytes=LIMIT * 1024 * 1024),
     )(*[in_hbm(a) for a in (out_grad[0], k, v)])
     early = passed_round(tail, "ctx", 1)
-    near = parts[:1] + [exchanged(part, "tp", step) for step, part in enumerate(parts[1:NEAR], 1)]
+    near = [exchanged(part, "tp", step) for step, part in enumerate(parts[: NEAR - 1], 1)]
+    grad_in, near[-1] = lax.optimization_barrier((out_grad[0], near[-1]))
+    own, *second_parts = pl.pallas_call(
+        functools.partial(second_pack_kernel, second_cuts, count),
+        in_specs=[ANYWHERE],
+        out_specs=[ANYWHERE] * len(second_pieces),
+        out_shape=second_pieces,
+        scratch_shapes=[pltpu.SemaphoreType.DMA((len(second_pieces),))],
+        name="second_pack",
+        compiler_params=pltpu.CompilerParams(vmem_limit_bytes=LIMIT * 1024 * 1024),
+    )(in_hbm(grad_in))
+    near = [own] + near
     inner_rows = jax.ShapeDtypeStruct((rows - taps, channels), jnp.float32)
     (inner,) = call(
         functools.partial(inner_mixed_kernel, taps, group_width), "inner_causal", (k, v, filters), [inner_rows], False, COST
     )
     grads, heads, inners = [], [], []
     for half in range(HALVES):
-        mine = parts[NEAR + half * far : NEAR + (half + 1) * far]
-        if half:
-            mine, near[-1] = lax.optimization_barrier((mine, near[-1]))
+        mine = second_parts if half else parts[NEAR - 1 :]
         brought_in = [exchanged(part, "tp", step) for step, part in enumerate(mine, NEAR)]
         if half:
             brought_in, inners[0] = lax.optimization_barrier((brought_in, inners[0]))
@@ -363,10 +385,11 @@
             head = product(grad[:taps], q[:taps, c])
         grads.append(grad)
         heads.append(head)
-        (lags,) = call(
-            functools.partial(inner_scores_kernel, taps, group_width, half), "inner_scores", (q, grad, k, v), [half_small], False, COST
-        )
-        inners.append(lags)
+        if not half:
+            (lags,) = call(
+                functools.partial(inner_scores_kernel, taps, group_width, 0), "inner_scores", (q, grad, k, v), [half_small], False, COST
+            )
+            inners.append(lags)
     work = functools.partial
     (lags,) = call(
         work(scores_kernel, taps, group_width), "edge_scores", (q, *grads, k, v, early, *inners), [small], False, COST

time: 35.1 us -> 34.3 us (0.977)
  waiting for transfers between devices: 6.54 us -> 5.59 us
  Pallas kernels: 11.3 us -> 11.8 us
    ppermute x5, waiting for transfers between devices: 4.25 us -> 3.12 us  [exchanged(): return lax.ppermute(part, axis, pairs)]
    ppermute x1, waiting for transfers between devices: 0.55 us -> 1.43 us  [passed_round(): lax.ppermute(value, axis, [(index, (index + steps) % count) for index in...]
    pallas_call x1 -> x2, Pallas kernels: 1.74 us -> 2.51 us  [the longest x1 1.45 us: local(): pl.pallas_call(functools.partial(pack_kernel, first_cuts, count, lax.axis...]
    ppermute x4, waiting for transfers between devices: 1.15 us -> 0.4 us  [brought(): lax.ppermute(value, axes, [(index, index ^ step) for index in range(count)])]
    pallas_call x8 -> x7, Pallas kernels: 9.6 us -> 9.24 us  [call(): pl.pallas_call(kernel, in_specs=[SCALAR if a.dtype == jnp.int32 else VMEM...]
  transfers between devices with their start and end apart: 12 -> 12, of which waited for: 8 -> 6; matrix products, arithmetic and copies ran while one was open for 0% -> 0% of each run, Pallas kernels for 28% -> 30%
where the time goes in v5:
time: 34.3 us; the launch traced here: 34.1 us
  starting transfers between devices  15.3 us (45%)
  Pallas kernels  11.8 us (34%)
  waiting for transfers between devices  5.59 us (16%)
  between operations  0.76 us (2%)
  other arithmetic  0.67 us (2%)
    pallas_call x7, Pallas kernels, call(): pl.pallas_call(kernel, in_specs=[SCALAR if a.dtype == jnp.int32 else VMEM...  9.24 us
    ppermute x4, starting transfers between devices, brought(): lax.ppermute(value, axes, [(index, index ^ step) for index in range(count)])  6.04 us
    ppermute x5, starting transfers between devices, exchanged(): return lax.ppermute(part, axis, pairs)  3.56 us
    ppermute x5, waiting for transfers between devices, exchanged(): return lax.ppermute(part, axis, pairs)  3.12 us
    ppermute x1, starting transfers between devices, passed_round(): lax.ppermute(value, axis, [(index, (index + steps) % count) for index in...  3.08 us
    ppermute x2, starting transfers between devices, passed_along(): lax.ppermute(value, axis, [(source, source + steps) for source in range(f...  2.58 us
    pallas_call x1, Pallas kernels, local(): pl.pallas_call(functools.partial(pack_kernel, first_cuts, count, lax.axis...  1.45 us
    ppermute x1, waiting for transfers between devices, passed_round(): lax.ppermute(value, axis, [(index, (index + steps) % count) for index in...  1.43 us
  transfers between devices with their start and end apart: 12, of which 6 were waited for; matrix products, arithmetic and copies ran while one was open for 0% of the time, Pallas kernels for 30%

profile of v5, /device:TPU:0, one launch (start us, length us, event | category | flops | bytes accessed | tf_op | source)
XLA Modules:
  0.0 34.1 jit_solution(2754507508623731228)
XLA Ops:
  0.7 1.4 %pack.1 = (bf16[48,2048]{1,0:T(8,128)(2,1)S(1)}, bf16[48,1024]{1,0:T(8,128)(2,1)S(1)}, bf16[48,1024]{1,0:T(8,128)(2,1)S(1)}, bf16[128,2048]{1,0:T(8,128)(2,1)S(1)}) custom-call(bf16[48,8192]{1,0:T(8,128)(2,1)} %bitcast.24, bf16[192,2048]{1,0:T(8,128)(2,1)} %bitcast.7, bf16[192,2048]{1,0:T(8,128)(2,1)} %bitcast.13), custom_call_target="tpu_custom_call" | custom-call | tf_op jit(solution)/shard_map/pack/pallas_call | solution.py:338
  2.1 0.0 copy-start
  2.1 3.1 %collective-permute-start.5 = (bf16[128,2048]{1,0:T(8,128)(2,1)S(1)}, bf16[128,2048]{1,0:T(8,128)(2,1)S(1)}, u32[]{:S(2)}, u32[]{:S(2)}) collective-permute-start(bf16[128,2048]{1,0:T(8,128)(2,1)S(1)} %get-tuple-element.47), channel_id=1, source_target_pairs={{0,8},{8,16},{16,24},{24,0},{1,9},{9,17},{17,25},{25,1},{2,10},{10... | collective-permute-start | bytes 1572872 | tf_op jit(solution)/shard_map/ppermute | solution.py:39
  5.2 1.5 %collective-permute-start.1 = (bf16[48,1024]{1,0:T(8,128)(2,1)S(1)}, bf16[48,1024]{1,0:T(8,128)(2,1)S(1)}, u32[]{:S(2)}, u32[]{:S(2)}) collective-permute-start(bf16[48,1024]{1,0:T(8,128)(2,1)S(1)} %get-tuple-element.37), channel_id=1, source_target_pairs={{0,4},{2,6},{4,0},{6,2},{1,5},{3,7},{5,1},{7,3},{8,12},{10,14},{12... | collective-permute-start | bytes 294920 | tf_op jit(solution)/shard_map/ppermute | solution.py:57
  6.7 0.4 %collective-permute-start.2 = (bf16[48,1024]{1,0:T(8,128)(2,1)S(1)}, bf16[48,1024]{1,0:T(8,128)(2,1)S(1)}, u32[]{:S(2)}, u32[]{:S(2)}) collective-permute-start(bf16[48,1024]{1,0:T(8,128)(2,1)S(1)} %get-tuple-element.38), channel_id=1, source_target_pairs={{0,6},{2,4},{4,2},{6,0},{1,7},{3,5},{5,3},{7,1},{8,14},{10,12},{12... | collective-permute-start | bytes 294920 | tf_op jit(solution)/shard_map/ppermute | solution.py:57
  7.1 1.1 %second_pack.1 = (bf16[48,2048]{1,0:T(8,128)(2,1)S(1)}, bf16[48,1024]{1,0:T(8,128)(2,1)S(1)}, bf16[48,1024]{1,0:T(8,128)(2,1)S(1)}) custom-call(bf16[48,8192]{1,0:T(8,128)(2,1)} %bitcast.25), custom_call_target="tpu_custom_call" | custom-call | tf_op jit(solution)/shard_map/second_pack/pallas_call | solution.py:351
  8.1 1.6 %collective-permute-start.3 = (bf16[48,1024]{1,0:T(8,128)(2,1)S(1)}, bf16[48,1024]{1,0:T(8,128)(2,1)S(1)}, u32[]{:S(2)}, u32[]{:S(2)}) collective-permute-start(bf16[48,1024]{1,0:T(8,128)(2,1)S(1)} %get-tuple-element.42), channel_id=1, source_target_pairs={{0,4},{2,6},{4,0},{6,2},{1,5},{3,7},{5,1},{7,3},{8,12},{10,14},{12... | collective-permute-start | bytes 294920 | tf_op jit(solution)/shard_map/ppermute | solution.py:57
  9.7 0.1 collective-permute-start.4
  9.8 1.1 %inner_causal.1.inner_ref = f32[64,2048]{1,0:T(8,128)S(1)} custom-call(bf16[192,2048]{1,0:T(8,128)(2,1)S(1)} %bitcast.8, bf16[192,2048]{1,0:T(8,128)(2,1)S(1)} %bitcast.14, f32[128,128]{1,0:T(8,128)S(1)} %copy-done.3), custom_call_target="tpu_custom_call" | custom-call | flops 100000000 | bytes 1000 | tf_op jit(solution)/shard_map/inner_causal/pallas_call | solution.py:304
  10.9 0.0 collective-permute-done.1.refs_2_
  10.9 1.2 %collective-permute-done.2.refs_3_ = bf16[48,1024]{1,0:T(8,128)(2,1)S(1)} collective-permute-done((bf16[48,1024]{1,0:T(8,128)(2,1)S(1)}, bf16[48,1024]{1,0:T(8,128)(2,1)S(1)}, u32[]{:S(2)}, u32[]{:S(2)}) %collective-permute-start.2) | collective-permute-done | bytes 98336 | tf_op jit(solution)/shard_map/ppermute | solution.py:57
  12.1 0.1 gather.2
  12.3 1.3 %collective-permute-start.10 = (bf16[128,1024]{1,0:T(8,128)(2,1)S(1)}, bf16[128,1024]{1,0:T(8,128)(2,1)S(1)}, u32[]{:S(2)}, u32[]{:S(2)}) collective-permute-start(bf16[128,1024]{1,0:T(8,128)(2,1)S(1)} %get-tuple-element.53), channel_id=1, source_target_pairs={{8,0},{16,8},{24,16},{9,1},{17,9},{25,17},{10,2},{18,10},{26,18},{... | collective-permute-start | bytes 786440 | tf_op jit(solution)/shard_map/ppermute | solution.py:34
  13.6 0.8 %inner_scores.1.refs_5_ = f32[64,128]{1,0:T(8,128)S(1)} custom-call(bf16[192,2048]{1,0:T(8,128)(2,1)S(1)} %bitcast.20, bf16[192,1024]{1,0:T(8,128)(2,1)S(1)} %get-tuple-element.41.og_ref.refs_0_, bf16[192,2048]{1,0:T(8,128)(2,1)S(1)} %bitcast.9, bf16[192,2048]{1,0:T(8,128)(2,1)S(1)} %bitcast.15), custom_call_target="tpu_custom_call" | custom-call | flops 100000000 | bytes 1000 | tf_op jit(solution)/shard_map/inner_scores/pallas_call | solution.py:304
  14.4 0.6 %collective-permute-done.3.refs_2_ = bf16[48,1024]{1,0:T(8,128)(2,1)S(1)} collective-permute-done((bf16[48,1024]{1,0:T(8,128)(2,1)S(1)}, bf16[48,1024]{1,0:T(8,128)(2,1)S(1)}, u32[]{:S(2)}, u32[]{:S(2)}) %collective-permute-start.3) | collective-permute-done | bytes 98336 | tf_op jit(solution)/shard_map/ppermute | solution.py:57
  15.0 1.3 %collective-permute-done.4.refs_3_ = bf16[48,1024]{1,0:T(8,128)(2,1)S(1)} collective-permute-done((bf16[48,1024]{1,0:T(8,128)(2,1)S(1)}, bf16[48,1024]{1,0:T(8,128)(2,1)S(1)}, u32[]{:S(2)}, u32[]{:S(2)}) %collective-permute-start.4) | collective-permute-done | bytes 98336 | tf_op jit(solution)/shard_map/ppermute | solution.py:57
  16.3 0.1 gather.3
  16.5 1.3 %collective-permute-start.11 = (bf16[128,1024]{1,0:T(8,128)(2,1)S(1)}, bf16[128,1024]{1,0:T(8,128)(2,1)S(1)}, u32[]{:S(2)}, u32[]{:S(2)}) collective-permute-start(bf16[128,1024]{1,0:T(8,128)(2,1)S(1)} %get-tuple-element.54), channel_id=1, source_target_pairs={{8,0},{16,8},{24,16},{9,1},{17,9},{25,17},{10,2},{18,10},{26,18},{... | collective-permute-start | bytes 786440 | tf_op jit(solution)/shard_map/ppermute | solution.py:34
  17.8 1.4 %collective-permute-done.5.refs_4_.early_ref = bf16[128,2048]{1,0:T(8,128)(2,1)S(1)} collective-permute-done((bf16[128,2048]{1,0:T(8,128)(2,1)S(1)}, bf16[128,2048]{1,0:T(8,128)(2,1)S(1)}, u32[]{:S(2)}, u32[]{:S(2)}) %collective-permute-start.5) | collective-permute-done | bytes 524320 | tf_op jit(solution)/shard_map/ppermute | solution.py:39
  19.2 1.7 %edge_scores.1.refs_0_ = f32[128,128]{1,0:T(8,128)S(1)} custom-call(bf16[192,2048]{1,0:T(8,128)(2,1)S(1)} %bitcast.22, bf16[192,1024]{1,0:T(8,128)(2,1)S(1)} %get-tuple-element.41.og_ref.refs_0_, bf16[192,1024]{1,0:T(8,128)(2,1)S(1)} %get-tuple-element.46.refs_1_, bf16[192,2048]{1,0:T(8,128)(2,1)S(1)} %bitcast.10, bf16[192,2048]{1,0:T(8,128)(2,1)S(1)} %bitcast.16, ...), custom_call_target="tpu_custom_call" | custom-call | flops 100000000 | bytes 1000 | tf_op jit(solution)/shard_map/edge_scores/pallas_call | solution.py:304
  20.9 1.6 %collective-permute-start.6 = (f32[128,128]{1,0:T(8,128)S(1)}, f32[128,128]{1,0:T(8,128)S(1)}, u32[]{:S(2)}, u32[]{:S(2)}) collective-permute-start(f32[128,128]{1,0:T(8,128)S(1)} %edge_scores.1.refs_0_), channel_id=1, source_target_pairs={{0,1},{1,0},{8,9},{9,8},{16,17},{17,16},{24,25},{25,24},{2,3},{3,2... | collective-permute-start | bytes 196616 | tf_op jit(solution)/shard_map/ppermute | solution.py:82
  22.5 2.4 %causal.1 = bf16[192,2048]{1,0:T(8,128)(2,1)} custom-call(bf16[192,2048]{1,0:T(8,128)(2,1)S(1)} %bitcast.11, bf16[192,2048]{1,0:T(8,128)(2,1)S(1)} %bitcast.17, bf16[128,2048]{1,0:T(8,128)(2,1)S(1)} %collective-permute-done.5.refs_4_.early_ref, f32[128,128]{1,0:T(8,128)S(1)} %copy-done.3, f32[64,2048]{1,0:T(8,128)S(1)} %inner_causal.1.inner_ref, ...), custom_call_target="tpu_custom_call" | custom-call | flops 100000000 | bytes 1000 | tf_op jit(solution)/shard_map/causal/pallas_call | solution.py:304
  24.9 0.4 %collective-permute-done.6.refs_1_ = f32[128,128]{1,0:T(8,128)S(1)} collective-permute-done((f32[128,128]{1,0:T(8,128)S(1)}, f32[128,128]{1,0:T(8,128)S(1)}, u32[]{:S(2)}, u32[]{:S(2)}) %collective-permute-start.6) | collective-permute-done | bytes 65568 | tf_op jit(solution)/shard_map/ppermute | solution.py:82
  25.3 3.3 %collective-permute-start.9 = (bf16[128,128]{1,0:T(8,128)(2,1)S(1)}, bf16[128,128]{1,0:T(8,128)(2,1)S(1)}, u32[]{:S(2)}, u32[]{:S(2)}) collective-permute-start(bf16[128,128]{1,0:T(8,128)(2,1)S(1)} %add.16), channel_id=1, source_target_pairs={{0,24},{1,25},{8,16},{9,17},{16,8},{17,9},{24,0},{25,1},{2,26},{3,... | collective-permute-start | bytes 98312 | tf_op jit(solution)/shard_map/ppermute | solution.py:82
  28.6 0.0 collective-permute-start.8
  28.6 1.1 %collective-permute-start.7 = (bf16[128,128]{1,0:T(8,128)(2,1)S(1)}, bf16[128,128]{1,0:T(8,128)(2,1)S(1)}, u32[]{:S(2)}, u32[]{:S(2)}) collective-permute-start(bf16[128,128]{1,0:T(8,128)(2,1)S(1)} %add.16), channel_id=1, source_target_pairs={{0,8},{1,9},{8,0},{9,1},{16,24},{17,25},{24,16},{25,17},{2,10},{3,... | collective-permute-start | bytes 98312 | tf_op jit(solution)/shard_map/ppermute | solution.py:82
  29.7 0.6 %collective-permute-done.11.refs_3_ = bf16[128,1024]{1,0:T(8,128)(2,1)S(1)} collective-permute-done((bf16[128,1024]{1,0:T(8,128)(2,1)S(1)}, bf16[128,1024]{1,0:T(8,128)(2,1)S(1)}, u32[]{:S(2)}, u32[]{:S(2)}) %collective-permute-start.11) | collective-permute-done | bytes 262176 | tf_op jit(solution)/shard_map/ppermute | solution.py:34
  30.4 3.0 %adjoint.1 = (bf16[192,2048]{1,0:T(8,128)(2,1)}, bf16[192,2048]{1,0:T(8,128)(2,1)}) custom-call(bf16[192,2048]{1,0:T(8,128)(2,1)S(1)} %bitcast.23, bf16[192,2048]{1,0:T(8,128)(2,1)S(1)} %bitcast.12, bf16[192,2048]{1,0:T(8,128)(2,1)S(1)} %bitcast.18, f32[128,128]{1,0:T(8,128)S(1)} %copy-done.3, bf16[192,1024]{1,0:T(8,128)(2,1)S(1)} %get-tuple-element.41.og_ref.refs_0_, ...), custom_call_target="tpu_custom_call" | custom-call | flops 100000000 | bytes 1000 | tf_op jit(solution)/shard_map/adjoint/pallas_call | solution.py:304
  33.3 0.0 collective-permute-done.9
  33.3 0.0 collective-permute-done.8
  33.4 0.1 rev.4
  33.5 0.6 %broadcast_multiply_fusion = f32[128,128]{1,0:T(8,128)} fusion(f32[128,128]{1,0:T(8,128)S(1)} %rev.4), kind=kLoop, calls=%fused_computation.1 | loop fusion | flops 16384 | bytes 131072 | tf_op jit(solution)/shard_map/mul | solution.py:412
  (13 shorter events, 0.1 us)
Async XLA Ops:
  0.6 9.2 %copy-start.1 = (bf16[1,192,2048]{2,1,0:T(8,128)(2,1)S(1)}, bf16[1,192,2048]{2,1,0:T(8,128)(2,1)}, u32[]{:S(2)}) copy-start(bf16[1,192,2048]{2,1,0:T(8,128)(2,1)} %param.7) | copy-start | bytes 2359300
  0.6 9.2 %copy-start.3 = (f32[128,128]{1,0:T(8,128)S(1)}, f32[128,128]{1,0:T(8,128)}, u32[]{:S(2)}) copy-start(f32[128,128]{1,0:T(8,128)} %filter_ref.5) | copy-start | bytes 196612
  2.1 7.7 %copy-start = (bf16[1,192,2048]{2,1,0:T(8,128)(2,1)S(1)}, bf16[1,192,2048]{2,1,0:T(8,128)(2,1)}, u32[]{:S(2)}) copy-start(bf16[1,192,2048]{2,1,0:T(8,128)(2,1)} %param.6) | copy-start | bytes 2359300
  2.1 17.1 %collective-permute-start.5 = (bf16[128,2048]{1,0:T(8,128)(2,1)S(1)}, bf16[128,2048]{1,0:T(8,128)(2,1)S(1)}, u32[]{:S(2)}, u32[]{:S(2)}) collective-permute-start(bf16[128,2048]{1,0:T(8,128)(2,1)S(1)} %get-tuple-element.47), channel_id=1, source_target_pairs={{0,8},{8,16},{16,24},{24,0},{1,9},{9,17},{17,25},{25,1},{2,10},{10... | collective-permute-start | bytes 1572872 | tf_op jit(solution)/shard_map/ppermute | solution.py:39
  5.2 1.9 %collective-permute-start = (bf16[48,2048]{1,0:T(8,128)(2,1)S(1)}, bf16[48,2048]{1,0:T(8,128)(2,1)S(1)}, u32[]{:S(2)}, u32[]{:S(2)}) collective-permute-start(bf16[48,2048]{1,0:T(8,128)(2,1)S(1)} %get-tuple-element.33), channel_id=1, source_target_pairs={{0,2},{2,0},{4,6},{6,4},{1,3},{3,1},{5,7},{7,5},{8,10},{10,8},{12,... | collective-permute-start | bytes 589832 | tf_op jit(solution)/shard_map/ppermute | solution.py:57
  5.2 5.7 %collective-permute-start.1 = (bf16[48,1024]{1,0:T(8,128)(2,1)S(1)}, bf16[48,1024]{1,0:T(8,128)(2,1)S(1)}, u32[]{:S(2)}, u32[]{:S(2)}) collective-permute-start(bf16[48,1024]{1,0:T(8,128)(2,1)S(1)} %get-tuple-element.37), channel_id=1, source_target_pairs={{0,4},{2,6},{4,0},{6,2},{1,5},{3,7},{5,1},{7,3},{8,12},{10,14},{12... | collective-permute-start | bytes 294920 | tf_op jit(solution)/shard_map/ppermute | solution.py:57
  6.7 5.4 %collective-permute-start.2 = (bf16[48,1024]{1,0:T(8,128)(2,1)S(1)}, bf16[48,1024]{1,0:T(8,128)(2,1)S(1)}, u32[]{:S(2)}, u32[]{:S(2)}) collective-permute-start(bf16[48,1024]{1,0:T(8,128)(2,1)S(1)} %get-tuple-element.38), channel_id=1, source_target_pairs={{0,6},{2,4},{4,2},{6,0},{1,7},{3,5},{5,3},{7,1},{8,14},{10,12},{12... | collective-permute-start | bytes 294920 | tf_op jit(solution)/shard_map/ppermute | solution.py:57
  8.1 6.9 %collective-permute-start.3 = (bf16[48,1024]{1,0:T(8,128)(2,1)S(1)}, bf16[48,1024]{1,0:T(8,128)(2,1)S(1)}, u32[]{:S(2)}, u32[]{:S(2)}) collective-permute-start(bf16[48,1024]{1,0:T(8,128)(2,1)S(1)} %get-tuple-element.42), channel_id=1, source_target_pairs={{0,4},{2,6},{4,0},{6,2},{1,5},{3,7},{5,1},{7,3},{8,12},{10,14},{12... | collective-permute-start | bytes 294920 | tf_op jit(solution)/shard_map/ppermute | solution.py:57
  9.7 2.4 %copy-start.2 = (bf16[1,192,2048]{2,1,0:T(8,128)(2,1)S(1)}, bf16[1,192,2048]{2,1,0:T(8,128)(2,1)}, u32[]{:S(2)}) copy-start(bf16[1,192,2048]{2,1,0:T(8,128)(2,1)} %param.5) | copy-start | bytes 2359300
  9.7 6.6 %collective-permute-start.4 = (bf16[48,1024]{1,0:T(8,128)(2,1)S(1)}, bf16[48,1024]{1,0:T(8,128)(2,1)S(1)}, u32[]{:S(2)}, u32[]{:S(2)}) collective-permute-start(bf16[48,1024]{1,0:T(8,128)(2,1)S(1)} %get-tuple-element.43), channel_id=1, source_target_pairs={{0,6},{2,4},{4,2},{6,0},{1,7},{3,5},{5,3},{7,1},{8,14},{10,12},{12... | collective-permute-start | bytes 294920 | tf_op jit(solution)/shard_map/ppermute | solution.py:57
  12.3 17.4 %collective-permute-start.10 = (bf16[128,1024]{1,0:T(8,128)(2,1)S(1)}, bf16[128,1024]{1,0:T(8,128)(2,1)S(1)}, u32[]{:S(2)}, u32[]{:S(2)}) collective-permute-start(bf16[128,1024]{1,0:T(8,128)(2,1)S(1)} %get-tuple-element.53), channel_id=1, source_target_pairs={{8,0},{16,8},{24,16},{9,1},{17,9},{25,17},{10,2},{18,10},{26,18},{... | collective-permute-start | bytes 786440 | tf_op jit(solution)/shard_map/ppermute | solution.py:34
  16.5 13.9 %collective-permute-start.11 = (bf16[128,1024]{1,0:T(8,128)(2,1)S(1)}, bf16[128,1024]{1,0:T(8,128)(2,1)S(1)}, u32[]{:S(2)}, u32[]{:S(2)}) collective-permute-start(bf16[128,1024]{1,0:T(8,128)(2,1)S(1)} %get-tuple-element.54), channel_id=1, source_target_pairs={{8,0},{16,8},{24,16},{9,1},{17,9},{25,17},{10,2},{18,10},{26,18},{... | collective-permute-start | bytes 786440 | tf_op jit(solution)/shard_map/ppermute | solution.py:34
  20.9 4.3 %collective-permute-start.6 = (f32[128,128]{1,0:T(8,128)S(1)}, f32[128,128]{1,0:T(8,128)S(1)}, u32[]{:S(2)}, u32[]{:S(2)}) collective-permute-start(f32[128,128]{1,0:T(8,128)S(1)} %edge_scores.1.refs_0_), channel_id=1, source_target_pairs={{0,1},{1,0},{8,9},{9,8},{16,17},{17,16},{24,25},{25,24},{2,3},{3,2... | collective-permute-start | bytes 196616 | tf_op jit(solution)/shard_map/ppermute | solution.py:82
  25.3 8.1 %collective-permute-start.9 = (bf16[128,128]{1,0:T(8,128)(2,1)S(1)}, bf16[128,128]{1,0:T(8,128)(2,1)S(1)}, u32[]{:S(2)}, u32[]{:S(2)}) collective-permute-start(bf16[128,128]{1,0:T(8,128)(2,1)S(1)} %add.16), channel_id=1, source_target_pairs={{0,24},{1,25},{8,16},{9,17},{16,8},{17,9},{24,0},{25,1},{2,26},{3,... | collective-permute-start | bytes 98312 | tf_op jit(solution)/shard_map/ppermute | solution.py:82
  28.6 4.8 %collective-permute-start.8 = (bf16[128,128]{1,0:T(8,128)(2,1)S(1)}, bf16[128,128]{1,0:T(8,128)(2,1)S(1)}, u32[]{:S(2)}, u32[]{:S(2)}) collective-permute-start(bf16[128,128]{1,0:T(8,128)(2,1)S(1)} %add.16), channel_id=1, source_target_pairs={{0,16},{1,17},{8,24},{9,25},{16,0},{17,1},{24,8},{25,9},{2,18},{3,... | collective-permute-start | bytes 98312 | tf_op jit(solution)/shard_map/ppermute | solution.py:82
  28.6 4.8 %collective-permute-start.7 = (bf16[128,128]{1,0:T(8,128)(2,1)S(1)}, bf16[128,128]{1,0:T(8,128)(2,1)S(1)}, u32[]{:S(2)}, u32[]{:S(2)}) collective-permute-start(bf16[128,128]{1,0:T(8,128)(2,1)S(1)} %add.16), channel_id=1, source_target_pairs={{0,8},{1,9},{8,0},{9,1},{16,24},{17,25},{24,16},{25,17},{2,10},{3,... | collective-permute-start | bytes 98312 | tf_op jit(solution)/shard_map/ppermute | solution.py:82

commit v6 on v5

--- a/solution.py
+++ b/solution.py
@@ -13,7 +13,6 @@
 STEP = 1 * LANES
 VMEM = pl.BlockSpec(memory_space=pltpu.VMEM)
 ANYWHERE = pl.BlockSpec(memory_space=pl.ANY)
-SCALAR = pl.BlockSpec(memory_space=pltpu.SMEM)
 
 
 def in_hbm(value):
@@ -121,12 +120,14 @@
         yield slice(tile * LANES, (tile + 1) * LANES), slice(tile * count, (tile + 1) * count)
 
 
-def send_out(stage_ref, out_ref, sem, c):
+def send_out(stage_ref, out_ref, sem, c, shift):
     if c.stop % STEP == 0 or c.stop == stage_ref.shape[1]:
         begin = (c.stop - 1) // STEP * STEP
         columns = pl.ds(begin, c.stop - begin)
         copy = pltpu.make_async_copy(
-            stage_ref.at[:, columns], out_ref.at[:, columns], sem.at[begin // STEP]
+            stage_ref.at[:, columns],
+            out_ref.at[:, pl.ds(shift + begin, c.stop - begin)],
+            sem.at[begin // STEP],
         )
         copy.start()
         return [copy]
@@ -244,7 +245,8 @@
         window = product(k_ref[:last, c], v_ref[:last, c])
         window = jnp.concatenate([early_ref[:, c], window], axis=0)
         sums = lag_sums(taps, group_width, grad_mix, window)
-        out_ref[rows, :] = sums + inner_ref[rows, :] if there else sums
+        sums = sums + inner_ref[rows, :] if there else sums
+        out_ref[rows, :] = sums.astype(out_ref.dtype)
 
 
 def turned_base(filter_ref):
@@ -264,49 +266,69 @@
 
 
 def mixed_kernel(taps, group_width, k_ref, v_ref, early_ref, filter_ref, inner_ref, *refs):
-    og_refs, (out_ref, stage_ref, sem) = refs[:HALVES], refs[HALVES:]
+    og_refs, out_ref = refs[:HALVES], refs[HALVES]
     blocks = taps // BLOCK
     base = turned_base(filter_ref)
-    copies = []
     for c, rows in tiles(k_ref.shape[1], group_width):
         window = product(k_ref[:taps, c], v_ref[:taps, c])
         window = jnp.concatenate([early_ref[:, c], window], axis=0)
         mixed = convolved(base[rows], window, blocks, taps, group_width)
         og = columns_of(og_refs, c)
-        stage_ref[:taps, c] = (widen(og[:taps]) * mixed).astype(jnp.bfloat16)
-        stage_ref[taps:, c] = (widen(og[taps:]) * inner_ref[:, c]).astype(jnp.bfloat16)
-        copies += send_out(stage_ref, out_ref, sem, c)
-    for copy in copies:
-        copy.wait()
-
-
-def back_kernel(taps, group_width, q_ref, k_ref, v_ref, filter_ref, *refs):
-    og_refs, late_refs, refs = refs[:HALVES], refs[HALVES : 2 * HALVES], refs[2 * HALVES :]
-    kg_ref, vg_ref, k_stage, v_stage, k_sem, v_sem = refs
+        out_ref[:taps, c] = (widen(og[:taps]) * mixed).astype(jnp.bfloat16)
+        out_ref[taps:, c] = (widen(og[taps:]) * inner_ref[:, c]).astype(jnp.bfloat16)
+
+
+def back_columns(taps, group_width, half, q_ref, k_ref, v_ref, filter_ref, og_ref, late_ref):
     blocks = k_ref.shape[0] // BLOCK
     coeffs = widen(filter_ref[...].astype(jnp.bfloat16))
     base = jnp.concatenate([coeffs, jnp.zeros_like(coeffs)], axis=1)
-    copies = []
-    for c, rows in tiles(k_ref.shape[1], group_width):
-        grad_mix = product(columns_of(og_refs, c), q_ref[:, c])
-        window = jnp.concatenate([grad_mix, columns_of(late_refs, c)], axis=0)
+    begin = half * og_ref.shape[1]
+    for own, _ in tiles(og_ref.shape[1], group_width):
+        c = slice(begin + own.start, begin + own.stop)
+        rows = slice(c.start // group_width, c.stop // group_width)
+        window = jnp.concatenate([product(og_ref[:, own], q_ref[:, c]), late_ref[:, own]], axis=0)
         back = convolved(base[rows], window, blocks, taps, group_width)
-        k_stage[:, c] = (back * widen(v_ref[:, c])).astype(jnp.bfloat16)
-        v_stage[:, c] = (back * widen(k_ref[:, c])).astype(jnp.bfloat16)
-        copies += send_out(k_stage, kg_ref, k_sem, c) + send_out(v_stage, vg_ref, v_sem, c)
+        yield own, [(back * widen(ref[:, c])).astype(jnp.bfloat16) for ref in (v_ref, k_ref)]
+
+
+def first_back_kernel(taps, group_width, *refs):
+    inputs, (qg_ref, kg_ref, vg_ref, out_ref, sem) = refs[:6], refs[6:]
+    copy = pltpu.make_async_copy(qg_ref, out_ref, sem)
+    copy.start()
+    for own, (kg, vg) in back_columns(taps, group_width, 0, *inputs):
+        kg_ref[:, own] = kg
+        vg_ref[:, own] = vg
+    copy.wait()
+
+
+def second_back_kernel(taps, group_width, *refs):
+    inputs, refs = refs[:6], refs[6:]
+    kg_first, vg_first, kg_ref, vg_ref, k_stage, v_stage, first_sem, k_sem, v_sem = refs
+    width = kg_first.shape[1]
+    first = pl.ds(0, width)
+    copies = [
+        pltpu.make_async_copy(kg_first, kg_ref.at[:, first], first_sem.at[0]),
+        pltpu.make_async_copy(vg_first, vg_ref.at[:, first], first_sem.at[1]),
+    ]
+    for copy in copies:
+        copy.start()
+    for own, (kg, vg) in back_columns(taps, group_width, 1, *inputs):
+        k_stage[:, own] = kg
+        v_stage[:, own] = vg
+        copies += send_out(k_stage, kg_ref, k_sem, own, width)
+        copies += send_out(v_stage, vg_ref, v_sem, own, width)
     for copy in copies:
         copy.wait()
 
 
-def call(kernel, name, args, outs, staged, cost):
-    steps = -(-outs[0].shape[-1] // STEP)
-    stages = [pltpu.VMEM(o.shape, o.dtype) for o in outs] + [pltpu.SemaphoreType.DMA((steps,)) for _ in outs]
+def call(kernel, name, args, outs, cost, in_hbm_from=None, scratch=()):
+    kept = len(outs) if in_hbm_from is None else in_hbm_from
     return pl.pallas_call(
         kernel,
-        in_specs=[SCALAR if a.dtype == jnp.int32 else VMEM for a in args],
-        out_specs=[ANYWHERE if staged else VMEM for _ in outs],
+        in_specs=[VMEM] * len(args),
+        out_specs=[VMEM] * kept + [ANYWHERE] * (len(outs) - kept),
         out_shape=outs,
-        scratch_shapes=stages if staged else [],
+        scratch_shapes=scratch,
         name=name,
         cost_estimate=pl.CostEstimate(flops=cost, bytes_accessed=1000, transcendentals=0),
         compiler_params=pltpu.CompilerParams(vmem_limit_bytes=LIMIT * 1024 * 1024),
@@ -360,7 +382,7 @@
     near = [own] + near
     inner_rows = jax.ShapeDtypeStruct((rows - taps, channels), jnp.float32)
     (inner,) = call(
-        functools.partial(inner_mixed_kernel, taps, group_width), "inner_causal", (k, v, filters), [inner_rows], False, COST
+        functools.partial(inner_mixed_kernel, taps, group_width), "inner_causal", (k, v, filters), [inner_rows], COST
     )
     grads, heads, inners = [], [], []
     for half in range(HALVES):
@@ -373,7 +395,7 @@
         if height % 16 == 0:
             grad, head = call(
                 functools.partial(gather_kernel, count, half), "gather", (q, *near, *brought_in),
-                [half_wide, half_edge], False, 1000,
+                [half_wide, half_edge], 1000,
             )
         else:
             here = lax.axis_index("tp")
@@ -387,22 +409,31 @@
         heads.append(head)
         if not half:
             (lags,) = call(
-                functools.partial(inner_scores_kernel, taps, group_width, 0), "inner_scores", (q, grad, k, v), [half_small], False, COST
+                functools.partial(inner_scores_kernel, taps, group_width, 0), "inner_scores", (q, grad, k, v), [half_small], COST
             )
             inners.append(lags)
     work = functools.partial
     (lags,) = call(
-        work(scores_kernel, taps, group_width), "edge_scores", (q, *grads, k, v, early, *inners), [small], False, COST
+        work(scores_kernel, taps, group_width), "edge_scores", (q, *grads, k, v, early, *inners), [thin], COST
     )
     lates = [passed_along(head, "ctx", -1) for head in heads]
     (query_grad,) = call(
-        work(mixed_kernel, taps, group_width), "causal", (k, v, early, filters, inner, *grads), [wide], True, COST
+        work(mixed_kernel, taps, group_width), "causal", (k, v, early, filters, inner, *grads), [wide], COST
     )
     lags = [lags] + [brought(lags, step) for step in FIRST]
     lags, query_grad = lax.optimization_barrier((lags, query_grad))
     lags = added(lags, TRAVEL)
+    sides = (q, k, v, filters)
+    kept = jax.ShapeDtypeStruct((rows, width), jnp.bfloat16)
+    key_first, value_first, query_grad = call(
+        work(first_back_kernel, taps, group_width), "adjoint", (*sides, grads[0], lates[0], query_grad),
+        [kept, kept, wide], COST_A, 2, [pltpu.SemaphoreType.DMA],
+    )
+    steps = pltpu.SemaphoreType.DMA((-(-width // STEP),))
     key_grad, value_grad = call(
-        work(back_kernel, taps, group_width), "adjoint", (q, k, v, filters, *grads, *lates), [wide, wide], True, COST
+        work(second_back_kernel, taps, group_width), "adjoint",
+        (*sides, grads[1], lates[1], key_first, value_first), [wide, wide], COST_B, 0,
+        [pltpu.VMEM(kept.shape, kept.dtype)] * 2 + [pltpu.SemaphoreType.DMA((2,)), steps, steps],
     )
     lags = [lags] + [brought(lags, step) for step in SECOND]
     lags, key_grad = lax.optimization_barrier((lags, key_grad))
@@ -413,6 +444,8 @@
 
 
 COST = 100_000_000
+COST_A = 100_000_000
+COST_B = 1000
 HALVES = 2
 NEAR = 2
 TRAVEL = jnp.bfloat16

time: 34.3 us -> 34 us (level)
  Pallas kernels: 11.8 us -> 11.1 us
    ppermute x4, waiting for transfers between devices: 0.4 us -> 1.32 us  [brought(): lax.ppermute(value, axes, [(index, index ^ step) for index in range(count)])]
    pallas_call x7 -> x8, Pallas kernels: 9.24 us -> 8.59 us  [call(): pl.pallas_call(kernel, in_specs=[VMEM] * len(args), out_specs=[VMEM] * ke...]
    ppermute x2, waiting for transfers between devices: 0.64 us -> 0.01 us  [passed_along(): lax.ppermute(value, axis, [(source, source + steps) for source in range(f...]
  transfers between devices with their start and end apart: 12 -> 12, of which waited for: 6 -> 6; matrix products, arithmetic and copies ran while one was open for 0% -> 0% of each run, Pallas kernels for 30% -> 29%
where the time goes in v6:
time: 34 us; the launch traced here: 33.8 us
  starting transfers between devices  15.3 us (45%)
  Pallas kernels  11.1 us (33%)
  waiting for transfers between devices  5.87 us (17%)
  between operations  0.77 us (2%)
  other arithmetic  0.67 us (2%)
    pallas_call x8, Pallas kernels, call(): pl.pallas_call(kernel, in_specs=[VMEM] * len(args), out_specs=[VMEM] * ke...  8.59 us
    ppermute x4, starting transfers between devices, brought(): lax.ppermute(value, axes, [(index, index ^ step) for index in range(count)])  6.04 us
    ppermute x5, starting transfers between devices, exchanged(): return lax.ppermute(part, axis, pairs)  3.56 us
    ppermute x5, waiting for transfers between devices, exchanged(): return lax.ppermute(part, axis, pairs)  3.12 us
    ppermute x1, starting transfers between devices, passed_round(): lax.ppermute(value, axis, [(index, (index + steps) % count) for index in...  3.08 us
    ppermute x2, starting transfers between devices, passed_along(): lax.ppermute(value, axis, [(source, source + steps) for source in range(f...  2.58 us
    pallas_call x1, Pallas kernels, local(): pl.pallas_call(functools.partial(pack_kernel, first_cuts, count, lax.axis...  1.45 us
    ppermute x1, waiting for transfers between devices, passed_round(): lax.ppermute(value, axis, [(index, (index + steps) % count) for index in...  1.43 us
  transfers between devices with their start and end apart: 12, of which 6 were waited for; matrix products, arithmetic and copies ran while one was open for 0% of the time, Pallas kernels for 29%

profile of v6, /device:TPU:0, one launch (start us, length us, event | category | flops | bytes accessed | tf_op | source)
XLA Modules:
  0.0 33.8 jit_solution(9430891124137608646)
XLA Ops:
  0.7 1.4 %pack.1 = (bf16[48,2048]{1,0:T(8,128)(2,1)S(1)}, bf16[48,1024]{1,0:T(8,128)(2,1)S(1)}, bf16[48,1024]{1,0:T(8,128)(2,1)S(1)}, bf16[128,2048]{1,0:T(8,128)(2,1)S(1)}) custom-call(bf16[48,8192]{1,0:T(8,128)(2,1)} %bitcast.27, bf16[192,2048]{1,0:T(8,128)(2,1)} %bitcast.7, bf16[192,2048]{1,0:T(8,128)(2,1)} %bitcast.14), custom_call_target="tpu_custom_call" | custom-call | tf_op jit(solution)/shard_map/pack/pallas_call | solution.py:360
  2.1 0.0 copy-start
  2.1 3.1 %collective-permute-start.6 = (bf16[128,2048]{1,0:T(8,128)(2,1)S(1)}, bf16[128,2048]{1,0:T(8,128)(2,1)S(1)}, u32[]{:S(2)}, u32[]{:S(2)}) collective-permute-start(bf16[128,2048]{1,0:T(8,128)(2,1)S(1)} %get-tuple-element.51), channel_id=1, source_target_pairs={{0,8},{8,16},{16,24},{24,0},{1,9},{9,17},{17,25},{25,1},{2,10},{10... | collective-permute-start | bytes 1572872 | tf_op jit(solution)/shard_map/ppermute | solution.py:38
  5.2 0.0 collective-permute-start
  5.2 1.5 %collective-permute-start.1 = (bf16[48,1024]{1,0:T(8,128)(2,1)S(1)}, bf16[48,1024]{1,0:T(8,128)(2,1)S(1)}, u32[]{:S(2)}, u32[]{:S(2)}) collective-permute-start(bf16[48,1024]{1,0:T(8,128)(2,1)S(1)} %get-tuple-element.40), channel_id=1, source_target_pairs={{0,4},{2,6},{4,0},{6,2},{1,5},{3,7},{5,1},{7,3},{8,12},{10,14},{12... | collective-permute-start | bytes 294920 | tf_op jit(solution)/shard_map/ppermute | solution.py:56
  6.7 0.4 %collective-permute-start.2 = (bf16[48,1024]{1,0:T(8,128)(2,1)S(1)}, bf16[48,1024]{1,0:T(8,128)(2,1)S(1)}, u32[]{:S(2)}, u32[]{:S(2)}) collective-permute-start(bf16[48,1024]{1,0:T(8,128)(2,1)S(1)} %get-tuple-element.41), channel_id=1, source_target_pairs={{0,6},{2,4},{4,2},{6,0},{1,7},{3,5},{5,3},{7,1},{8,14},{10,12},{12... | collective-permute-start | bytes 294920 | tf_op jit(solution)/shard_map/ppermute | solution.py:56
  7.1 0.0 collective-permute-done.refs_1_
  7.1 1.1 %second_pack.1 = (bf16[48,2048]{1,0:T(8,128)(2,1)S(1)}, bf16[48,1024]{1,0:T(8,128)(2,1)S(1)}, bf16[48,1024]{1,0:T(8,128)(2,1)S(1)}) custom-call(bf16[48,8192]{1,0:T(8,128)(2,1)} %bitcast.28), custom_call_target="tpu_custom_call" | custom-call | tf_op jit(solution)/shard_map/second_pack/pallas_call | solution.py:373
  8.1 1.6 %collective-permute-start.4 = (bf16[48,1024]{1,0:T(8,128)(2,1)S(1)}, bf16[48,1024]{1,0:T(8,128)(2,1)S(1)}, u32[]{:S(2)}, u32[]{:S(2)}) collective-permute-start(bf16[48,1024]{1,0:T(8,128)(2,1)S(1)} %get-tuple-element.46), channel_id=1, source_target_pairs={{0,4},{2,6},{4,0},{6,2},{1,5},{3,7},{5,1},{7,3},{8,12},{10,14},{12... | collective-permute-start | bytes 294920 | tf_op jit(solution)/shard_map/ppermute | solution.py:56
  9.7 0.1 collective-permute-start.5
  9.8 1.1 %inner_causal.1.inner_ref = f32[64,2048]{1,0:T(8,128)S(1)} custom-call(bf16[192,2048]{1,0:T(8,128)(2,1)S(1)} %bitcast.8, bf16[192,2048]{1,0:T(8,128)(2,1)S(1)} %bitcast.15, f32[128,128]{1,0:T(8,128)S(1)} %copy-done.3), custom_call_target="tpu_custom_call" | custom-call | flops 100000000 | bytes 1000 | tf_op jit(solution)/shard_map/inner_causal/pallas_call | solution.py:326
  10.9 1.2 %collective-permute-done.2.refs_3_ = bf16[48,1024]{1,0:T(8,128)(2,1)S(1)} collective-permute-done((bf16[48,1024]{1,0:T(8,128)(2,1)S(1)}, bf16[48,1024]{1,0:T(8,128)(2,1)S(1)}, u32[]{:S(2)}, u32[]{:S(2)}) %collective-permute-start.2) | collective-permute-done | bytes 98336 | tf_op jit(solution)/shard_map/ppermute | solution.py:56
  12.1 0.1 gather.2
  12.3 1.3 %collective-permute-start.3 = (bf16[128,1024]{1,0:T(8,128)(2,1)S(1)}, bf16[128,1024]{1,0:T(8,128)(2,1)S(1)}, u32[]{:S(2)}, u32[]{:S(2)}) collective-permute-start(bf16[128,1024]{1,0:T(8,128)(2,1)S(1)} %get-tuple-element.45), channel_id=1, source_target_pairs={{8,0},{16,8},{24,16},{9,1},{17,9},{25,17},{10,2},{18,10},{26,18},{... | collective-permute-start | bytes 786440 | tf_op jit(solution)/shard_map/ppermute | solution.py:33
  13.6 0.8 %inner_scores.1.refs_5_ = f32[64,128]{1,0:T(8,128)S(1)} custom-call(bf16[192,2048]{1,0:T(8,128)(2,1)S(1)} %bitcast.22, bf16[192,1024]{1,0:T(8,128)(2,1)S(1)} %get-tuple-element.44.og_ref.refs_0_.refs_4_, bf16[192,2048]{1,0:T(8,128)(2,1)S(1)} %bitcast.9, bf16[192,2048]{1,0:T(8,128)(2,1)S(1)} %bitcast.16), custom_call_target="tpu_custom_call" | custom-call | flops 100000000 | bytes 1000 | tf_op jit(solution)/shard_map/inner_scores/pallas_call | solution.py:326
  14.4 0.6 %collective-permute-done.4.refs_2_ = bf16[48,1024]{1,0:T(8,128)(2,1)S(1)} collective-permute-done((bf16[48,1024]{1,0:T(8,128)(2,1)S(1)}, bf16[48,1024]{1,0:T(8,128)(2,1)S(1)}, u32[]{:S(2)}, u32[]{:S(2)}) %collective-permute-start.4) | collective-permute-done | bytes 98336 | tf_op jit(solution)/shard_map/ppermute | solution.py:56
  15.0 1.3 %collective-permute-done.5.refs_3_ = bf16[48,1024]{1,0:T(8,128)(2,1)S(1)} collective-permute-done((bf16[48,1024]{1,0:T(8,128)(2,1)S(1)}, bf16[48,1024]{1,0:T(8,128)(2,1)S(1)}, u32[]{:S(2)}, u32[]{:S(2)}) %collective-permute-start.5) | collective-permute-done | bytes 98336 | tf_op jit(solution)/shard_map/ppermute | solution.py:56
  16.3 0.1 gather.3
  16.5 1.3 %collective-permute-start.11 = (bf16[128,1024]{1,0:T(8,128)(2,1)S(1)}, bf16[128,1024]{1,0:T(8,128)(2,1)S(1)}, u32[]{:S(2)}, u32[]{:S(2)}) collective-permute-start(bf16[128,1024]{1,0:T(8,128)(2,1)S(1)} %get-tuple-element.58), channel_id=1, source_target_pairs={{8,0},{16,8},{24,16},{9,1},{17,9},{25,17},{10,2},{18,10},{26,18},{... | collective-permute-start | bytes 786440 | tf_op jit(solution)/shard_map/ppermute | solution.py:33
  17.8 1.4 %collective-permute-done.6.refs_4_.early_ref = bf16[128,2048]{1,0:T(8,128)(2,1)S(1)} collective-permute-done((bf16[128,2048]{1,0:T(8,128)(2,1)S(1)}, bf16[128,2048]{1,0:T(8,128)(2,1)S(1)}, u32[]{:S(2)}, u32[]{:S(2)}) %collective-permute-start.6) | collective-permute-done | bytes 524320 | tf_op jit(solution)/shard_map/ppermute | solution.py:38
  19.2 1.7 %edge_scores.1.refs_0_ = bf16[128,128]{1,0:T(8,128)(2,1)S(1)} custom-call(bf16[192,2048]{1,0:T(8,128)(2,1)S(1)} %bitcast.24, bf16[192,1024]{1,0:T(8,128)(2,1)S(1)} %get-tuple-element.44.og_ref.refs_0_.refs_4_, bf16[192,1024]{1,0:T(8,128)(2,1)S(1)} %get-tuple-element.50.refs_1_.refs_4_, bf16[192,2048]{1,0:T(8,128)(2,1)S(1)} %bitcast.10, ...), custom_call_target="tpu_custom_call" | custom-call | flops 100000000 | bytes 1000 | tf_op jit(solution)/shard_map/edge_scores/pallas_call | solution.py:326
  20.9 1.6 %collective-permute-start.7 = (bf16[128,128]{1,0:T(8,128)(2,1)S(1)}, bf16[128,128]{1,0:T(8,128)(2,1)S(1)}, u32[]{:S(2)}, u32[]{:S(2)}) collective-permute-start(bf16[128,128]{1,0:T(8,128)(2,1)S(1)} %edge_scores.1.refs_0_), channel_id=1, source_target_pairs={{0,1},{1,0},{8,9},{9,8},{16,17},{17,16},{24,25},{25,24},{2,3},{3,2... | collective-permute-start | bytes 98312 | tf_op jit(solution)/shard_map/ppermute | solution.py:81
  22.5 1.6 %causal.1.refs_6_ = bf16[192,2048]{1,0:T(8,128)(2,1)S(1)} custom-call(bf16[192,2048]{1,0:T(8,128)(2,1)S(1)} %bitcast.11, bf16[192,2048]{1,0:T(8,128)(2,1)S(1)} %bitcast.18, bf16[128,2048]{1,0:T(8,128)(2,1)S(1)} %collective-permute-done.6.refs_4_.early_ref, f32[128,128]{1,0:T(8,128)S(1)} %copy-done.3, f32[64,2048]{1,0:T(8,128)S(1)} %inner_causal.1.inner_ref, ...), custom_call_target="tpu_custom_call" | custom-call | flops 100000000 | bytes 1000 | tf_op jit(solution)/shard_map/causal/pallas_call | solution.py:326
  24.2 0.7 %collective-permute-done.7.refs_1_ = bf16[128,128]{1,0:T(8,128)(2,1)S(1)} collective-permute-done((bf16[128,128]{1,0:T(8,128)(2,1)S(1)}, bf16[128,128]{1,0:T(8,128)(2,1)S(1)}, u32[]{:S(2)}, u32[]{:S(2)}) %collective-permute-start.7) | collective-permute-done | bytes 32800 | tf_op jit(solution)/shard_map/ppermute | solution.py:81
  24.9 3.3 %collective-permute-start.10 = (bf16[128,128]{1,0:T(8,128)(2,1)S(1)}, bf16[128,128]{1,0:T(8,128)(2,1)S(1)}, u32[]{:S(2)}, u32[]{:S(2)}) collective-permute-start(bf16[128,128]{1,0:T(8,128)(2,1)S(1)} %add.16), channel_id=1, source_target_pairs={{0,24},{1,25},{8,16},{9,17},{16,8},{17,9},{24,0},{25,1},{2,26},{3,... | collective-permute-start | bytes 98312 | tf_op jit(solution)/shard_map/ppermute | solution.py:81
  28.2 1.1 %collective-permute-start.9 = (bf16[128,128]{1,0:T(8,128)(2,1)S(1)}, bf16[128,128]{1,0:T(8,128)(2,1)S(1)}, u32[]{:S(2)}, u32[]{:S(2)}) collective-permute-start(bf16[128,128]{1,0:T(8,128)(2,1)S(1)} %add.16), channel_id=1, source_target_pairs={{0,16},{1,17},{8,24},{9,25},{16,0},{17,1},{24,8},{25,9},{2,18},{3,... | collective-permute-start | bytes 98312 | tf_op jit(solution)/shard_map/ppermute | solution.py:81
  29.4 1.1 %adjoint.2 = (bf16[192,1024]{1,0:T(8,128)(2,1)S(1)}, bf16[192,1024]{1,0:T(8,128)(2,1)S(1)}, bf16[192,2048]{1,0:T(8,128)(2,1)}) custom-call(bf16[192,2048]{1,0:T(8,128)(2,1)S(1)} %bitcast.25, bf16[192,2048]{1,0:T(8,128)(2,1)S(1)} %bitcast.12, bf16[192,2048]{1,0:T(8,128)(2,1)S(1)} %bitcast.19, f32[128,128]{1,0:T(8,128)S(1)} %copy-done.3, ...), custom_call_target="tpu_custom_call" | custom-call | flops 100000000 | bytes 1000 | tf_op jit(solution)/shard_map/adjoint/pallas_call | solution.py:326
  30.5 1.9 %adjoint.3 = (bf16[192,2048]{1,0:T(8,128)(2,1)}, bf16[192,2048]{1,0:T(8,128)(2,1)}) custom-call(bf16[192,2048]{1,0:T(8,128)(2,1)S(1)} %bitcast.26, bf16[192,2048]{1,0:T(8,128)(2,1)S(1)} %bitcast.13, bf16[192,2048]{1,0:T(8,128)(2,1)S(1)} %bitcast.20, f32[128,128]{1,0:T(8,128)S(1)} %copy-done.3, bf16[192,1024]{1,0:T(8,128)(2,1)S(1)} %get-tuple-element.50.refs_1_.refs_4_, ...), custom_call_target="tpu_custom_call" | custom-call | flops 1000 | bytes 1000 | tf_op jit(solution)/shard_map/adjoint/pallas_call | solution.py:326
  32.4 0.0 collective-permute-done.8
  32.5 0.6 %collective-permute-done.9 = bf16[128,128]{1,0:T(8,128)(2,1)S(1)} collective-permute-done((bf16[128,128]{1,0:T(8,128)(2,1)S(1)}, bf16[128,128]{1,0:T(8,128)(2,1)S(1)}, u32[]{:S(2)}, u32[]{:S(2)}) %collective-permute-start.9) | collective-permute-done | bytes 32800 | tf_op jit(solution)/shard_map/ppermute | solution.py:81
  33.0 0.1 rev.4
  33.1 0.6 %broadcast_multiply_fusion = f32[128,128]{1,0:T(8,128)} fusion(f32[128,128]{1,0:T(8,128)S(1)} %rev.4), kind=kLoop, calls=%fused_computation.1 | loop fusion | flops 16384 | bytes 131072 | tf_op jit(solution)/shard_map/mul | solution.py:443
  (14 shorter events, 0.1 us)
Async XLA Ops:
  0.6 9.2 %copy-start.1 = (bf16[1,192,2048]{2,1,0:T(8,128)(2,1)S(1)}, bf16[1,192,2048]{2,1,0:T(8,128)(2,1)}, u32[]{:S(2)}) copy-start(bf16[1,192,2048]{2,1,0:T(8,128)(2,1)} %param.7) | copy-start | bytes 2359300
  0.6 9.2 %copy-start.3 = (f32[128,128]{1,0:T(8,128)S(1)}, f32[128,128]{1,0:T(8,128)}, u32[]{:S(2)}) copy-start(f32[128,128]{1,0:T(8,128)} %refs_3_.3) | copy-start | bytes 196612
  2.1 7.7 %copy-start = (bf16[1,192,2048]{2,1,0:T(8,128)(2,1)S(1)}, bf16[1,192,2048]{2,1,0:T(8,128)(2,1)}, u32[]{:S(2)}) copy-start(bf16[1,192,2048]{2,1,0:T(8,128)(2,1)} %param.6) | copy-start | bytes 2359300
  2.1 17.1 %collective-permute-start.6 = (bf16[128,2048]{1,0:T(8,128)(2,1)S(1)}, bf16[128,2048]{1,0:T(8,128)(2,1)S(1)}, u32[]{:S(2)}, u32[]{:S(2)}) collective-permute-start(bf16[128,2048]{1,0:T(8,128)(2,1)S(1)} %get-tuple-element.51), channel_id=1, source_target_pairs={{0,8},{8,16},{16,24},{24,0},{1,9},{9,17},{17,25},{25,1},{2,10},{10... | collective-permute-start | bytes 1572872 | tf_op jit(solution)/shard_map/ppermute | solution.py:38
  5.2 1.9 %collective-permute-start = (bf16[48,2048]{1,0:T(8,128)(2,1)S(1)}, bf16[48,2048]{1,0:T(8,128)(2,1)S(1)}, u32[]{:S(2)}, u32[]{:S(2)}) collective-permute-start(bf16[48,2048]{1,0:T(8,128)(2,1)S(1)} %get-tuple-element.36), channel_id=1, source_target_pairs={{0,2},{2,0},{4,6},{6,4},{1,3},{3,1},{5,7},{7,5},{8,10},{10,8},{12,... | collective-permute-start | bytes 589832 | tf_op jit(solution)/shard_map/ppermute | solution.py:56
  5.2 5.7 %collective-permute-start.1 = (bf16[48,1024]{1,0:T(8,128)(2,1)S(1)}, bf16[48,1024]{1,0:T(8,128)(2,1)S(1)}, u32[]{:S(2)}, u32[]{:S(2)}) collective-permute-start(bf16[48,1024]{1,0:T(8,128)(2,1)S(1)} %get-tuple-element.40), channel_id=1, source_target_pairs={{0,4},{2,6},{4,0},{6,2},{1,5},{3,7},{5,1},{7,3},{8,12},{10,14},{12... | collective-permute-start | bytes 294920 | tf_op jit(solution)/shard_map/ppermute | solution.py:56
  6.7 5.4 %collective-permute-start.2 = (bf16[48,1024]{1,0:T(8,128)(2,1)S(1)}, bf16[48,1024]{1,0:T(8,128)(2,1)S(1)}, u32[]{:S(2)}, u32[]{:S(2)}) collective-permute-start(bf16[48,1024]{1,0:T(8,128)(2,1)S(1)} %get-tuple-element.41), channel_id=1, source_target_pairs={{0,6},{2,4},{4,2},{6,0},{1,7},{3,5},{5,3},{7,1},{8,14},{10,12},{12... | collective-permute-start | bytes 294920 | tf_op jit(solution)/shard_map/ppermute | solution.py:56
  8.1 6.9 %collective-permute-start.4 = (bf16[48,1024]{1,0:T(8,128)(2,1)S(1)}, bf16[48,1024]{1,0:T(8,128)(2,1)S(1)}, u32[]{:S(2)}, u32[]{:S(2)}) collective-permute-start(bf16[48,1024]{1,0:T(8,128)(2,1)S(1)} %get-tuple-element.46), channel_id=1, source_target_pairs={{0,4},{2,6},{4,0},{6,2},{1,5},{3,7},{5,1},{7,3},{8,12},{10,14},{12... | collective-permute-start | bytes 294920 | tf_op jit(solution)/shard_map/ppermute | solution.py:56
  9.7 2.4 %copy-start.2 = (bf16[1,192,2048]{2,1,0:T(8,128)(2,1)S(1)}, bf16[1,192,2048]{2,1,0:T(8,128)(2,1)}, u32[]{:S(2)}) copy-start(bf16[1,192,2048]{2,1,0:T(8,128)(2,1)} %param.5) | copy-start | bytes 2359300
  9.7 6.6 %collective-permute-start.5 = (bf16[48,1024]{1,0:T(8,128)(2,1)S(1)}, bf16[48,1024]{1,0:T(8,128)(2,1)S(1)}, u32[]{:S(2)}, u32[]{:S(2)}) collective-permute-start(bf16[48,1024]{1,0:T(8,128)(2,1)S(1)} %get-tuple-element.47), channel_id=1, source_target_pairs={{0,6},{2,4},{4,2},{6,0},{1,7},{3,5},{5,3},{7,1},{8,14},{10,12},{12... | collective-permute-start | bytes 294920 | tf_op jit(solution)/shard_map/ppermute | solution.py:56
  12.3 17.1 %collective-permute-start.3 = (bf16[128,1024]{1,0:T(8,128)(2,1)S(1)}, bf16[128,1024]{1,0:T(8,128)(2,1)S(1)}, u32[]{:S(2)}, u32[]{:S(2)}) collective-permute-start(bf16[128,1024]{1,0:T(8,128)(2,1)S(1)} %get-tuple-element.45), channel_id=1, source_target_pairs={{8,0},{16,8},{24,16},{9,1},{17,9},{25,17},{10,2},{18,10},{26,18},{... | collective-permute-start | bytes 786440 | tf_op jit(solution)/shard_map/ppermute | solution.py:33
  16.5 14.0 %collective-permute-start.11 = (bf16[128,1024]{1,0:T(8,128)(2,1)S(1)}, bf16[128,1024]{1,0:T(8,128)(2,1)S(1)}, u32[]{:S(2)}, u32[]{:S(2)}) collective-permute-start(bf16[128,1024]{1,0:T(8,128)(2,1)S(1)} %get-tuple-element.58), channel_id=1, source_target_pairs={{8,0},{16,8},{24,16},{9,1},{17,9},{25,17},{10,2},{18,10},{26,18},{... | collective-permute-start | bytes 786440 | tf_op jit(solution)/shard_map/ppermute | solution.py:33
  20.9 4.0 %collective-permute-start.7 = (bf16[128,128]{1,0:T(8,128)(2,1)S(1)}, bf16[128,128]{1,0:T(8,128)(2,1)S(1)}, u32[]{:S(2)}, u32[]{:S(2)}) collective-permute-start(bf16[128,128]{1,0:T(8,128)(2,1)S(1)} %edge_scores.1.refs_0_), channel_id=1, source_target_pairs={{0,1},{1,0},{8,9},{9,8},{16,17},{17,16},{24,25},{25,24},{2,3},{3,2... | collective-permute-start | bytes 98312 | tf_op jit(solution)/shard_map/ppermute | solution.py:81
  24.9 7.5 %collective-permute-start.10 = (bf16[128,128]{1,0:T(8,128)(2,1)S(1)}, bf16[128,128]{1,0:T(8,128)(2,1)S(1)}, u32[]{:S(2)}, u32[]{:S(2)}) collective-permute-start(bf16[128,128]{1,0:T(8,128)(2,1)S(1)} %add.16), channel_id=1, source_target_pairs={{0,24},{1,25},{8,16},{9,17},{16,8},{17,9},{24,0},{25,1},{2,26},{3,... | collective-permute-start | bytes 98312 | tf_op jit(solution)/shard_map/ppermute | solution.py:81
  28.2 4.2 %collective-permute-start.8 = (bf16[128,128]{1,0:T(8,128)(2,1)S(1)}, bf16[128,128]{1,0:T(8,128)(2,1)S(1)}, u32[]{:S(2)}, u32[]{:S(2)}) collective-permute-start(bf16[128,128]{1,0:T(8,128)(2,1)S(1)} %add.16), channel_id=1, source_target_pairs={{0,8},{1,9},{8,0},{9,1},{16,24},{17,25},{24,16},{25,17},{2,10},{3,... | collective-permute-start | bytes 98312 | tf_op jit(solution)/shard_map/ppermute | solution.py:81
  28.2 4.8 %collective-permute-start.9 = (bf16[128,128]{1,0:T(8,128)(2,1)S(1)}, bf16[128,128]{1,0:T(8,128)(2,1)S(1)}, u32[]{:S(2)}, u32[]{:S(2)}) collective-permute-start(bf16[128,128]{1,0:T(8,128)(2,1)S(1)} %add.16), channel_id=1, source_target_pairs={{0,16},{1,17},{8,24},{9,25},{16,0},{17,1},{24,8},{25,9},{2,18},{3,... | collective-permute-start | bytes 98312 | tf_op jit(solution)/shard_map/ppermute | solution.py:81

commit v7 on v6

--- a/solution.py
+++ b/solution.py
@@ -79,6 +79,43 @@
     axes = ("ctx", "dp")
     count = lax.axis_size("ctx") * lax.axis_size("dp")
     return lax.ppermute(value, axes, [(index, index ^ step) for index in range(count)])
+
+
+def rounds_of_sum():
+    rounds, base = [], 1
+    for size in (lax.axis_size("dp"), lax.axis_size("ctx")):
+        if size & (size - 1):
+            return None
+        while size > 1:
+            width = 4 if size % 4 == 0 else 2
+            rounds.append([base * step for step in range(1, width)])
+            base *= width
+            size //= width
+    return rounds
+
+
+def first_rounds(value, after):
+    rounds = rounds_of_sum()
+    if rounds is None:
+        return lax.psum(widen(value), ("dp", "ctx")), after
+    for n, steps in enumerate(rounds[:-1]):
+        parts = [value] + [brought(value, step) for step in steps]
+        if n == 0:
+            parts, after = lax.optimization_barrier((parts, after))
+        value = added(parts, TRAVEL if n == len(rounds) - 2 else jnp.float32)
+    return value, after
+
+
+def last_round(value, after):
+    rounds = rounds_of_sum()
+    if not rounds:
+        return widen(value), after
+    parts = [value] + [brought(value, step) for step in rounds[-1]]
+    parts, after = lax.optimization_barrier((parts, after))
+    parts = [widen(part) for part in parts]
+    while len(parts) > 1:
+        parts = [parts[m] + parts[m + 1] for m in range(0, len(parts), 2)]
+    return parts[0], after
 
 
 def windows(rows, blocks, height):
@@ -414,15 +451,13 @@
             inners.append(lags)
     work = functools.partial
     (lags,) = call(
-        work(scores_kernel, taps, group_width), "edge_scores", (q, *grads, k, v, early, *inners), [thin], COST
+        work(scores_kernel, taps, group_width), "edge_scores", (q, *grads, k, v, early, *inners), [small], COST
     )
     lates = [passed_along(head, "ctx", -1) for head in heads]
     (query_grad,) = call(
         work(mixed_kernel, taps, group_width), "causal", (k, v, early, filters, inner, *grads), [wide], COST
     )
-    lags = [lags] + [brought(lags, step) for step in FIRST]
-    lags, query_grad = lax.optimization_barrier((lags, query_grad))
-    lags = added(lags, TRAVEL)
+    lags, query_grad = first_rounds(lags, query_grad)
     sides = (q, k, v, filters)
     kept = jax.ShapeDtypeStruct((rows, width), jnp.bfloat16)
     key_first, value_first, query_grad = call(
@@ -435,10 +470,7 @@
         (*sides, grads[1], lates[1], key_first, value_first), [wide, wide], COST_B, 0,
         [pltpu.VMEM(kept.shape, kept.dtype)] * 2 + [pltpu.SemaphoreType.DMA((2,)), steps, steps],
     )
-    lags = [lags] + [brought(lags, step) for step in SECOND]
-    lags, key_grad = lax.optimization_barrier((lags, key_grad))
-    lags = [widen(part) for part in lags]
-    lags = (lags[0] + lags[1]) + (lags[2] + lags[3])
+    lags, key_grad = last_round(lags, key_grad)
     scale = 1.0 / math.sqrt(lax.axis_size("dp") * lax.axis_size("ctx") * rows * group_width)
     return (query_grad[None], key_grad[None], value_grad[None], jnp.flip(lags, 1) * scale)
 
@@ -449,8 +481,6 @@
 HALVES = 2
 NEAR = 2
 TRAVEL = jnp.bfloat16
-FIRST = (1,)
-SECOND = (2, 4, 6)
 LIMIT = 8
 
 

time: 34 us -> 34.3 us (level)
  waiting for transfers between devices: 5.87 us -> 6.23 us
    ppermute x4, waiting for transfers between devices: 1.32 us -> 1.67 us  [brought(): lax.ppermute(value, axes, [(index, index ^ step) for index in range(count)])]
  transfers between devices with their start and end apart: 12 -> 12, of which waited for: 6 -> 6; matrix products, arithmetic and copies ran while one was open for 0% -> 0% of each run, Pallas kernels for 29% -> 28%
where the time goes in v7:
time: 34.3 us; the launch traced here: 34.1 us
  starting transfers between devices  15.3 us (45%)
  Pallas kernels  11.1 us (32%)
  waiting for transfers between devices  6.23 us (18%)
  between operations  0.77 us (2%)
  other arithmetic  0.67 us (2%)
    pallas_call x8, Pallas kernels, call(): pl.pallas_call(kernel, in_specs=[VMEM] * len(args), out_specs=[VMEM] * ke...  8.59 us
    ppermute x4, starting transfers between devices, brought(): lax.ppermute(value, axes, [(index, index ^ step) for index in range(count)])  6.04 us
    ppermute x5, starting transfers between devices, exchanged(): return lax.ppermute(part, axis, pairs)  3.56 us
    ppermute x5, waiting for transfers between devices, exchanged(): return lax.ppermute(part, axis, pairs)  3.12 us
    ppermute x1, starting transfers between devices, passed_round(): lax.ppermute(value, axis, [(index, (index + steps) % count) for index in...  3.08 us
    ppermute x2, starting transfers between devices, passed_along(): lax.ppermute(value, axis, [(source, source + steps) for source in range(f...  2.58 us
    ppermute x4, waiting for transfers between devices, brought(): lax.ppermute(value, axes, [(index, index ^ step) for index in range(count)])  1.67 us
    pallas_call x1, Pallas kernels, local(): pl.pallas_call(functools.partial(pack_kernel, first_cuts, count, lax.axis...  1.45 us
  transfers between devices with their start and end apart: 12, of which 6 were waited for; matrix products, arithmetic and copies ran while one was open for 0% of the time, Pallas kernels for 28%

profile of v7, /device:TPU:0, one launch (start us, length us, event | category | flops | bytes accessed | tf_op | source)
XLA Modules:
  0.0 34.1 jit_solution(11784962100899673018)
XLA Ops:
  0.7 1.4 %pack.1 = (bf16[48,2048]{1,0:T(8,128)(2,1)S(1)}, bf16[48,1024]{1,0:T(8,128)(2,1)S(1)}, bf16[48,1024]{1,0:T(8,128)(2,1)S(1)}, bf16[128,2048]{1,0:T(8,128)(2,1)S(1)}) custom-call(bf16[48,8192]{1,0:T(8,128)(2,1)} %bitcast.27, bf16[192,2048]{1,0:T(8,128)(2,1)} %bitcast.7, bf16[192,2048]{1,0:T(8,128)(2,1)} %bitcast.14), custom_call_target="tpu_custom_call" | custom-call | tf_op jit(solution)/shard_map/pack/pallas_call | solution.py:397
  2.1 0.0 copy-start
  2.1 3.1 %collective-permute-start.6 = (bf16[128,2048]{1,0:T(8,128)(2,1)S(1)}, bf16[128,2048]{1,0:T(8,128)(2,1)S(1)}, u32[]{:S(2)}, u32[]{:S(2)}) collective-permute-start(bf16[128,2048]{1,0:T(8,128)(2,1)S(1)} %get-tuple-element.51), channel_id=1, source_target_pairs={{0,8},{8,16},{16,24},{24,0},{1,9},{9,17},{17,25},{25,1},{2,10},{10... | collective-permute-start | bytes 1572872 | tf_op jit(solution)/shard_map/ppermute | solution.py:38
  5.2 1.5 %collective-permute-start.1 = (bf16[48,1024]{1,0:T(8,128)(2,1)S(1)}, bf16[48,1024]{1,0:T(8,128)(2,1)S(1)}, u32[]{:S(2)}, u32[]{:S(2)}) collective-permute-start(bf16[48,1024]{1,0:T(8,128)(2,1)S(1)} %get-tuple-element.40), channel_id=1, source_target_pairs={{0,4},{2,6},{4,0},{6,2},{1,5},{3,7},{5,1},{7,3},{8,12},{10,14},{12... | collective-permute-start | bytes 294920 | tf_op jit(solution)/shard_map/ppermute | solution.py:56
  6.7 0.4 %collective-permute-start.2 = (bf16[48,1024]{1,0:T(8,128)(2,1)S(1)}, bf16[48,1024]{1,0:T(8,128)(2,1)S(1)}, u32[]{:S(2)}, u32[]{:S(2)}) collective-permute-start(bf16[48,1024]{1,0:T(8,128)(2,1)S(1)} %get-tuple-element.41), channel_id=1, source_target_pairs={{0,6},{2,4},{4,2},{6,0},{1,7},{3,5},{5,3},{7,1},{8,14},{10,12},{12... | collective-permute-start | bytes 294920 | tf_op jit(solution)/shard_map/ppermute | solution.py:56
  7.1 0.0 collective-permute-done.refs_1_
  7.1 1.1 %second_pack.1 = (bf16[48,2048]{1,0:T(8,128)(2,1)S(1)}, bf16[48,1024]{1,0:T(8,128)(2,1)S(1)}, bf16[48,1024]{1,0:T(8,128)(2,1)S(1)}) custom-call(bf16[48,8192]{1,0:T(8,128)(2,1)} %bitcast.28), custom_call_target="tpu_custom_call" | custom-call | tf_op jit(solution)/shard_map/second_pack/pallas_call | solution.py:410
  8.1 1.6 %collective-permute-start.4 = (bf16[48,1024]{1,0:T(8,128)(2,1)S(1)}, bf16[48,1024]{1,0:T(8,128)(2,1)S(1)}, u32[]{:S(2)}, u32[]{:S(2)}) collective-permute-start(bf16[48,1024]{1,0:T(8,128)(2,1)S(1)} %get-tuple-element.46), channel_id=1, source_target_pairs={{0,4},{2,6},{4,0},{6,2},{1,5},{3,7},{5,1},{7,3},{8,12},{10,14},{12... | collective-permute-start | bytes 294920 | tf_op jit(solution)/shard_map/ppermute | solution.py:56
  9.7 0.1 collective-permute-start.5
  9.8 1.1 %inner_causal.1.inner_ref = f32[64,2048]{1,0:T(8,128)S(1)} custom-call(bf16[192,2048]{1,0:T(8,128)(2,1)S(1)} %bitcast.8, bf16[192,2048]{1,0:T(8,128)(2,1)S(1)} %bitcast.15, f32[128,128]{1,0:T(8,128)S(1)} %copy-done.3), custom_call_target="tpu_custom_call" | custom-call | flops 100000000 | bytes 1000 | tf_op jit(solution)/shard_map/inner_causal/pallas_call | solution.py:363
  10.9 0.0 collective-permute-done.1.refs_2_
  10.9 1.2 %collective-permute-done.2.refs_3_ = bf16[48,1024]{1,0:T(8,128)(2,1)S(1)} collective-permute-done((bf16[48,1024]{1,0:T(8,128)(2,1)S(1)}, bf16[48,1024]{1,0:T(8,128)(2,1)S(1)}, u32[]{:S(2)}, u32[]{:S(2)}) %collective-permute-start.2) | collective-permute-done | bytes 98336 | tf_op jit(solution)/shard_map/ppermute | solution.py:56
  12.1 0.1 gather.2
  12.3 1.3 %collective-permute-start.3 = (bf16[128,1024]{1,0:T(8,128)(2,1)S(1)}, bf16[128,1024]{1,0:T(8,128)(2,1)S(1)}, u32[]{:S(2)}, u32[]{:S(2)}) collective-permute-start(bf16[128,1024]{1,0:T(8,128)(2,1)S(1)} %get-tuple-element.45), channel_id=1, source_target_pairs={{8,0},{16,8},{24,16},{9,1},{17,9},{25,17},{10,2},{18,10},{26,18},{... | collective-permute-start | bytes 786440 | tf_op jit(solution)/shard_map/ppermute | solution.py:33
  13.6 0.8 %inner_scores.1.refs_5_ = f32[64,128]{1,0:T(8,128)S(1)} custom-call(bf16[192,2048]{1,0:T(8,128)(2,1)S(1)} %bitcast.22, bf16[192,1024]{1,0:T(8,128)(2,1)S(1)} %get-tuple-element.44.og_ref.refs_0_.refs_4_, bf16[192,2048]{1,0:T(8,128)(2,1)S(1)} %bitcast.9, bf16[192,2048]{1,0:T(8,128)(2,1)S(1)} %bitcast.16), custom_call_target="tpu_custom_call" | custom-call | flops 100000000 | bytes 1000 | tf_op jit(solution)/shard_map/inner_scores/pallas_call | solution.py:363
  14.4 0.6 %collective-permute-done.4.refs_2_ = bf16[48,1024]{1,0:T(8,128)(2,1)S(1)} collective-permute-done((bf16[48,1024]{1,0:T(8,128)(2,1)S(1)}, bf16[48,1024]{1,0:T(8,128)(2,1)S(1)}, u32[]{:S(2)}, u32[]{:S(2)}) %collective-permute-start.4) | collective-permute-done | bytes 98336 | tf_op jit(solution)/shard_map/ppermute | solution.py:56
  15.0 1.3 %collective-permute-done.5.refs_3_ = bf16[48,1024]{1,0:T(8,128)(2,1)S(1)} collective-permute-done((bf16[48,1024]{1,0:T(8,128)(2,1)S(1)}, bf16[48,1024]{1,0:T(8,128)(2,1)S(1)}, u32[]{:S(2)}, u32[]{:S(2)}) %collective-permute-start.5) | collective-permute-done | bytes 98336 | tf_op jit(solution)/shard_map/ppermute | solution.py:56
  16.3 0.1 gather.3
  16.5 1.3 %collective-permute-start.11 = (bf16[128,1024]{1,0:T(8,128)(2,1)S(1)}, bf16[128,1024]{1,0:T(8,128)(2,1)S(1)}, u32[]{:S(2)}, u32[]{:S(2)}) collective-permute-start(bf16[128,1024]{1,0:T(8,128)(2,1)S(1)} %get-tuple-element.58), channel_id=1, source_target_pairs={{8,0},{16,8},{24,16},{9,1},{17,9},{25,17},{10,2},{18,10},{26,18},{... | collective-permute-start | bytes 786440 | tf_op jit(solution)/shard_map/ppermute | solution.py:33
  17.8 1.4 %collective-permute-done.6.refs_4_.early_ref = bf16[128,2048]{1,0:T(8,128)(2,1)S(1)} collective-permute-done((bf16[128,2048]{1,0:T(8,128)(2,1)S(1)}, bf16[128,2048]{1,0:T(8,128)(2,1)S(1)}, u32[]{:S(2)}, u32[]{:S(2)}) %collective-permute-start.6) | collective-permute-done | bytes 524320 | tf_op jit(solution)/shard_map/ppermute | solution.py:38
  19.2 1.7 %edge_scores.1.refs_0_ = f32[128,128]{1,0:T(8,128)S(1)} custom-call(bf16[192,2048]{1,0:T(8,128)(2,1)S(1)} %bitcast.24, bf16[192,1024]{1,0:T(8,128)(2,1)S(1)} %get-tuple-element.44.og_ref.refs_0_.refs_4_, bf16[192,1024]{1,0:T(8,128)(2,1)S(1)} %get-tuple-element.50.refs_1_.refs_4_, bf16[192,2048]{1,0:T(8,128)(2,1)S(1)} %bitcast.10, ...), custom_call_target="tpu_custom_call" | custom-call | flops 100000000 | bytes 1000 | tf_op jit(solution)/shard_map/edge_scores/pallas_call | solution.py:363
  20.9 1.6 %collective-permute-start.7 = (f32[128,128]{1,0:T(8,128)S(1)}, f32[128,128]{1,0:T(8,128)S(1)}, u32[]{:S(2)}, u32[]{:S(2)}) collective-permute-start(f32[128,128]{1,0:T(8,128)S(1)} %edge_scores.1.refs_0_), channel_id=1, source_target_pairs={{0,1},{1,0},{8,9},{9,8},{16,17},{17,16},{24,25},{25,24},{2,3},{3,2... | collective-permute-start | bytes 196616 | tf_op jit(solution)/shard_map/ppermute | solution.py:81
  22.5 1.6 %causal.1.refs_6_ = bf16[192,2048]{1,0:T(8,128)(2,1)S(1)} custom-call(bf16[192,2048]{1,0:T(8,128)(2,1)S(1)} %bitcast.11, bf16[192,2048]{1,0:T(8,128)(2,1)S(1)} %bitcast.18, bf16[128,2048]{1,0:T(8,128)(2,1)S(1)} %collective-permute-done.6.refs_4_.early_ref, f32[128,128]{1,0:T(8,128)S(1)} %copy-done.3, f32[64,2048]{1,0:T(8,128)S(1)} %inner_causal.1.inner_ref, ...), custom_call_target="tpu_custom_call" | custom-call | flops 100000000 | bytes 1000 | tf_op jit(solution)/shard_map/causal/pallas_call | solution.py:363
  24.1 1.1 %collective-permute-done.7.refs_1_ = f32[128,128]{1,0:T(8,128)S(1)} collective-permute-done((f32[128,128]{1,0:T(8,128)S(1)}, f32[128,128]{1,0:T(8,128)S(1)}, u32[]{:S(2)}, u32[]{:S(2)}) %collective-permute-start.7) | collective-permute-done | bytes 65568 | tf_op jit(solution)/shard_map/ppermute | solution.py:81
  25.3 3.3 %collective-permute-start.10 = (bf16[128,128]{1,0:T(8,128)(2,1)S(1)}, bf16[128,128]{1,0:T(8,128)(2,1)S(1)}, u32[]{:S(2)}, u32[]{:S(2)}) collective-permute-start(bf16[128,128]{1,0:T(8,128)(2,1)S(1)} %add.16), channel_id=1, source_target_pairs={{0,24},{1,25},{8,16},{9,17},{16,8},{17,9},{24,0},{25,1},{2,26},{3,... | collective-permute-start | bytes 98312 | tf_op jit(solution)/shard_map/ppermute | solution.py:81
  28.6 0.0 collective-permute-start.9
  28.6 1.1 %collective-permute-start.8 = (bf16[128,128]{1,0:T(8,128)(2,1)S(1)}, bf16[128,128]{1,0:T(8,128)(2,1)S(1)}, u32[]{:S(2)}, u32[]{:S(2)}) collective-permute-start(bf16[128,128]{1,0:T(8,128)(2,1)S(1)} %add.16), channel_id=1, source_target_pairs={{0,8},{1,9},{8,0},{9,1},{16,24},{17,25},{24,16},{25,17},{2,10},{3,... | collective-permute-start | bytes 98312 | tf_op jit(solution)/shard_map/ppermute | solution.py:81
  29.7 1.1 %adjoint.2 = (bf16[192,1024]{1,0:T(8,128)(2,1)S(1)}, bf16[192,1024]{1,0:T(8,128)(2,1)S(1)}, bf16[192,2048]{1,0:T(8,128)(2,1)}) custom-call(bf16[192,2048]{1,0:T(8,128)(2,1)S(1)} %bitcast.25, bf16[192,2048]{1,0:T(8,128)(2,1)S(1)} %bitcast.12, bf16[192,2048]{1,0:T(8,128)(2,1)S(1)} %bitcast.19, f32[128,128]{1,0:T(8,128)S(1)} %copy-done.3, ...), custom_call_target="tpu_custom_call" | custom-call | flops 100000000 | bytes 1000 | tf_op jit(solution)/shard_map/adjoint/pallas_call | solution.py:363
  30.9 1.9 %adjoint.3 = (bf16[192,2048]{1,0:T(8,128)(2,1)}, bf16[192,2048]{1,0:T(8,128)(2,1)}) custom-call(bf16[192,2048]{1,0:T(8,128)(2,1)S(1)} %bitcast.26, bf16[192,2048]{1,0:T(8,128)(2,1)S(1)} %bitcast.13, bf16[192,2048]{1,0:T(8,128)(2,1)S(1)} %bitcast.20, f32[128,128]{1,0:T(8,128)S(1)} %copy-done.3, bf16[192,1024]{1,0:T(8,128)(2,1)S(1)} %get-tuple-element.50.refs_1_.refs_4_, ...), custom_call_target="tpu_custom_call" | custom-call | flops 1000 | bytes 1000 | tf_op jit(solution)/shard_map/adjoint/pallas_call | solution.py:363
  32.8 0.6 %collective-permute-done.9 = bf16[128,128]{1,0:T(8,128)(2,1)S(1)} collective-permute-done((bf16[128,128]{1,0:T(8,128)(2,1)S(1)}, bf16[128,128]{1,0:T(8,128)(2,1)S(1)}, u32[]{:S(2)}, u32[]{:S(2)}) %collective-permute-start.9) | collective-permute-done | bytes 32800 | tf_op jit(solution)/shard_map/ppermute | solution.py:81
  33.4 0.1 rev.4
  33.5 0.6 %broadcast_multiply_fusion = f32[128,128]{1,0:T(8,128)} fusion(f32[128,128]{1,0:T(8,128)S(1)} %rev.4), kind=kLoop, calls=%fused_computation.1 | loop fusion | flops 16384 | bytes 131072 | tf_op jit(solution)/shard_map/mul | solution.py:475
  (14 shorter events, 0.1 us)
Async XLA Ops:
  0.6 9.2 %copy-start.1 = (bf16[1,192,2048]{2,1,0:T(8,128)(2,1)S(1)}, bf16[1,192,2048]{2,1,0:T(8,128)(2,1)}, u32[]{:S(2)}) copy-start(bf16[1,192,2048]{2,1,0:T(8,128)(2,1)} %param.7) | copy-start | bytes 2359300
  0.6 9.2 %copy-start.3 = (f32[128,128]{1,0:T(8,128)S(1)}, f32[128,128]{1,0:T(8,128)}, u32[]{:S(2)}) copy-start(f32[128,128]{1,0:T(8,128)} %refs_3_.3) | copy-start | bytes 196612
  2.1 7.7 %copy-start = (bf16[1,192,2048]{2,1,0:T(8,128)(2,1)S(1)}, bf16[1,192,2048]{2,1,0:T(8,128)(2,1)}, u32[]{:S(2)}) copy-start(bf16[1,192,2048]{2,1,0:T(8,128)(2,1)} %param.6) | copy-start | bytes 2359300
  2.1 17.1 %collective-permute-start.6 = (bf16[128,2048]{1,0:T(8,128)(2,1)S(1)}, bf16[128,2048]{1,0:T(8,128)(2,1)S(1)}, u32[]{:S(2)}, u32[]{:S(2)}) collective-permute-start(bf16[128,2048]{1,0:T(8,128)(2,1)S(1)} %get-tuple-element.51), channel_id=1, source_target_pairs={{0,8},{8,16},{16,24},{24,0},{1,9},{9,17},{17,25},{25,1},{2,10},{10... | collective-permute-start | bytes 1572872 | tf_op jit(solution)/shard_map/ppermute | solution.py:38
  5.2 1.9 %collective-permute-start = (bf16[48,2048]{1,0:T(8,128)(2,1)S(1)}, bf16[48,2048]{1,0:T(8,128)(2,1)S(1)}, u32[]{:S(2)}, u32[]{:S(2)}) collective-permute-start(bf16[48,2048]{1,0:T(8,128)(2,1)S(1)} %get-tuple-element.36), channel_id=1, source_target_pairs={{0,2},{2,0},{4,6},{6,4},{1,3},{3,1},{5,7},{7,5},{8,10},{10,8},{12,... | collective-permute-start | bytes 589832 | tf_op jit(solution)/shard_map/ppermute | solution.py:56
  5.2 5.7 %collective-permute-start.1 = (bf16[48,1024]{1,0:T(8,128)(2,1)S(1)}, bf16[48,1024]{1,0:T(8,128)(2,1)S(1)}, u32[]{:S(2)}, u32[]{:S(2)}) collective-permute-start(bf16[48,1024]{1,0:T(8,128)(2,1)S(1)} %get-tuple-element.40), channel_id=1, source_target_pairs={{0,4},{2,6},{4,0},{6,2},{1,5},{3,7},{5,1},{7,3},{8,12},{10,14},{12... | collective-permute-start | bytes 294920 | tf_op jit(solution)/shard_map/ppermute | solution.py:56
  6.7 5.4 %collective-permute-start.2 = (bf16[48,1024]{1,0:T(8,128)(2,1)S(1)}, bf16[48,1024]{1,0:T(8,128)(2,1)S(1)}, u32[]{:S(2)}, u32[]{:S(2)}) collective-permute-start(bf16[48,1024]{1,0:T(8,128)(2,1)S(1)} %get-tuple-element.41), channel_id=1, source_target_pairs={{0,6},{2,4},{4,2},{6,0},{1,7},{3,5},{5,3},{7,1},{8,14},{10,12},{12... | collective-permute-start | bytes 294920 | tf_op jit(solution)/shard_map/ppermute | solution.py:56
  8.1 6.9 %collective-permute-start.4 = (bf16[48,1024]{1,0:T(8,128)(2,1)S(1)}, bf16[48,1024]{1,0:T(8,128)(2,1)S(1)}, u32[]{:S(2)}, u32[]{:S(2)}) collective-permute-start(bf16[48,1024]{1,0:T(8,128)(2,1)S(1)} %get-tuple-element.46), channel_id=1, source_target_pairs={{0,4},{2,6},{4,0},{6,2},{1,5},{3,7},{5,1},{7,3},{8,12},{10,14},{12... | collective-permute-start | bytes 294920 | tf_op jit(solution)/shard_map/ppermute | solution.py:56
  9.7 2.4 %copy-start.2 = (bf16[1,192,2048]{2,1,0:T(8,128)(2,1)S(1)}, bf16[1,192,2048]{2,1,0:T(8,128)(2,1)}, u32[]{:S(2)}) copy-start(bf16[1,192,2048]{2,1,0:T(8,128)(2,1)} %param.5) | copy-start | bytes 2359300
  9.7 6.6 %collective-permute-start.5 = (bf16[48,1024]{1,0:T(8,128)(2,1)S(1)}, bf16[48,1024]{1,0:T(8,128)(2,1)S(1)}, u32[]{:S(2)}, u32[]{:S(2)}) collective-permute-start(bf16[48,1024]{1,0:T(8,128)(2,1)S(1)} %get-tuple-element.47), channel_id=1, source_target_pairs={{0,6},{2,4},{4,2},{6,0},{1,7},{3,5},{5,3},{7,1},{8,14},{10,12},{12... | collective-permute-start | bytes 294920 | tf_op jit(solution)/shard_map/ppermute | solution.py:56
  12.3 17.4 %collective-permute-start.3 = (bf16[128,1024]{1,0:T(8,128)(2,1)S(1)}, bf16[128,1024]{1,0:T(8,128)(2,1)S(1)}, u32[]{:S(2)}, u32[]{:S(2)}) collective-permute-start(bf16[128,1024]{1,0:T(8,128)(2,1)S(1)} %get-tuple-element.45), channel_id=1, source_target_pairs={{8,0},{16,8},{24,16},{9,1},{17,9},{25,17},{10,2},{18,10},{26,18},{... | collective-permute-start | bytes 786440 | tf_op jit(solution)/shard_map/ppermute | solution.py:33
  16.5 14.4 %collective-permute-start.11 = (bf16[128,1024]{1,0:T(8,128)(2,1)S(1)}, bf16[128,1024]{1,0:T(8,128)(2,1)S(1)}, u32[]{:S(2)}, u32[]{:S(2)}) collective-permute-start(bf16[128,1024]{1,0:T(8,128)(2,1)S(1)} %get-tuple-element.58), channel_id=1, source_target_pairs={{8,0},{16,8},{24,16},{9,1},{17,9},{25,17},{10,2},{18,10},{26,18},{... | collective-permute-start | bytes 786440 | tf_op jit(solution)/shard_map/ppermute | solution.py:33
  20.9 4.3 %collective-permute-start.7 = (f32[128,128]{1,0:T(8,128)S(1)}, f32[128,128]{1,0:T(8,128)S(1)}, u32[]{:S(2)}, u32[]{:S(2)}) collective-permute-start(f32[128,128]{1,0:T(8,128)S(1)} %edge_scores.1.refs_0_), channel_id=1, source_target_pairs={{0,1},{1,0},{8,9},{9,8},{16,17},{17,16},{24,25},{25,24},{2,3},{3,2... | collective-permute-start | bytes 196616 | tf_op jit(solution)/shard_map/ppermute | solution.py:81
  25.3 7.5 %collective-permute-start.10 = (bf16[128,128]{1,0:T(8,128)(2,1)S(1)}, bf16[128,128]{1,0:T(8,128)(2,1)S(1)}, u32[]{:S(2)}, u32[]{:S(2)}) collective-permute-start(bf16[128,128]{1,0:T(8,128)(2,1)S(1)} %add.16), channel_id=1, source_target_pairs={{0,24},{1,25},{8,16},{9,17},{16,8},{17,9},{24,0},{25,1},{2,26},{3,... | collective-permute-start | bytes 98312 | tf_op jit(solution)/shard_map/ppermute | solution.py:81
  28.6 4.8 %collective-permute-start.9 = (bf16[128,128]{1,0:T(8,128)(2,1)S(1)}, bf16[128,128]{1,0:T(8,128)(2,1)S(1)}, u32[]{:S(2)}, u32[]{:S(2)}) collective-permute-start(bf16[128,128]{1,0:T(8,128)(2,1)S(1)} %add.16), channel_id=1, source_target_pairs={{0,16},{1,17},{8,24},{9,25},{16,0},{17,1},{24,8},{25,9},{2,18},{3,... | collective-permute-start | bytes 98312 | tf_op jit(solution)/shard_map/ppermute | solution.py:81
  28.6 4.8 %collective-permute-start.8 = (bf16[128,128]{1,0:T(8,128)(2,1)S(1)}, bf16[128,128]{1,0:T(8,128)(2,1)S(1)}, u32[]{:S(2)}, u32[]{:S(2)}) collective-permute-start(bf16[128,128]{1,0:T(8,128)(2,1)S(1)} %add.16), channel_id=1, source_target_pairs={{0,8},{1,9},{8,0},{9,1},{16,24},{17,25},{24,16},{25,17},{2,10},{3,... | collective-permute-start | bytes 98312 | tf_op jit(solution)/shard_map/ppermute | solution.py:81

commit v8 on v7

--- a/solution.py
+++ b/solution.py
@@ -157,14 +157,12 @@
         yield slice(tile * LANES, (tile + 1) * LANES), slice(tile * count, (tile + 1) * count)
 
 
-def send_out(stage_ref, out_ref, sem, c, shift):
+def send_out(stage_ref, out_ref, sem, c, below, right):
     if c.stop % STEP == 0 or c.stop == stage_ref.shape[1]:
         begin = (c.stop - 1) // STEP * STEP
-        columns = pl.ds(begin, c.stop - begin)
+        place = (pl.ds(below, stage_ref.shape[0]), pl.ds(right + begin, c.stop - begin))
         copy = pltpu.make_async_copy(
-            stage_ref.at[:, columns],
-            out_ref.at[:, pl.ds(shift + begin, c.stop - begin)],
-            sem.at[begin // STEP],
+            stage_ref.at[:, pl.ds(begin, c.stop - begin)], out_ref.at[place], sem.at[begin // STEP]
         )
         copy.start()
         return [copy]
@@ -315,45 +313,55 @@
         out_ref[taps:, c] = (widen(og[taps:]) * inner_ref[:, c]).astype(jnp.bfloat16)
 
 
-def back_columns(taps, group_width, half, q_ref, k_ref, v_ref, filter_ref, og_ref, late_ref):
-    blocks = k_ref.shape[0] // BLOCK
+def back_columns(taps, group_width, half, rows, q_ref, k_ref, v_ref, filter_ref, og_ref, late_ref):
+    blocks = (rows.stop - rows.start) // BLOCK
     coeffs = widen(filter_ref[...].astype(jnp.bfloat16))
     base = jnp.concatenate([coeffs, jnp.zeros_like(coeffs)], axis=1)
     begin = half * og_ref.shape[1]
+    last = min(rows.stop + taps, og_ref.shape[0])
     for own, _ in tiles(og_ref.shape[1], group_width):
         c = slice(begin + own.start, begin + own.stop)
-        rows = slice(c.start // group_width, c.stop // group_width)
-        window = jnp.concatenate([product(og_ref[:, own], q_ref[:, c]), late_ref[:, own]], axis=0)
-        back = convolved(base[rows], window, blocks, taps, group_width)
-        yield own, [(back * widen(ref[:, c])).astype(jnp.bfloat16) for ref in (v_ref, k_ref)]
+        groups = slice(c.start // group_width, c.stop // group_width)
+        window = product(og_ref[rows.start : last, own], q_ref[rows.start : last, c])
+        if last < rows.stop + taps:
+            window = jnp.concatenate([window, late_ref[:, own]], axis=0)
+        back = convolved(base[groups], window, blocks, taps, group_width)
+        yield own, [(back * widen(ref[rows, c])).astype(jnp.bfloat16) for ref in (v_ref, k_ref)]
 
 
 def first_back_kernel(taps, group_width, *refs):
-    inputs, (qg_ref, kg_ref, vg_ref, out_ref, sem) = refs[:6], refs[6:]
+    sides, (og_ref, other_ref, late_ref, qg_ref), refs = refs[:4], refs[4:8], refs[8:]
+    kg_ref, vg_ref, kg_top, vg_top, out_ref, sem = refs
     copy = pltpu.make_async_copy(qg_ref, out_ref, sem)
     copy.start()
-    for own, (kg, vg) in back_columns(taps, group_width, 0, *inputs):
+    height = og_ref.shape[0]
+    for own, (kg, vg) in back_columns(taps, group_width, 0, slice(0, height), *sides, og_ref, late_ref):
         kg_ref[:, own] = kg
         vg_ref[:, own] = vg
+    above = slice(0, kg_top.shape[0])
+    for own, (kg, vg) in back_columns(taps, group_width, 1, above, *sides, other_ref, None):
+        kg_top[:, own] = kg
+        vg_top[:, own] = vg
     copy.wait()
 
 
 def second_back_kernel(taps, group_width, *refs):
-    inputs, refs = refs[:6], refs[6:]
-    kg_first, vg_first, kg_ref, vg_ref, k_stage, v_stage, first_sem, k_sem, v_sem = refs
-    width = kg_first.shape[1]
-    first = pl.ds(0, width)
-    copies = [
-        pltpu.make_async_copy(kg_first, kg_ref.at[:, first], first_sem.at[0]),
-        pltpu.make_async_copy(vg_first, vg_ref.at[:, first], first_sem.at[1]),
-    ]
+    inputs, done_refs, refs = refs[:6], refs[6:10], refs[10:]
+    kg_ref, vg_ref, k_stage, v_stage, first_sem, k_sem, v_sem = refs
+    width = done_refs[0].shape[1]
+    height = done_refs[2].shape[0]
+    copies = []
+    for n, (done_ref, out_ref) in enumerate(zip(done_refs, (kg_ref, vg_ref, kg_ref, vg_ref))):
+        place = (pl.ds(0, done_ref.shape[0]), pl.ds(0 if n < 2 else width, done_ref.shape[1]))
+        copies.append(pltpu.make_async_copy(done_ref, out_ref.at[place], first_sem.at[n]))
     for copy in copies:
         copy.start()
-    for own, (kg, vg) in back_columns(taps, group_width, 1, *inputs):
+    rows = slice(height, kg_ref.shape[0])
+    for own, (kg, vg) in back_columns(taps, group_width, 1, rows, *inputs):
         k_stage[:, own] = kg
         v_stage[:, own] = vg
-        copies += send_out(k_stage, kg_ref, k_sem, own, width)
-        copies += send_out(v_stage, vg_ref, v_sem, own, width)
+        copies += send_out(k_stage, kg_ref, k_sem, own, height, width)
+        copies += send_out(v_stage, vg_ref, v_sem, own, height, width)
     for copy in copies:
         copy.wait()
 
@@ -451,7 +459,7 @@
             inners.append(lags)
     work = functools.partial
     (lags,) = call(
-        work(scores_kernel, taps, group_width), "edge_scores", (q, *grads, k, v, early, *inners), [small], COST
+        work(scores_kernel, taps, group_width), "edge_scores", (q, *grads, k, v, early, *inners), [thin], COST
     )
     lates = [passed_along(head, "ctx", -1) for head in heads]
     (query_grad,) = call(
@@ -459,16 +467,18 @@
     )
     lags, query_grad = first_rounds(lags, query_grad)
     sides = (q, k, v, filters)
-    kept = jax.ShapeDtypeStruct((rows, width), jnp.bfloat16)
-    key_first, value_first, query_grad = call(
-        work(first_back_kernel, taps, group_width), "adjoint", (*sides, grads[0], lates[0], query_grad),
-        [kept, kept, wide], COST_A, 2, [pltpu.SemaphoreType.DMA],
+    kept, above, rest = [
+        jax.ShapeDtypeStruct((size, width), jnp.bfloat16) for size in (rows, rows - taps, taps)
+    ]
+    *done, query_grad = call(
+        work(first_back_kernel, taps, group_width), "adjoint", (*sides, *grads, lates[0], query_grad),
+        [kept, kept, above, above, wide], COST_A, 4, [pltpu.SemaphoreType.DMA],
     )
     steps = pltpu.SemaphoreType.DMA((-(-width // STEP),))
     key_grad, value_grad = call(
         work(second_back_kernel, taps, group_width), "adjoint",
-        (*sides, grads[1], lates[1], key_first, value_first), [wide, wide], COST_B, 0,
-        [pltpu.VMEM(kept.shape, kept.dtype)] * 2 + [pltpu.SemaphoreType.DMA((2,)), steps, steps],
+        (*sides, grads[1], lates[1], *done), [wide, wide], COST_B, 0,
+        [pltpu.VMEM(rest.shape, rest.dtype)] * 2 + [pltpu.SemaphoreType.DMA((4,)), steps, steps],
     )
     lags, key_grad = last_round(lags, key_grad)
     scale = 1.0 / math.sqrt(lax.axis_size("dp") * lax.axis_size("ctx") * rows * group_width)
@@ -476,7 +486,7 @@
 
 
 COST = 100_000_000
-COST_A = 100_000_000
+COST_A = 1_000_000_000
 COST_B = 1000
 HALVES = 2
 NEAR = 2

time: 34.3 us -> 34 us (level)
  waiting for transfers between devices: 6.23 us -> 5.76 us
    ppermute x4, waiting for transfers between devices: 1.67 us -> 1.2 us  [brought(): lax.ppermute(value, axes, [(index, index ^ step) for index in range(count)])]
  transfers between devices with their start and end apart: 12 -> 12, of which waited for: 6 -> 6; matrix products, arithmetic and copies ran while one was open for 0% -> 0% of each run, Pallas kernels for 28% -> 29%
where the time goes in v8:
time: 34 us; the launch traced here: 33.8 us
  starting transfers between devices  15.3 us (45%)
  Pallas kernels  11.2 us (33%)
  waiting for transfers between devices  5.76 us (17%)
  between operations  0.78 us (2%)
  other arithmetic  0.67 us (2%)
    pallas_call x8, Pallas kernels, call(): pl.pallas_call(kernel, in_specs=[VMEM] * len(args), out_specs=[VMEM] * ke...  8.7 us
    ppermute x4, starting transfers between devices, brought(): lax.ppermute(value, axes, [(index, index ^ step) for index in range(count)])  6.04 us
    ppermute x5, starting transfers between devices, exchanged(): return lax.ppermute(part, axis, pairs)  3.56 us
    ppermute x5, waiting for transfers between devices, exchanged(): return lax.ppermute(part, axis, pairs)  3.12 us
    ppermute x1, starting transfers between devices, passed_round(): lax.ppermute(value, axis, [(index, (index + steps) % count) for index in...  3.08 us
    ppermute x2, starting transfers between devices, passed_along(): lax.ppermute(value, axis, [(source, source + steps) for source in range(f...  2.58 us
    pallas_call x1, Pallas kernels, local(): pl.pallas_call(functools.partial(pack_kernel, first_cuts, count, lax.axis...  1.45 us
    ppermute x1, waiting for transfers between devices, passed_round(): lax.ppermute(value, axis, [(index, (index + steps) % count) for index in...  1.43 us
  transfers between devices with their start and end apart: 12, of which 6 were waited for; matrix products, arithmetic and copies ran while one was open for 0% of the time, Pallas kernels for 29%

profile of v8, /device:TPU:0, one launch (start us, length us, event | category | flops | bytes accessed | tf_op | source)
XLA Modules:
  0.0 33.8 jit_solution(17170810838783251675)
XLA Ops:
  0.7 1.4 %pack.1 = (bf16[48,2048]{1,0:T(8,128)(2,1)S(1)}, bf16[48,1024]{1,0:T(8,128)(2,1)S(1)}, bf16[48,1024]{1,0:T(8,128)(2,1)S(1)}, bf16[128,2048]{1,0:T(8,128)(2,1)S(1)}) custom-call(bf16[48,8192]{1,0:T(8,128)(2,1)} %bitcast.27, bf16[192,2048]{1,0:T(8,128)(2,1)} %bitcast.7, bf16[192,2048]{1,0:T(8,128)(2,1)} %bitcast.14), custom_call_target="tpu_custom_call" | custom-call | tf_op jit(solution)/shard_map/pack/pallas_call | solution.py:405
  2.1 0.0 copy-start
  2.1 3.1 %collective-permute-start.6 = (bf16[128,2048]{1,0:T(8,128)(2,1)S(1)}, bf16[128,2048]{1,0:T(8,128)(2,1)S(1)}, u32[]{:S(2)}, u32[]{:S(2)}) collective-permute-start(bf16[128,2048]{1,0:T(8,128)(2,1)S(1)} %get-tuple-element.53), channel_id=1, source_target_pairs={{0,8},{8,16},{16,24},{24,0},{1,9},{9,17},{17,25},{25,1},{2,10},{10... | collective-permute-start | bytes 1572872 | tf_op jit(solution)/shard_map/ppermute | solution.py:38
  5.2 0.0 collective-permute-start
  5.2 1.5 %collective-permute-start.1 = (bf16[48,1024]{1,0:T(8,128)(2,1)S(1)}, bf16[48,1024]{1,0:T(8,128)(2,1)S(1)}, u32[]{:S(2)}, u32[]{:S(2)}) collective-permute-start(bf16[48,1024]{1,0:T(8,128)(2,1)S(1)} %get-tuple-element.42), channel_id=1, source_target_pairs={{0,4},{2,6},{4,0},{6,2},{1,5},{3,7},{5,1},{7,3},{8,12},{10,14},{12... | collective-permute-start | bytes 294920 | tf_op jit(solution)/shard_map/ppermute | solution.py:56
  6.7 0.4 %collective-permute-start.2 = (bf16[48,1024]{1,0:T(8,128)(2,1)S(1)}, bf16[48,1024]{1,0:T(8,128)(2,1)S(1)}, u32[]{:S(2)}, u32[]{:S(2)}) collective-permute-start(bf16[48,1024]{1,0:T(8,128)(2,1)S(1)} %get-tuple-element.43), channel_id=1, source_target_pairs={{0,6},{2,4},{4,2},{6,0},{1,7},{3,5},{5,3},{7,1},{8,14},{10,12},{12... | collective-permute-start | bytes 294920 | tf_op jit(solution)/shard_map/ppermute | solution.py:56
  7.1 0.0 collective-permute-done.refs_1_
  7.1 1.1 %second_pack.1 = (bf16[48,2048]{1,0:T(8,128)(2,1)S(1)}, bf16[48,1024]{1,0:T(8,128)(2,1)S(1)}, bf16[48,1024]{1,0:T(8,128)(2,1)S(1)}) custom-call(bf16[48,8192]{1,0:T(8,128)(2,1)} %bitcast.28), custom_call_target="tpu_custom_call" | custom-call | tf_op jit(solution)/shard_map/second_pack/pallas_call | solution.py:418
  8.1 1.6 %collective-permute-start.3 = (bf16[48,1024]{1,0:T(8,128)(2,1)S(1)}, bf16[48,1024]{1,0:T(8,128)(2,1)S(1)}, u32[]{:S(2)}, u32[]{:S(2)}) collective-permute-start(bf16[48,1024]{1,0:T(8,128)(2,1)S(1)} %get-tuple-element.47), channel_id=1, source_target_pairs={{0,4},{2,6},{4,0},{6,2},{1,5},{3,7},{5,1},{7,3},{8,12},{10,14},{12... | collective-permute-start | bytes 294920 | tf_op jit(solution)/shard_map/ppermute | solution.py:56
  9.7 0.1 collective-permute-start.4
  9.8 1.1 %inner_causal.1.inner_ref = f32[64,2048]{1,0:T(8,128)S(1)} custom-call(bf16[192,2048]{1,0:T(8,128)(2,1)S(1)} %bitcast.8, bf16[192,2048]{1,0:T(8,128)(2,1)S(1)} %bitcast.15, f32[128,128]{1,0:T(8,128)S(1)} %copy-done.3), custom_call_target="tpu_custom_call" | custom-call | flops 100000000 | bytes 1000 | tf_op jit(solution)/shard_map/inner_causal/pallas_call | solution.py:371
  10.9 1.2 %collective-permute-done.2.refs_3_ = bf16[48,1024]{1,0:T(8,128)(2,1)S(1)} collective-permute-done((bf16[48,1024]{1,0:T(8,128)(2,1)S(1)}, bf16[48,1024]{1,0:T(8,128)(2,1)S(1)}, u32[]{:S(2)}, u32[]{:S(2)}) %collective-permute-start.2) | collective-permute-done | bytes 98336 | tf_op jit(solution)/shard_map/ppermute | solution.py:56
  12.1 0.1 gather.2
  12.3 1.3 %collective-permute-start.5 = (bf16[128,1024]{1,0:T(8,128)(2,1)S(1)}, bf16[128,1024]{1,0:T(8,128)(2,1)S(1)}, u32[]{:S(2)}, u32[]{:S(2)}) collective-permute-start(bf16[128,1024]{1,0:T(8,128)(2,1)S(1)} %get-tuple-element.52), channel_id=1, source_target_pairs={{8,0},{16,8},{24,16},{9,1},{17,9},{25,17},{10,2},{18,10},{26,18},{... | collective-permute-start | bytes 786440 | tf_op jit(solution)/shard_map/ppermute | solution.py:33
  13.6 0.8 %inner_scores.1.refs_5_ = f32[64,128]{1,0:T(8,128)S(1)} custom-call(bf16[192,2048]{1,0:T(8,128)(2,1)S(1)} %bitcast.22, bf16[192,1024]{1,0:T(8,128)(2,1)S(1)} %get-tuple-element.46.og_ref.refs_0_.refs_4_, bf16[192,2048]{1,0:T(8,128)(2,1)S(1)} %bitcast.9, bf16[192,2048]{1,0:T(8,128)(2,1)S(1)} %bitcast.16), custom_call_target="tpu_custom_call" | custom-call | flops 100000000 | bytes 1000 | tf_op jit(solution)/shard_map/inner_scores/pallas_call | solution.py:371
  14.4 0.6 %collective-permute-done.3.refs_2_ = bf16[48,1024]{1,0:T(8,128)(2,1)S(1)} collective-permute-done((bf16[48,1024]{1,0:T(8,128)(2,1)S(1)}, bf16[48,1024]{1,0:T(8,128)(2,1)S(1)}, u32[]{:S(2)}, u32[]{:S(2)}) %collective-permute-start.3) | collective-permute-done | bytes 98336 | tf_op jit(solution)/shard_map/ppermute | solution.py:56
  15.0 1.3 %collective-permute-done.4.refs_3_ = bf16[48,1024]{1,0:T(8,128)(2,1)S(1)} collective-permute-done((bf16[48,1024]{1,0:T(8,128)(2,1)S(1)}, bf16[48,1024]{1,0:T(8,128)(2,1)S(1)}, u32[]{:S(2)}, u32[]{:S(2)}) %collective-permute-start.4) | collective-permute-done | bytes 98336 | tf_op jit(solution)/shard_map/ppermute | solution.py:56
  16.3 0.1 gather.3
  16.5 1.3 %collective-permute-start.11 = (bf16[128,1024]{1,0:T(8,128)(2,1)S(1)}, bf16[128,1024]{1,0:T(8,128)(2,1)S(1)}, u32[]{:S(2)}, u32[]{:S(2)}) collective-permute-start(bf16[128,1024]{1,0:T(8,128)(2,1)S(1)} %get-tuple-element.60), channel_id=1, source_target_pairs={{8,0},{16,8},{24,16},{9,1},{17,9},{25,17},{10,2},{18,10},{26,18},{... | collective-permute-start | bytes 786440 | tf_op jit(solution)/shard_map/ppermute | solution.py:33
  17.8 1.4 %collective-permute-done.6.refs_4_.early_ref = bf16[128,2048]{1,0:T(8,128)(2,1)S(1)} collective-permute-done((bf16[128,2048]{1,0:T(8,128)(2,1)S(1)}, bf16[128,2048]{1,0:T(8,128)(2,1)S(1)}, u32[]{:S(2)}, u32[]{:S(2)}) %collective-permute-start.6) | collective-permute-done | bytes 524320 | tf_op jit(solution)/shard_map/ppermute | solution.py:38
  19.2 1.7 %edge_scores.1.refs_0_ = bf16[128,128]{1,0:T(8,128)(2,1)S(1)} custom-call(bf16[192,2048]{1,0:T(8,128)(2,1)S(1)} %bitcast.24, bf16[192,1024]{1,0:T(8,128)(2,1)S(1)} %get-tuple-element.46.og_ref.refs_0_.refs_4_, bf16[192,1024]{1,0:T(8,128)(2,1)S(1)} %get-tuple-element.51.refs_1_.refs_5_.refs_4_, bf16[192,2048]{1,0:T(8,128)(2,1)S(1)} %bitcast.10, ...), custom_call_target="tpu_custom_call" | custom-call | flops 100000000 | bytes 1000 | tf_op jit(solution)/shard_map/edge_scores/pallas_call | solution.py:371
  20.9 1.6 %collective-permute-start.7 = (bf16[128,128]{1,0:T(8,128)(2,1)S(1)}, bf16[128,128]{1,0:T(8,128)(2,1)S(1)}, u32[]{:S(2)}, u32[]{:S(2)}) collective-permute-start(bf16[128,128]{1,0:T(8,128)(2,1)S(1)} %edge_scores.1.refs_0_), channel_id=1, source_target_pairs={{0,1},{1,0},{8,9},{9,8},{16,17},{17,16},{24,25},{25,24},{2,3},{3,2... | collective-permute-start | bytes 98312 | tf_op jit(solution)/shard_map/ppermute | solution.py:81
  22.5 1.6 %causal.1.refs_7_ = bf16[192,2048]{1,0:T(8,128)(2,1)S(1)} custom-call(bf16[192,2048]{1,0:T(8,128)(2,1)S(1)} %bitcast.11, bf16[192,2048]{1,0:T(8,128)(2,1)S(1)} %bitcast.18, bf16[128,2048]{1,0:T(8,128)(2,1)S(1)} %collective-permute-done.6.refs_4_.early_ref, f32[128,128]{1,0:T(8,128)S(1)} %copy-done.3, f32[64,2048]{1,0:T(8,128)S(1)} %inner_causal.1.inner_ref, ...), custom_call_target="tpu_custom_call" | custom-call | flops 100000000 | bytes 1000 | tf_op jit(solution)/shard_map/causal/pallas_call | solution.py:371
  24.2 0.7 %collective-permute-done.7.refs_1_ = bf16[128,128]{1,0:T(8,128)(2,1)S(1)} collective-permute-done((bf16[128,128]{1,0:T(8,128)(2,1)S(1)}, bf16[128,128]{1,0:T(8,128)(2,1)S(1)}, u32[]{:S(2)}, u32[]{:S(2)}) %collective-permute-start.7) | collective-permute-done | bytes 32800 | tf_op jit(solution)/shard_map/ppermute | solution.py:81
  24.9 3.3 %collective-permute-start.10 = (bf16[128,128]{1,0:T(8,128)(2,1)S(1)}, bf16[128,128]{1,0:T(8,128)(2,1)S(1)}, u32[]{:S(2)}, u32[]{:S(2)}) collective-permute-start(bf16[128,128]{1,0:T(8,128)(2,1)S(1)} %add.16), channel_id=1, source_target_pairs={{0,24},{1,25},{8,16},{9,17},{16,8},{17,9},{24,0},{25,1},{2,26},{3,... | collective-permute-start | bytes 98312 | tf_op jit(solution)/shard_map/ppermute | solution.py:81
  28.2 0.0 collective-permute-start.8
  28.2 1.1 %collective-permute-start.9 = (bf16[128,128]{1,0:T(8,128)(2,1)S(1)}, bf16[128,128]{1,0:T(8,128)(2,1)S(1)}, u32[]{:S(2)}, u32[]{:S(2)}) collective-permute-start(bf16[128,128]{1,0:T(8,128)(2,1)S(1)} %add.16), channel_id=1, source_target_pairs={{0,16},{1,17},{8,24},{9,25},{16,0},{17,1},{24,8},{25,9},{2,18},{3,... | collective-permute-start | bytes 98312 | tf_op jit(solution)/shard_map/ppermute | solution.py:81
  29.4 1.5 %adjoint.2 = (bf16[192,1024]{1,0:T(8,128)(2,1)S(1)}, bf16[192,1024]{1,0:T(8,128)(2,1)S(1)}, bf16[64,1024]{1,0:T(8,128)(2,1)S(1)}, bf16[64,1024]{1,0:T(8,128)(2,1)S(1)}, bf16[192,2048]{1,0:T(8,128)(2,1)}) custom-call(bf16[192,2048]{1,0:T(8,128)(2,1)S(1)} %bitcast.25, bf16[192,2048]{1,0:T(8,128)(2,1)S(1)} %bitcast.12, bf16[192,2048]{1,0:T(8,128)(2,1)S(1)} %bitcast.19, ...), custom_call_target="tpu_custom_call" | custom-call | flops 1000000000 | bytes 1000 | tf_op jit(solution)/shard_map/adjoint/pallas_call | solution.py:371
  30.9 1.6 %adjoint.3 = (bf16[192,2048]{1,0:T(8,128)(2,1)}, bf16[192,2048]{1,0:T(8,128)(2,1)}) custom-call(bf16[192,2048]{1,0:T(8,128)(2,1)S(1)} %bitcast.26, bf16[192,2048]{1,0:T(8,128)(2,1)S(1)} %bitcast.13, bf16[192,2048]{1,0:T(8,128)(2,1)S(1)} %bitcast.20, f32[128,128]{1,0:T(8,128)S(1)} %copy-done.3, ...), custom_call_target="tpu_custom_call" | custom-call | flops 1000 | bytes 1000 | tf_op jit(solution)/shard_map/adjoint/pallas_call | solution.py:371
  32.6 0.5 %collective-permute-done.9 = bf16[128,128]{1,0:T(8,128)(2,1)S(1)} collective-permute-done((bf16[128,128]{1,0:T(8,128)(2,1)S(1)}, bf16[128,128]{1,0:T(8,128)(2,1)S(1)}, u32[]{:S(2)}, u32[]{:S(2)}) %collective-permute-start.9) | collective-permute-done | bytes 32800 | tf_op jit(solution)/shard_map/ppermute | solution.py:81
  33.0 0.1 rev.4
  33.1 0.6 %broadcast_multiply_fusion = f32[128,128]{1,0:T(8,128)} fusion(f32[128,128]{1,0:T(8,128)S(1)} %rev.4), kind=kLoop, calls=%fused_computation.1 | loop fusion | flops 16384 | bytes 131072 | tf_op jit(solution)/shard_map/mul | solution.py:485
  (14 shorter events, 0.1 us)
Async XLA Ops:
  0.6 9.2 %copy-start.1 = (bf16[1,192,2048]{2,1,0:T(8,128)(2,1)S(1)}, bf16[1,192,2048]{2,1,0:T(8,128)(2,1)}, u32[]{:S(2)}) copy-start(bf16[1,192,2048]{2,1,0:T(8,128)(2,1)} %param.7) | copy-start | bytes 2359300
  0.6 9.2 %copy-start.3 = (f32[128,128]{1,0:T(8,128)S(1)}, f32[128,128]{1,0:T(8,128)}, u32[]{:S(2)}) copy-start(f32[128,128]{1,0:T(8,128)} %refs_3_.3) | copy-start | bytes 196612
  2.1 7.7 %copy-start = (bf16[1,192,2048]{2,1,0:T(8,128)(2,1)S(1)}, bf16[1,192,2048]{2,1,0:T(8,128)(2,1)}, u32[]{:S(2)}) copy-start(bf16[1,192,2048]{2,1,0:T(8,128)(2,1)} %param.6) | copy-start | bytes 2359300
  2.1 17.1 %collective-permute-start.6 = (bf16[128,2048]{1,0:T(8,128)(2,1)S(1)}, bf16[128,2048]{1,0:T(8,128)(2,1)S(1)}, u32[]{:S(2)}, u32[]{:S(2)}) collective-permute-start(bf16[128,2048]{1,0:T(8,128)(2,1)S(1)} %get-tuple-element.53), channel_id=1, source_target_pairs={{0,8},{8,16},{16,24},{24,0},{1,9},{9,17},{17,25},{25,1},{2,10},{10... | collective-permute-start | bytes 1572872 | tf_op jit(solution)/shard_map/ppermute | solution.py:38
  5.2 1.9 %collective-permute-start = (bf16[48,2048]{1,0:T(8,128)(2,1)S(1)}, bf16[48,2048]{1,0:T(8,128)(2,1)S(1)}, u32[]{:S(2)}, u32[]{:S(2)}) collective-permute-start(bf16[48,2048]{1,0:T(8,128)(2,1)S(1)} %get-tuple-element.38), channel_id=1, source_target_pairs={{0,2},{2,0},{4,6},{6,4},{1,3},{3,1},{5,7},{7,5},{8,10},{10,8},{12,... | collective-permute-start | bytes 589832 | tf_op jit(solution)/shard_map/ppermute | solution.py:56
  5.2 5.7 %collective-permute-start.1 = (bf16[48,1024]{1,0:T(8,128)(2,1)S(1)}, bf16[48,1024]{1,0:T(8,128)(2,1)S(1)}, u32[]{:S(2)}, u32[]{:S(2)}) collective-permute-start(bf16[48,1024]{1,0:T(8,128)(2,1)S(1)} %get-tuple-element.42), channel_id=1, source_target_pairs={{0,4},{2,6},{4,0},{6,2},{1,5},{3,7},{5,1},{7,3},{8,12},{10,14},{12... | collective-permute-start | bytes 294920 | tf_op jit(solution)/shard_map/ppermute | solution.py:56
  6.7 5.4 %collective-permute-start.2 = (bf16[48,1024]{1,0:T(8,128)(2,1)S(1)}, bf16[48,1024]{1,0:T(8,128)(2,1)S(1)}, u32[]{:S(2)}, u32[]{:S(2)}) collective-permute-start(bf16[48,1024]{1,0:T(8,128)(2,1)S(1)} %get-tuple-element.43), channel_id=1, source_target_pairs={{0,6},{2,4},{4,2},{6,0},{1,7},{3,5},{5,3},{7,1},{8,14},{10,12},{12... | collective-permute-start | bytes 294920 | tf_op jit(solution)/shard_map/ppermute | solution.py:56
  8.1 6.9 %collective-permute-start.3 = (bf16[48,1024]{1,0:T(8,128)(2,1)S(1)}, bf16[48,1024]{1,0:T(8,128)(2,1)S(1)}, u32[]{:S(2)}, u32[]{:S(2)}) collective-permute-start(bf16[48,1024]{1,0:T(8,128)(2,1)S(1)} %get-tuple-element.47), channel_id=1, source_target_pairs={{0,4},{2,6},{4,0},{6,2},{1,5},{3,7},{5,1},{7,3},{8,12},{10,14},{12... | collective-permute-start | bytes 294920 | tf_op jit(solution)/shard_map/ppermute | solution.py:56
  9.7 2.4 %copy-start.2 = (bf16[1,192,2048]{2,1,0:T(8,128)(2,1)S(1)}, bf16[1,192,2048]{2,1,0:T(8,128)(2,1)}, u32[]{:S(2)}) copy-start(bf16[1,192,2048]{2,1,0:T(8,128)(2,1)} %param.5) | copy-start | bytes 2359300
  9.7 6.6 %collective-permute-start.4 = (bf16[48,1024]{1,0:T(8,128)(2,1)S(1)}, bf16[48,1024]{1,0:T(8,128)(2,1)S(1)}, u32[]{:S(2)}, u32[]{:S(2)}) collective-permute-start(bf16[48,1024]{1,0:T(8,128)(2,1)S(1)} %get-tuple-element.48), channel_id=1, source_target_pairs={{0,6},{2,4},{4,2},{6,0},{1,7},{3,5},{5,3},{7,1},{8,14},{10,12},{12... | collective-permute-start | bytes 294920 | tf_op jit(solution)/shard_map/ppermute | solution.py:56
  12.3 17.1 %collective-permute-start.5 = (bf16[128,1024]{1,0:T(8,128)(2,1)S(1)}, bf16[128,1024]{1,0:T(8,128)(2,1)S(1)}, u32[]{:S(2)}, u32[]{:S(2)}) collective-permute-start(bf16[128,1024]{1,0:T(8,128)(2,1)S(1)} %get-tuple-element.52), channel_id=1, source_target_pairs={{8,0},{16,8},{24,16},{9,1},{17,9},{25,17},{10,2},{18,10},{26,18},{... | collective-permute-start | bytes 786440 | tf_op jit(solution)/shard_map/ppermute | solution.py:33
  16.5 14.4 %collective-permute-start.11 = (bf16[128,1024]{1,0:T(8,128)(2,1)S(1)}, bf16[128,1024]{1,0:T(8,128)(2,1)S(1)}, u32[]{:S(2)}, u32[]{:S(2)}) collective-permute-start(bf16[128,1024]{1,0:T(8,128)(2,1)S(1)} %get-tuple-element.60), channel_id=1, source_target_pairs={{8,0},{16,8},{24,16},{9,1},{17,9},{25,17},{10,2},{18,10},{26,18},{... | collective-permute-start | bytes 786440 | tf_op jit(solution)/shard_map/ppermute | solution.py:33
  20.9 4.0 %collective-permute-start.7 = (bf16[128,128]{1,0:T(8,128)(2,1)S(1)}, bf16[128,128]{1,0:T(8,128)(2,1)S(1)}, u32[]{:S(2)}, u32[]{:S(2)}) collective-permute-start(bf16[128,128]{1,0:T(8,128)(2,1)S(1)} %edge_scores.1.refs_0_), channel_id=1, source_target_pairs={{0,1},{1,0},{8,9},{9,8},{16,17},{17,16},{24,25},{25,24},{2,3},{3,2... | collective-permute-start | bytes 98312 | tf_op jit(solution)/shard_map/ppermute | solution.py:81
  24.9 7.6 %collective-permute-start.10 = (bf16[128,128]{1,0:T(8,128)(2,1)S(1)}, bf16[128,128]{1,0:T(8,128)(2,1)S(1)}, u32[]{:S(2)}, u32[]{:S(2)}) collective-permute-start(bf16[128,128]{1,0:T(8,128)(2,1)S(1)} %add.16), channel_id=1, source_target_pairs={{0,24},{1,25},{8,16},{9,17},{16,8},{17,9},{24,0},{25,1},{2,26},{3,... | collective-permute-start | bytes 98312 | tf_op jit(solution)/shard_map/ppermute | solution.py:81
  28.2 4.4 %collective-permute-start.8 = (bf16[128,128]{1,0:T(8,128)(2,1)S(1)}, bf16[128,128]{1,0:T(8,128)(2,1)S(1)}, u32[]{:S(2)}, u32[]{:S(2)}) collective-permute-start(bf16[128,128]{1,0:T(8,128)(2,1)S(1)} %add.16), channel_id=1, source_target_pairs={{0,8},{1,9},{8,0},{9,1},{16,24},{17,25},{24,16},{25,17},{2,10},{3,... | collective-permute-start | bytes 98312 | tf_op jit(solution)/shard_map/ppermute | solution.py:81
  28.2 4.8 %collective-permute-start.9 = (bf16[128,128]{1,0:T(8,128)(2,1)S(1)}, bf16[128,128]{1,0:T(8,128)(2,1)S(1)}, u32[]{:S(2)}, u32[]{:S(2)}) collective-permute-start(bf16[128,128]{1,0:T(8,128)(2,1)S(1)} %add.16), channel_id=1, source_target_pairs={{0,16},{1,17},{8,24},{9,25},{16,0},{17,1},{24,8},{25,9},{2,18},{3,... | collective-permute-start | bytes 98312 | tf_op jit(solution)/shard_map/ppermute | solution.py:81

commit v9 on v8

--- a/solution.py
+++ b/solution.py
@@ -109,13 +109,24 @@
 def last_round(value, after):
     rounds = rounds_of_sum()
     if not rounds:
-        return widen(value), after
+        return [widen(value)], after
     parts = [value] + [brought(value, step) for step in rounds[-1]]
     parts, after = lax.optimization_barrier((parts, after))
-    parts = [widen(part) for part in parts]
-    while len(parts) > 1:
-        parts = [parts[m] + parts[m + 1] for m in range(0, len(parts), 2)]
-    return parts[0], after
+    return parts, after
+
+
+def finish_kernel(scale, *refs):
+    parts, (out_ref, stage_ref, sem) = refs[:-3], refs[-3:]
+    total = [widen(part[...]) for part in parts]
+    while len(total) > 1:
+        total = [total[m] + total[m + 1] for m in range(0, len(total), 2)]
+    size = total[0].shape[1]
+    backward = size - 1 - lax.broadcasted_iota(jnp.int32, total[0].shape, 1)
+    turned = jnp.take_along_axis(total[0], backward, axis=1, mode="promise_in_bounds")
+    stage_ref[...] = turned * scale
+    copy = pltpu.make_async_copy(stage_ref, out_ref, sem)
+    copy.start()
+    copy.wait()
 
 
 def windows(rows, blocks, height):
@@ -482,7 +493,11 @@
     )
     lags, key_grad = last_round(lags, key_grad)
     scale = 1.0 / math.sqrt(lax.axis_size("dp") * lax.axis_size("ctx") * rows * group_width)
-    return (query_grad[None], key_grad[None], value_grad[None], jnp.flip(lags, 1) * scale)
+    (filter_grad,) = call(
+        work(finish_kernel, scale), "finish", lags, [small], COST_B, 0,
+        [pltpu.VMEM(small.shape, small.dtype), pltpu.SemaphoreType.DMA],
+    )
+    return (query_grad[None], key_grad[None], value_grad[None], filter_grad)
 
 
 COST = 100_000_000

time: 34 us -> 34 us (level)
  Pallas kernels: 11.2 us -> 12 us
  other arithmetic: 0.67 us -> 0 us
    pallas_call x8 -> x9, Pallas kernels: 8.7 us -> 9.43 us  [call(): pl.pallas_call(kernel, in_specs=[VMEM] * len(args), out_specs=[VMEM] * ke...]
    mul x1 -> x0, other arithmetic: 0.65 us -> none  [local(): jnp.flip(lags, 1) * scale]
where the time goes in v9:
time: 34 us; the launch traced here: 33.8 us
  starting transfers between devices  15.3 us (45%)
  Pallas kernels  12 us (35%)
  waiting for transfers between devices  5.76 us (17%)
  between operations  0.77 us (2%)
    pallas_call x9, Pallas kernels, call(): pl.pallas_call(kernel, in_specs=[VMEM] * len(args), out_specs=[VMEM] * ke...  9.43 us
    ppermute x4, starting transfers between devices, brought(): lax.ppermute(value, axes, [(index, index ^ step) for index in range(count)])  6.04 us
    ppermute x5, starting transfers between devices, exchanged(): return lax.ppermute(part, axis, pairs)  3.56 us
    ppermute x5, waiting for transfers between devices, exchanged(): return lax.ppermute(part, axis, pairs)  3.12 us
    ppermute x1, starting transfers between devices, passed_round(): lax.ppermute(value, axis, [(index, (index + steps) % count) for index in...  3.08 us
    ppermute x2, starting transfers between devices, passed_along(): lax.ppermute(value, axis, [(source, source + steps) for source in range(f...  2.58 us
    pallas_call x1, Pallas kernels, local(): pl.pallas_call(functools.partial(pack_kernel, first_cuts, count, lax.axis...  1.45 us
    ppermute x1, waiting for transfers between devices, passed_round(): lax.ppermute(value, axis, [(index, (index + steps) % count) for index in...  1.43 us
  transfers between devices with their start and end apart: 12, of which 6 were waited for; matrix products, arithmetic and copies ran while one was open for 0% of the time, Pallas kernels for 29%

profile of v9, /device:TPU:0, one launch (start us, length us, event | category | flops | bytes accessed | tf_op | source)
XLA Modules:
  0.0 33.8 jit_solution(5980479133671357808)
XLA Ops:
  0.7 1.4 %pack.1 = (bf16[48,2048]{1,0:T(8,128)(2,1)S(1)}, bf16[48,1024]{1,0:T(8,128)(2,1)S(1)}, bf16[48,1024]{1,0:T(8,128)(2,1)S(1)}, bf16[128,2048]{1,0:T(8,128)(2,1)S(1)}) custom-call(bf16[48,8192]{1,0:T(8,128)(2,1)} %bitcast.27, bf16[192,2048]{1,0:T(8,128)(2,1)} %bitcast.7, bf16[192,2048]{1,0:T(8,128)(2,1)} %bitcast.14), custom_call_target="tpu_custom_call" | custom-call | tf_op jit(solution)/shard_map/pack/pallas_call | solution.py:416
  2.1 0.0 copy-start
  2.1 3.1 %collective-permute-start.6 = (bf16[128,2048]{1,0:T(8,128)(2,1)S(1)}, bf16[128,2048]{1,0:T(8,128)(2,1)S(1)}, u32[]{:S(2)}, u32[]{:S(2)}) collective-permute-start(bf16[128,2048]{1,0:T(8,128)(2,1)S(1)} %get-tuple-element.53), channel_id=1, source_target_pairs={{0,8},{8,16},{16,24},{24,0},{1,9},{9,17},{17,25},{25,1},{2,10},{10... | collective-permute-start | bytes 1572872 | tf_op jit(solution)/shard_map/ppermute | solution.py:38
  5.2 1.5 %collective-permute-start.1 = (bf16[48,1024]{1,0:T(8,128)(2,1)S(1)}, bf16[48,1024]{1,0:T(8,128)(2,1)S(1)}, u32[]{:S(2)}, u32[]{:S(2)}) collective-permute-start(bf16[48,1024]{1,0:T(8,128)(2,1)S(1)} %get-tuple-element.42), channel_id=1, source_target_pairs={{0,4},{2,6},{4,0},{6,2},{1,5},{3,7},{5,1},{7,3},{8,12},{10,14},{12... | collective-permute-start | bytes 294920 | tf_op jit(solution)/shard_map/ppermute | solution.py:56
  6.7 0.4 %collective-permute-start.2 = (bf16[48,1024]{1,0:T(8,128)(2,1)S(1)}, bf16[48,1024]{1,0:T(8,128)(2,1)S(1)}, u32[]{:S(2)}, u32[]{:S(2)}) collective-permute-start(bf16[48,1024]{1,0:T(8,128)(2,1)S(1)} %get-tuple-element.43), channel_id=1, source_target_pairs={{0,6},{2,4},{4,2},{6,0},{1,7},{3,5},{5,3},{7,1},{8,14},{10,12},{12... | collective-permute-start | bytes 294920 | tf_op jit(solution)/shard_map/ppermute | solution.py:56
  7.1 0.0 collective-permute-done.refs_1_
  7.1 1.1 %second_pack.1 = (bf16[48,2048]{1,0:T(8,128)(2,1)S(1)}, bf16[48,1024]{1,0:T(8,128)(2,1)S(1)}, bf16[48,1024]{1,0:T(8,128)(2,1)S(1)}) custom-call(bf16[48,8192]{1,0:T(8,128)(2,1)} %bitcast.28), custom_call_target="tpu_custom_call" | custom-call | tf_op jit(solution)/shard_map/second_pack/pallas_call | solution.py:429
  8.1 1.6 %collective-permute-start.3 = (bf16[48,1024]{1,0:T(8,128)(2,1)S(1)}, bf16[48,1024]{1,0:T(8,128)(2,1)S(1)}, u32[]{:S(2)}, u32[]{:S(2)}) collective-permute-start(bf16[48,1024]{1,0:T(8,128)(2,1)S(1)} %get-tuple-element.47), channel_id=1, source_target_pairs={{0,4},{2,6},{4,0},{6,2},{1,5},{3,7},{5,1},{7,3},{8,12},{10,14},{12... | collective-permute-start | bytes 294920 | tf_op jit(solution)/shard_map/ppermute | solution.py:56
  9.7 0.1 collective-permute-start.4
  9.8 1.1 %inner_causal.1.inner_ref = f32[64,2048]{1,0:T(8,128)S(1)} custom-call(bf16[192,2048]{1,0:T(8,128)(2,1)S(1)} %bitcast.8, bf16[192,2048]{1,0:T(8,128)(2,1)S(1)} %bitcast.15, f32[128,128]{1,0:T(8,128)S(1)} %copy-done.3), custom_call_target="tpu_custom_call" | custom-call | flops 100000000 | bytes 1000 | tf_op jit(solution)/shard_map/inner_causal/pallas_call | solution.py:382
  10.9 0.0 collective-permute-done.1.refs_2_
  10.9 1.2 %collective-permute-done.2.refs_3_ = bf16[48,1024]{1,0:T(8,128)(2,1)S(1)} collective-permute-done((bf16[48,1024]{1,0:T(8,128)(2,1)S(1)}, bf16[48,1024]{1,0:T(8,128)(2,1)S(1)}, u32[]{:S(2)}, u32[]{:S(2)}) %collective-permute-start.2) | collective-permute-done | bytes 98336 | tf_op jit(solution)/shard_map/ppermute | solution.py:56
  12.1 0.1 gather.2
  12.3 1.3 %collective-permute-start.5 = (bf16[128,1024]{1,0:T(8,128)(2,1)S(1)}, bf16[128,1024]{1,0:T(8,128)(2,1)S(1)}, u32[]{:S(2)}, u32[]{:S(2)}) collective-permute-start(bf16[128,1024]{1,0:T(8,128)(2,1)S(1)} %get-tuple-element.52), channel_id=1, source_target_pairs={{8,0},{16,8},{24,16},{9,1},{17,9},{25,17},{10,2},{18,10},{26,18},{... | collective-permute-start | bytes 786440 | tf_op jit(solution)/shard_map/ppermute | solution.py:33
  13.6 0.8 %inner_scores.1.refs_5_ = f32[64,128]{1,0:T(8,128)S(1)} custom-call(bf16[192,2048]{1,0:T(8,128)(2,1)S(1)} %bitcast.22, bf16[192,1024]{1,0:T(8,128)(2,1)S(1)} %get-tuple-element.46.og_ref.refs_0_.refs_4_, bf16[192,2048]{1,0:T(8,128)(2,1)S(1)} %bitcast.9, bf16[192,2048]{1,0:T(8,128)(2,1)S(1)} %bitcast.16), custom_call_target="tpu_custom_call" | custom-call | flops 100000000 | bytes 1000 | tf_op jit(solution)/shard_map/inner_scores/pallas_call | solution.py:382
  14.4 0.6 %collective-permute-done.3.refs_2_ = bf16[48,1024]{1,0:T(8,128)(2,1)S(1)} collective-permute-done((bf16[48,1024]{1,0:T(8,128)(2,1)S(1)}, bf16[48,1024]{1,0:T(8,128)(2,1)S(1)}, u32[]{:S(2)}, u32[]{:S(2)}) %collective-permute-start.3) | collective-permute-done | bytes 98336 | tf_op jit(solution)/shard_map/ppermute | solution.py:56
  15.0 1.3 %collective-permute-done.4.refs_3_ = bf16[48,1024]{1,0:T(8,128)(2,1)S(1)} collective-permute-done((bf16[48,1024]{1,0:T(8,128)(2,1)S(1)}, bf16[48,1024]{1,0:T(8,128)(2,1)S(1)}, u32[]{:S(2)}, u32[]{:S(2)}) %collective-permute-start.4) | collective-permute-done | bytes 98336 | tf_op jit(solution)/shard_map/ppermute | solution.py:56
  16.3 0.1 gather.3
  16.5 1.3 %collective-permute-start.11 = (bf16[128,1024]{1,0:T(8,128)(2,1)S(1)}, bf16[128,1024]{1,0:T(8,128)(2,1)S(1)}, u32[]{:S(2)}, u32[]{:S(2)}) collective-permute-start(bf16[128,1024]{1,0:T(8,128)(2,1)S(1)} %get-tuple-element.60), channel_id=1, source_target_pairs={{8,0},{16,8},{24,16},{9,1},{17,9},{25,17},{10,2},{18,10},{26,18},{... | collective-permute-start | bytes 786440 | tf_op jit(solution)/shard_map/ppermute | solution.py:33
  17.8 1.4 %collective-permute-done.6.refs_4_.early_ref = bf16[128,2048]{1,0:T(8,128)(2,1)S(1)} collective-permute-done((bf16[128,2048]{1,0:T(8,128)(2,1)S(1)}, bf16[128,2048]{1,0:T(8,128)(2,1)S(1)}, u32[]{:S(2)}, u32[]{:S(2)}) %collective-permute-start.6) | collective-permute-done | bytes 524320 | tf_op jit(solution)/shard_map/ppermute | solution.py:38
  19.2 1.7 %edge_scores.1.refs_0_ = bf16[128,128]{1,0:T(8,128)(2,1)S(1)} custom-call(bf16[192,2048]{1,0:T(8,128)(2,1)S(1)} %bitcast.24, bf16[192,1024]{1,0:T(8,128)(2,1)S(1)} %get-tuple-element.46.og_ref.refs_0_.refs_4_, bf16[192,1024]{1,0:T(8,128)(2,1)S(1)} %get-tuple-element.51.refs_1_.refs_5_.refs_4_, bf16[192,2048]{1,0:T(8,128)(2,1)S(1)} %bitcast.10, ...), custom_call_target="tpu_custom_call" | custom-call | flops 100000000 | bytes 1000 | tf_op jit(solution)/shard_map/edge_scores/pallas_call | solution.py:382
  20.9 1.6 %collective-permute-start.7 = (bf16[128,128]{1,0:T(8,128)(2,1)S(1)}, bf16[128,128]{1,0:T(8,128)(2,1)S(1)}, u32[]{:S(2)}, u32[]{:S(2)}) collective-permute-start(bf16[128,128]{1,0:T(8,128)(2,1)S(1)} %edge_scores.1.refs_0_), channel_id=1, source_target_pairs={{0,1},{1,0},{8,9},{9,8},{16,17},{17,16},{24,25},{25,24},{2,3},{3,2... | collective-permute-start | bytes 98312 | tf_op jit(solution)/shard_map/ppermute | solution.py:81
  22.5 1.6 %causal.1.refs_7_ = bf16[192,2048]{1,0:T(8,128)(2,1)S(1)} custom-call(bf16[192,2048]{1,0:T(8,128)(2,1)S(1)} %bitcast.11, bf16[192,2048]{1,0:T(8,128)(2,1)S(1)} %bitcast.18, bf16[128,2048]{1,0:T(8,128)(2,1)S(1)} %collective-permute-done.6.refs_4_.early_ref, f32[128,128]{1,0:T(8,128)S(1)} %copy-done.3, f32[64,2048]{1,0:T(8,128)S(1)} %inner_causal.1.inner_ref, ...), custom_call_target="tpu_custom_call" | custom-call | flops 100000000 | bytes 1000 | tf_op jit(solution)/shard_map/causal/pallas_call | solution.py:382
  24.2 0.7 %collective-permute-done.7.refs_1_ = bf16[128,128]{1,0:T(8,128)(2,1)S(1)} collective-permute-done((bf16[128,128]{1,0:T(8,128)(2,1)S(1)}, bf16[128,128]{1,0:T(8,128)(2,1)S(1)}, u32[]{:S(2)}, u32[]{:S(2)}) %collective-permute-start.7) | collective-permute-done | bytes 32800 | tf_op jit(solution)/shard_map/ppermute | solution.py:81
  24.9 3.3 %collective-permute-start.10 = (bf16[128,128]{1,0:T(8,128)(2,1)S(1)}, bf16[128,128]{1,0:T(8,128)(2,1)S(1)}, u32[]{:S(2)}, u32[]{:S(2)}) collective-permute-start(bf16[128,128]{1,0:T(8,128)(2,1)S(1)} %add.1.refs_0_), channel_id=1, source_target_pairs={{0,24},{1,25},{8,16},{9,17},{16,8},{17,9},{24,0},{25,1},{2,26},{3,... | collective-permute-start | bytes 98312 | tf_op jit(solution)/shard_map/ppermute | solution.py:81
  28.2 1.1 %collective-permute-start.9 = (bf16[128,128]{1,0:T(8,128)(2,1)S(1)}, bf16[128,128]{1,0:T(8,128)(2,1)S(1)}, u32[]{:S(2)}, u32[]{:S(2)}) collective-permute-start(bf16[128,128]{1,0:T(8,128)(2,1)S(1)} %add.1.refs_0_), channel_id=1, source_target_pairs={{0,16},{1,17},{8,24},{9,25},{16,0},{17,1},{24,8},{25,9},{2,18},{3,... | collective-permute-start | bytes 98312 | tf_op jit(solution)/shard_map/ppermute | solution.py:81
  29.4 0.0 collective-permute-done.5.refs_6_
  29.4 1.5 %adjoint.2 = (bf16[192,1024]{1,0:T(8,128)(2,1)S(1)}, bf16[192,1024]{1,0:T(8,128)(2,1)S(1)}, bf16[64,1024]{1,0:T(8,128)(2,1)S(1)}, bf16[64,1024]{1,0:T(8,128)(2,1)S(1)}, bf16[192,2048]{1,0:T(8,128)(2,1)}) custom-call(bf16[192,2048]{1,0:T(8,128)(2,1)S(1)} %bitcast.25, bf16[192,2048]{1,0:T(8,128)(2,1)S(1)} %bitcast.12, bf16[192,2048]{1,0:T(8,128)(2,1)S(1)} %bitcast.19, ...), custom_call_target="tpu_custom_call" | custom-call | flops 1000000000 | bytes 1000 | tf_op jit(solution)/shard_map/adjoint/pallas_call | solution.py:382
  30.9 1.6 %adjoint.3 = (bf16[192,2048]{1,0:T(8,128)(2,1)}, bf16[192,2048]{1,0:T(8,128)(2,1)}) custom-call(bf16[192,2048]{1,0:T(8,128)(2,1)S(1)} %bitcast.26, bf16[192,2048]{1,0:T(8,128)(2,1)S(1)} %bitcast.13, bf16[192,2048]{1,0:T(8,128)(2,1)S(1)} %bitcast.20, f32[128,128]{1,0:T(8,128)S(1)} %copy-done.3, ...), custom_call_target="tpu_custom_call" | custom-call | flops 1000 | bytes 1000 | tf_op jit(solution)/shard_map/adjoint/pallas_call | solution.py:382
  32.6 0.0 collective-permute-done.10.refs_3_
  32.6 0.5 %collective-permute-done.9.refs_2_ = bf16[128,128]{1,0:T(8,128)(2,1)S(1)} collective-permute-done((bf16[128,128]{1,0:T(8,128)(2,1)S(1)}, bf16[128,128]{1,0:T(8,128)(2,1)S(1)}, u32[]{:S(2)}, u32[]{:S(2)}) %collective-permute-start.9) | collective-permute-done | bytes 32800 | tf_op jit(solution)/shard_map/ppermute | solution.py:81
  33.0 0.7 %finish.1 = f32[128,128]{1,0:T(8,128)} custom-call(bf16[128,128]{1,0:T(8,128)(2,1)S(1)} %add.1.refs_0_, bf16[128,128]{1,0:T(8,128)(2,1)S(1)} %collective-permute-done.8.refs_1_, bf16[128,128]{1,0:T(8,128)(2,1)S(1)} %collective-permute-done.9.refs_2_, bf16[128,128]{1,0:T(8,128)(2,1)S(1)} %collective-permute-done.10.refs_3_), custom_call_target="tpu_custom_call" | custom-call | flops 1000 | bytes 1000 | tf_op jit(solution)/shard_map/finish/pallas_call | solution.py:382
  (12 shorter events, 0.0 us)
Async XLA Ops:
  0.6 9.2 %copy-start.1 = (bf16[1,192,2048]{2,1,0:T(8,128)(2,1)S(1)}, bf16[1,192,2048]{2,1,0:T(8,128)(2,1)}, u32[]{:S(2)}) copy-start(bf16[1,192,2048]{2,1,0:T(8,128)(2,1)} %param.7) | copy-start | bytes 2359300
  0.6 9.2 %copy-start.3 = (f32[128,128]{1,0:T(8,128)S(1)}, f32[128,128]{1,0:T(8,128)}, u32[]{:S(2)}) copy-start(f32[128,128]{1,0:T(8,128)} %refs_3_.3) | copy-start | bytes 196612
  2.1 7.7 %copy-start = (bf16[1,192,2048]{2,1,0:T(8,128)(2,1)S(1)}, bf16[1,192,2048]{2,1,0:T(8,128)(2,1)}, u32[]{:S(2)}) copy-start(bf16[1,192,2048]{2,1,0:T(8,128)(2,1)} %param.6) | copy-start | bytes 2359300
  2.1 17.1 %collective-permute-start.6 = (bf16[128,2048]{1,0:T(8,128)(2,1)S(1)}, bf16[128,2048]{1,0:T(8,128)(2,1)S(1)}, u32[]{:S(2)}, u32[]{:S(2)}) collective-permute-start(bf16[128,2048]{1,0:T(8,128)(2,1)S(1)} %get-tuple-element.53), channel_id=1, source_target_pairs={{0,8},{8,16},{16,24},{24,0},{1,9},{9,17},{17,25},{25,1},{2,10},{10... | collective-permute-start | bytes 1572872 | tf_op jit(solution)/shard_map/ppermute | solution.py:38
  5.2 1.9 %collective-permute-start = (bf16[48,2048]{1,0:T(8,128)(2,1)S(1)}, bf16[48,2048]{1,0:T(8,128)(2,1)S(1)}, u32[]{:S(2)}, u32[]{:S(2)}) collective-permute-start(bf16[48,2048]{1,0:T(8,128)(2,1)S(1)} %get-tuple-element.38), channel_id=1, source_target_pairs={{0,2},{2,0},{4,6},{6,4},{1,3},{3,1},{5,7},{7,5},{8,10},{10,8},{12,... | collective-permute-start | bytes 589832 | tf_op jit(solution)/shard_map/ppermute | solution.py:56
  5.2 5.7 %collective-permute-start.1 = (bf16[48,1024]{1,0:T(8,128)(2,1)S(1)}, bf16[48,1024]{1,0:T(8,128)(2,1)S(1)}, u32[]{:S(2)}, u32[]{:S(2)}) collective-permute-start(bf16[48,1024]{1,0:T(8,128)(2,1)S(1)} %get-tuple-element.42), channel_id=1, source_target_pairs={{0,4},{2,6},{4,0},{6,2},{1,5},{3,7},{5,1},{7,3},{8,12},{10,14},{12... | collective-permute-start | bytes 294920 | tf_op jit(solution)/shard_map/ppermute | solution.py:56
  6.7 5.4 %collective-permute-start.2 = (bf16[48,1024]{1,0:T(8,128)(2,1)S(1)}, bf16[48,1024]{1,0:T(8,128)(2,1)S(1)}, u32[]{:S(2)}, u32[]{:S(2)}) collective-permute-start(bf16[48,1024]{1,0:T(8,128)(2,1)S(1)} %get-tuple-element.43), channel_id=1, source_target_pairs={{0,6},{2,4},{4,2},{6,0},{1,7},{3,5},{5,3},{7,1},{8,14},{10,12},{12... | collective-permute-start | bytes 294920 | tf_op jit(solution)/shard_map/ppermute | solution.py:56
  8.1 6.9 %collective-permute-start.3 = (bf16[48,1024]{1,0:T(8,128)(2,1)S(1)}, bf16[48,1024]{1,0:T(8,128)(2,1)S(1)}, u32[]{:S(2)}, u32[]{:S(2)}) collective-permute-start(bf16[48,1024]{1,0:T(8,128)(2,1)S(1)} %get-tuple-element.47), channel_id=1, source_target_pairs={{0,4},{2,6},{4,0},{6,2},{1,5},{3,7},{5,1},{7,3},{8,12},{10,14},{12... | collective-permute-start | bytes 294920 | tf_op jit(solution)/shard_map/ppermute | solution.py:56
  9.7 2.4 %copy-start.2 = (bf16[1,192,2048]{2,1,0:T(8,128)(2,1)S(1)}, bf16[1,192,2048]{2,1,0:T(8,128)(2,1)}, u32[]{:S(2)}) copy-start(bf16[1,192,2048]{2,1,0:T(8,128)(2,1)} %param.5) | copy-start | bytes 2359300
  9.7 6.6 %collective-permute-start.4 = (bf16[48,1024]{1,0:T(8,128)(2,1)S(1)}, bf16[48,1024]{1,0:T(8,128)(2,1)S(1)}, u32[]{:S(2)}, u32[]{:S(2)}) collective-permute-start(bf16[48,1024]{1,0:T(8,128)(2,1)S(1)} %get-tuple-element.48), channel_id=1, source_target_pairs={{0,6},{2,4},{4,2},{6,0},{1,7},{3,5},{5,3},{7,1},{8,14},{10,12},{12... | collective-permute-start | bytes 294920 | tf_op jit(solution)/shard_map/ppermute | solution.py:56
  12.3 17.1 %collective-permute-start.5 = (bf16[128,1024]{1,0:T(8,128)(2,1)S(1)}, bf16[128,1024]{1,0:T(8,128)(2,1)S(1)}, u32[]{:S(2)}, u32[]{:S(2)}) collective-permute-start(bf16[128,1024]{1,0:T(8,128)(2,1)S(1)} %get-tuple-element.52), channel_id=1, source_target_pairs={{8,0},{16,8},{24,16},{9,1},{17,9},{25,17},{10,2},{18,10},{26,18},{... | collective-permute-start | bytes 786440 | tf_op jit(solution)/shard_map/ppermute | solution.py:33
  16.5 14.4 %collective-permute-start.11 = (bf16[128,1024]{1,0:T(8,128)(2,1)S(1)}, bf16[128,1024]{1,0:T(8,128)(2,1)S(1)}, u32[]{:S(2)}, u32[]{:S(2)}) collective-permute-start(bf16[128,1024]{1,0:T(8,128)(2,1)S(1)} %get-tuple-element.60), channel_id=1, source_target_pairs={{8,0},{16,8},{24,16},{9,1},{17,9},{25,17},{10,2},{18,10},{26,18},{... | collective-permute-start | bytes 786440 | tf_op jit(solution)/shard_map/ppermute | solution.py:33
  20.9 4.0 %collective-permute-start.7 = (bf16[128,128]{1,0:T(8,128)(2,1)S(1)}, bf16[128,128]{1,0:T(8,128)(2,1)S(1)}, u32[]{:S(2)}, u32[]{:S(2)}) collective-permute-start(bf16[128,128]{1,0:T(8,128)(2,1)S(1)} %edge_scores.1.refs_0_), channel_id=1, source_target_pairs={{0,1},{1,0},{8,9},{9,8},{16,17},{17,16},{24,25},{25,24},{2,3},{3,2... | collective-permute-start | bytes 98312 | tf_op jit(solution)/shard_map/ppermute | solution.py:81
  24.9 7.6 %collective-permute-start.10 = (bf16[128,128]{1,0:T(8,128)(2,1)S(1)}, bf16[128,128]{1,0:T(8,128)(2,1)S(1)}, u32[]{:S(2)}, u32[]{:S(2)}) collective-permute-start(bf16[128,128]{1,0:T(8,128)(2,1)S(1)} %add.1.refs_0_), channel_id=1, source_target_pairs={{0,24},{1,25},{8,16},{9,17},{16,8},{17,9},{24,0},{25,1},{2,26},{3,... | collective-permute-start | bytes 98312 | tf_op jit(solution)/shard_map/ppermute | solution.py:81
  28.2 4.4 %collective-permute-start.8 = (bf16[128,128]{1,0:T(8,128)(2,1)S(1)}, bf16[128,128]{1,0:T(8,128)(2,1)S(1)}, u32[]{:S(2)}, u32[]{:S(2)}) collective-permute-start(bf16[128,128]{1,0:T(8,128)(2,1)S(1)} %add.1.refs_0_), channel_id=1, source_target_pairs={{0,8},{1,9},{8,0},{9,1},{16,24},{17,25},{24,16},{25,17},{2,10},{3,... | collective-permute-start | bytes 98312 | tf_op jit(solution)/shard_map/ppermute | solution.py:81
  28.2 4.8 %collective-permute-start.9 = (bf16[128,128]{1,0:T(8,128)(2,1)S(1)}, bf16[128,128]{1,0:T(8,128)(2,1)S(1)}, u32[]{:S(2)}, u32[]{:S(2)}) collective-permute-start(bf16[128,128]{1,0:T(8,128)(2,1)S(1)} %add.1.refs_0_), channel_id=1, source_target_pairs={{0,16},{1,17},{8,24},{9,25},{16,0},{17,1},{24,8},{25,9},{2,18},{3,... | collective-permute-start | bytes 98312 | tf_op jit(solution)/shard_map/ppermute | solution.py:81
